TPU v7x, 32 devices: a whole 2x2x4 slice. The times are simulated.
32 devices in a mesh: rep: 8 (over y, x, core), shard: 4 (over z).
Axes of the slice: x: 2, y: 2, z: 4, core: 2. Of those that a mesh axis runs over, the one named last changes fastest.
Arguments:
- tokens: bfloat16 [160, 197, 768], P(('rep', 'shard')), may hold values from -6 to 6
- counts: int32 [32], P(('rep', 'shard')), may hold values from 4 to 5, as said below
- w_qkv: bfloat16 [768, 2304], P('shard'), may hold values from -0.21875 to 0.21875
- b_query: bfloat16 [768], P('shard'), may hold values from -3 to 3
- b_value: bfloat16 [768], P('shard'), may hold values from -3 to 3
- w_proj: bfloat16 [768, 768], P('shard'), may hold values from -0.625 to 0.625
- b_proj: bfloat16 [768], P('shard'), may hold values from -3 to 3
- gain_one: bfloat16 [768], P('shard'), may hold values from 0.5 to 1.5
- bias_one: bfloat16 [768], P('shard'), may hold values from -2 to 2
- gain_two: bfloat16 [768], P('shard'), may hold values from 0.5 to 1.5
- bias_two: bfloat16 [768], P('shard'), may hold values from -2 to 2
- w_up: bfloat16 [768, 3072], P('shard'), may hold values from -0.21875 to 0.21875
- b_up: bfloat16 [3072], P('shard'), may hold values from -3 to 3
- w_down: bfloat16 [3072, 768], P('shard'), may hold values from -0.109375 to 0.109375
- b_down: bfloat16 [768], P('shard'), may hold values from -3 to 3
- out_grad: bfloat16 [160, 197, 768], P(('rep', 'shard')), may hold values from -6 to 6
Outputs:
- layer_out: bfloat16 [160, 197, 768], P(('rep', 'shard'))
- grad_tokens: bfloat16 [160, 197, 768], P(('rep', 'shard'))
- grad_w_qkv: float32 [768, 2304], P('shard')
- grad_b_query: float32 [768], P('shard')
- grad_b_value: float32 [768], P('shard')
- grad_w_proj: float32 [768, 768], P('shard')
- grad_b_proj: float32 [768], P('shard')
- grad_gain_one: float32 [768], P('shard')
- grad_bias_one: float32 [768], P('shard')
- grad_gain_two: float32 [768], P('shard')
- grad_bias_two: float32 [768], P('shard')
- grad_w_up: float32 [768, 3072], P('shard')
- grad_b_up: float32 [3072], P('shard')
- grad_w_down: float32 [3072, 768], P('shard')
- grad_b_down: float32 [768], P('shard')
Inputs may be any that keep to these rules, and one draw needn't show every extreme that they name: Device d holds images in its first counts[d] slots; in every draw some device holds 5 and some 4.
All inputs are finite; a program needn't handle non-finite values.
Results may differ from a plain program's by a relative error of at most 0.015.
Values may be sent and summed in bfloat16 or wider, within the bound.
No kernel may reach another device: no remote copies, remote signals or barrier semaphores. Data moves between devices by JAX's collectives and lax.ppermute only.
A program may use at most 192 MiB of HBM per device.

v0:
```python
import math

import jax
import jax.numpy as jnp
from jax import lax
from jax.sharding import PartitionSpec as P

H = 12
HD = 64


EPSILON = 1e-06
ROOT_HALF = 1.0 / math.sqrt(2.0)
INV_ROOT_TAU = 1.0 / math.sqrt(2.0 * math.pi)


def norm_parts(values_in):
    row_mean = jnp.mean(values_in, axis=-1, keepdims=True)
    centred = values_in - row_mean
    inverse = lax.rsqrt(jnp.mean(centred * centred, axis=-1, keepdims=True) + EPSILON)
    return (centred * inverse, inverse)


def norm_back(grad_normal, normal_rows, inverse_rows):
    first_mean = jnp.mean(grad_normal, axis=-1, keepdims=True)
    second_mean = jnp.mean(grad_normal * normal_rows, axis=-1, keepdims=True)
    return inverse_rows * (grad_normal - first_mean - normal_rows * second_mean)


def gelu_slope(hidden):
    return (
        0.5 * (1.0 + jax.scipy.special.erf(hidden * ROOT_HALF))
        + hidden * jnp.exp(-0.5 * hidden * hidden) * INV_ROOT_TAU
    )


def per_device(
    tokens,
    counts,
    w_qkv,
    b_query,
    b_value,
    w_proj,
    b_proj,
    gain_one,
    bias_one,
    gain_two,
    bias_two,
    w_up,
    b_up,
    w_down,
    b_down,
    out_grad,
):
    f32 = jnp.float32
    bf16 = jnp.bfloat16
    slot_count, length, feat_width = tokens.shape
    row_count = slot_count * length
    factor = HD ** (-0.5)
    (
        qkv_full,
        query_bias,
        value_bias,
        proj_full,
        proj_bias,
        gain_full_one,
        bias_full_one,
        gain_full_two,
        bias_full_two,
        up_full,
        up_bias,
        down_full,
        down_bias,
    ) = (
        lax.all_gather(w_qkv, "shard", axis=0, tiled=True),
        lax.all_gather(b_query, "shard", axis=0, tiled=True),
        lax.all_gather(b_value, "shard", axis=0, tiled=True),
        lax.all_gather(w_proj, "shard", axis=0, tiled=True),
        lax.all_gather(b_proj, "shard", axis=0, tiled=True),
        lax.all_gather(gain_one, "shard", axis=0, tiled=True),
        lax.all_gather(bias_one, "shard", axis=0, tiled=True),
        lax.all_gather(gain_two, "shard", axis=0, tiled=True),
        lax.all_gather(bias_two, "shard", axis=0, tiled=True),
        lax.all_gather(w_up, "shard", axis=0, tiled=True),
        lax.all_gather(b_up, "shard", axis=0, tiled=True),
        lax.all_gather(w_down, "shard", axis=0, tiled=True),
        lax.all_gather(b_down, "shard", axis=0, tiled=True),
    )
    live_slots = (jnp.arange(slot_count, dtype=jnp.int32) < counts[0]).astype(f32)
    live_rows = jnp.repeat(live_slots, length)[:, None]
    inputs = tokens.reshape(row_count, feat_width).astype(f32)
    normal_one, inverse_one = norm_parts(inputs)
    normed_one = (normal_one * gain_full_one.astype(f32) + bias_full_one.astype(f32)).astype(bf16)
    joined = jnp.dot(normed_one, qkv_full, preferred_element_type=f32)
    joined = joined + jnp.concatenate(
        [query_bias.astype(f32), jnp.zeros(query_bias.shape, f32), value_bias.astype(f32)]
    )
    split_heads = joined.astype(bf16).reshape(slot_count, length, 3, H, HD)
    queries = split_heads[:, :, 0]
    key_part = split_heads[:, :, 1]
    value_part = split_heads[:, :, 2]
    scores = jnp.einsum("bqhd,bkhd->bhqk", queries, key_part, preferred_element_type=f32) * factor
    top_score = jnp.max(scores, axis=-1, keepdims=True)
    expo = jnp.exp(scores - top_score)
    expo_sum = jnp.sum(expo, axis=-1, keepdims=True)
    log_total = top_score + jnp.log(expo_sum)
    probs_low = (expo / expo_sum).astype(bf16)
    mixed_heads = jnp.einsum("bhqk,bkhd->bqhd", probs_low, value_part, preferred_element_type=f32)
    mixed_heads = mixed_heads.reshape(row_count, feat_width).astype(bf16)
    attended = jnp.dot(mixed_heads, proj_full, preferred_element_type=f32) + proj_bias.astype(f32)
    middle = inputs + attended
    normal_two, inverse_two = norm_parts(middle)
    normed_two = (normal_two * gain_full_two.astype(f32) + bias_full_two.astype(f32)).astype(bf16)
    hidden = jnp.dot(normed_two, up_full, preferred_element_type=f32) + up_bias.astype(f32)
    active = jax.nn.gelu(hidden, approximate=False).astype(bf16)
    result = middle + (
        jnp.dot(active, down_full, preferred_element_type=f32) + down_bias.astype(f32)
    )
    layer_out = (result * live_rows).astype(bf16).reshape(tokens.shape)
    qkv_back, proj_back, up_back, down_back, gain_back_one, gain_back_two = (
        lax.all_gather(w_qkv, "shard", axis=0, tiled=True),
        lax.all_gather(w_proj, "shard", axis=0, tiled=True),
        lax.all_gather(w_up, "shard", axis=0, tiled=True),
        lax.all_gather(w_down, "shard", axis=0, tiled=True),
        lax.all_gather(gain_one, "shard", axis=0, tiled=True),
        lax.all_gather(gain_two, "shard", axis=0, tiled=True),
    )
    grad_out = out_grad.reshape(row_count, feat_width).astype(f32) * live_rows
    grad_branch = grad_out.astype(bf16)
    grad_down_b = jnp.sum(grad_branch.astype(f32), axis=0)
    grad_down_w = jnp.einsum("rf,rd->fd", active, grad_branch, preferred_element_type=f32)
    grad_active = jnp.einsum("rd,fd->rf", grad_branch, down_back, preferred_element_type=f32)
    grad_hidden = (grad_active * gelu_slope(hidden)).astype(bf16)
    grad_up_b = jnp.sum(grad_hidden.astype(f32), axis=0)
    grad_up_w = jnp.einsum("rd,rf->df", normed_two, grad_hidden, preferred_element_type=f32)
    grad_normed_two = jnp.einsum("rf,df->rd", grad_hidden, up_back, preferred_element_type=f32)
    grad_gain_two = jnp.sum(grad_normed_two * normal_two, axis=0)
    grad_bias_two = jnp.sum(grad_normed_two, axis=0)
    grad_middle = grad_out + norm_back(
        grad_normed_two * gain_back_two.astype(f32), normal_two, inverse_two
    )
    grad_attn = grad_middle.astype(bf16)
    grad_proj_b = jnp.sum(grad_attn.astype(f32), axis=0)
    grad_proj_w = jnp.einsum("rd,re->de", mixed_heads, grad_attn, preferred_element_type=f32)
    grad_mixed = jnp.einsum("re,de->rd", grad_attn, proj_back, preferred_element_type=f32)
    grad_mixed = grad_mixed.astype(bf16).reshape(slot_count, length, H, HD)
    scores_again = (
        jnp.einsum("bqhd,bkhd->bhqk", queries, key_part, preferred_element_type=f32) * factor
    )
    probs_again = jnp.exp(scores_again - log_total)
    grad_values = jnp.einsum("bhqk,bqhd->bkhd", probs_low, grad_mixed, preferred_element_type=f32)
    grad_probs = jnp.einsum("bqhd,bkhd->bhqk", grad_mixed, value_part, preferred_element_type=f32)
    row_delta = jnp.sum(grad_probs * probs_again, axis=-1, keepdims=True)
    grad_scores = (probs_again * (grad_probs - row_delta)).astype(bf16)
    grad_queries = (
        jnp.einsum("bhqk,bkhd->bqhd", grad_scores, key_part, preferred_element_type=f32) * factor
    )
    grad_keys = (
        jnp.einsum("bhqk,bqhd->bkhd", grad_scores, queries, preferred_element_type=f32) * factor
    )
    grad_joined = jnp.stack([grad_queries, grad_keys, grad_values], axis=2)
    grad_joined = grad_joined.reshape(row_count, 3 * feat_width).astype(bf16)
    joined_sums = jnp.sum(grad_joined.astype(f32), axis=0)
    grad_query_b = joined_sums[:feat_width]
    grad_value_b = joined_sums[2 * feat_width :]
    grad_qkv_w = jnp.einsum("rd,re->de", normed_one, grad_joined, preferred_element_type=f32)
    grad_normed_one = jnp.einsum("re,de->rd", grad_joined, qkv_back, preferred_element_type=f32)
    grad_gain_one = jnp.sum(grad_normed_one * normal_one, axis=0)
    grad_bias_one = jnp.sum(grad_normed_one, axis=0)
    grad_inputs = grad_middle + norm_back(
        grad_normed_one * gain_back_one.astype(f32), normal_one, inverse_one
    )
    grad_tokens = grad_inputs.astype(bf16).reshape(tokens.shape)
    all_grads = lax.psum(
        (
            lax.psum_scatter(
                grad_qkv_w.astype(jnp.bfloat16), "shard", scatter_dimension=0, tiled=True
            ).astype(jnp.float32),
            lax.psum_scatter(
                grad_query_b.astype(jnp.bfloat16), "shard", scatter_dimension=0, tiled=True
            ).astype(jnp.float32),
            lax.psum_scatter(
                grad_value_b.astype(jnp.bfloat16), "shard", scatter_dimension=0, tiled=True
            ).astype(jnp.float32),
            lax.psum_scatter(
                grad_proj_w.astype(jnp.bfloat16), "shard", scatter_dimension=0, tiled=True
            ).astype(jnp.float32),
            lax.psum_scatter(
                grad_proj_b.astype(jnp.bfloat16), "shard", scatter_dimension=0, tiled=True
            ).astype(jnp.float32),
            lax.psum_scatter(
                grad_gain_one.astype(jnp.bfloat16), "shard", scatter_dimension=0, tiled=True
            ).astype(jnp.float32),
            lax.psum_scatter(
                grad_bias_one.astype(jnp.bfloat16), "shard", scatter_dimension=0, tiled=True
            ).astype(jnp.float32),
            lax.psum_scatter(
                grad_gain_two.astype(jnp.bfloat16), "shard", scatter_dimension=0, tiled=True
            ).astype(jnp.float32),
            lax.psum_scatter(
                grad_bias_two.astype(jnp.bfloat16), "shard", scatter_dimension=0, tiled=True
            ).astype(jnp.float32),
            lax.psum_scatter(
                grad_up_w.astype(jnp.bfloat16), "shard", scatter_dimension=0, tiled=True
            ).astype(jnp.float32),
            lax.psum_scatter(
                grad_up_b.astype(jnp.bfloat16), "shard", scatter_dimension=0, tiled=True
            ).astype(jnp.float32),
            lax.psum_scatter(
                grad_down_w.astype(jnp.bfloat16), "shard", scatter_dimension=0, tiled=True
            ).astype(jnp.float32),
            lax.psum_scatter(
                grad_down_b.astype(jnp.bfloat16), "shard", scatter_dimension=0, tiled=True
            ).astype(jnp.float32),
        ),
        "rep",
    )
    return (
        layer_out,
        grad_tokens,
        all_grads[0],
        all_grads[1],
        all_grads[2],
        all_grads[3],
        all_grads[4],
        all_grads[5],
        all_grads[6],
        all_grads[7],
        all_grads[8],
        all_grads[9],
        all_grads[10],
        all_grads[11],
        all_grads[12],
    )


def solution(mesh):
    return jax.shard_map(
        per_device,
        mesh=mesh,
        in_specs=(
            P(("rep", "shard"), None, None),
            P(("rep", "shard")),
            P("shard", None),
            P("shard"),
            P("shard"),
            P("shard", None),
            P("shard"),
            P("shard"),
            P("shard"),
            P("shard"),
            P("shard"),
            P("shard", None),
            P("shard"),
            P("shard", None),
            P("shard"),
            P(("rep", "shard"), None, None),
        ),
        out_specs=(
            P(("rep", "shard"), None, None),
            P(("rep", "shard"), None, None),
            P("shard", None),
            P("shard"),
            P("shard"),
            P("shard", None),
            P("shard"),
            P("shard"),
            P("shard"),
            P("shard"),
            P("shard"),
            P("shard", None),
            P("shard"),
            P("shard", None),
            P("shard"),
        ),
        check_vma=False,
    )
```

profile of v0, /device:TPU:0, one launch (start us, length us, event | category | flops | bytes accessed | tf_op | source)
XLA Modules:
  0.0 788.7 jit_solution(14411562019421911148)
XLA Ops:
  11.1 2.0 reshape.172
  16.1 21.2 %all-reduce.19 = (bf16[768]{0:T(1024)(128)(2,1)S(1)}, bf16[768]{0:T(1024)(128)(2,1)S(1)}, bf16[768]{0:T(1024)(128)(2,1)S(1)}, bf16[768]{0:T(1024)(128)(2,1)S(1)}...) all-reduce(bf16[768]{0:T(1024)(128)(2,1)S(1)} %dynamic-update-slice, ...), channel_id=1, replica_groups=mesh['rep'=8,'shard'=4] {'shard'}, use_global_device_ids=true, to_apply=%add.3 | all-reduce | flops 5376 | bytes 21504
  38.0 13.4 %all-gather = bf16[4,1,768]{2,1,0:T(2,128)(2,1)S(1)} all-gather(bf16[1,1,768]{2,1,0:T(2,128)(2,1)S(1)} %reshape.198), channel_id=1, replica_groups=mesh['rep'=8,'shard'=4] {'shard'}, dimensions={0}, use_global_device_ids=true | all-gather | bytes 7680 | tf_op jit(solution)/shard_map/all_gather | solution.py:85
  53.4 2.0 reshape.173
  57.6 25.2 %all-gather.6.cloned.1.call-done = bf16[768,2304]{1,0:T(8,128)(2,1)} async-done(((bf16[192,2304]{1,0:T(8,128)(2,1)}), bf16[768,2304]{1,0:T(8,128)(2,1)}) %all-gather.6.cloned.1.call-update) | async-done | bytes 3538960 | tf_op jit(solution)/shard_map/all_gather | solution.py:75
  82.7 8.9 %add_convert_fusion = bf16[985,2304]{1,0:T(8,128)(2,1)} fusion(bf16[768,2304]{1,0:T(8,128)(2,1)} %all-gather.6.cloned.1.call-done, f32[2304]{0:T(1024)S(1)} %pad_maximum_fusion, f32[985,768]{1,0:T(8,128)} %reshape.172, f32[768]{0:T(1024)S(1)} %convert_element_type.204, f32[768]{0:T(1024)S(1)} %convert_element_type.203, f32[985]{0:T(1024)S(1)} %rsqrt.21, ...), kind=kOutput, calls=%fused_computation.34 | convolution fusion | flops 3494181120 | bytes 11126984 | tf_op jit(solution)/shard_map/dot_general | solution.py:94
  91.7 14.8 %reshape.226 = bf16[5,197,3,12,64]{4,3,2,1,0:T(8,128)(2,1)} reshape(bf16[985,2304]{1,0:T(8,128)(2,1)} %add_convert_fusion) | data formatting | bytes 9077760 | tf_op jit(solution)/shard_map/reshape | solution.py:98
  106.5 9.1 %fusion.37 = (bf16[5,197,1,12,64]{4,3,2,1,0:T(8,128)(2,1)}, bf16[5,197,1,12,64]{4,3,2,1,0:T(8,128)(2,1)}, bf16[5,197,1,12,64]{4,3,2,1,0:T(8,128)(2,1)}) fusion(bf16[5,197,3,12,64]{4,3,2,1,0:T(8,128)(2,1)} %reshape.226), kind=kLoop, calls=%fused_computation.103 | loop fusion | bytes 9077760 | tf_op jit(solution)/shard_map/slice | solution.py:101
  115.6 6.0 copy.75
  121.6 5.2 copy.76
  126.8 4.1 multiply_reduce_fusion.1
  131.0 2.9 fusion.16
  135.4 4.4 divide_convert_fusion
  140.5 5.0 copy.74
  145.5 4.1 convert_bitcast_fusion
  149.5 3.1 copy.58
  152.6 5.0 convert_element_type.212
  157.7 3.8 fusion.40
  163.8 39.9 %all-gather.10.cloned.1.call-done = bf16[768,3072]{1,0:T(8,128)(2,1)} async-done(((bf16[192,3072]{1,0:T(8,128)(2,1)}), bf16[768,3072]{1,0:T(8,128)(2,1)}) %all-gather.10.cloned.1.call-update) | async-done | bytes 4718608 | tf_op jit(solution)/shard_map/all_gather | solution.py:84
  203.6 35.7 %fusion.2 = (bf16[985,3072]{1,0:T(8,128)(2,1)}, f32[985,3072]{1,0:T(8,128)}) fusion(f32[3072]{0:T(1024)} %bitcast.71, bf16[768,3072]{1,0:T(8,128)(2,1)} %all-gather.10.cloned.1.call-done, f32[985,768]{1,0:T(8,128)} %copy-done.6, f32[768]{0:T(1024)} %convert_element_type.215, f32[768]{0:T(1024)S(1)} %convert_element_type.214, f32[985]{0:T(1024)S(1)} %add_rsqrt_fusion.1, ...), kind=kOutput, calls=%fused_computation.9 | convolution fusion | flops 4851306496 | bytes 25926344 | tf_op jit(solution)/shard_map/dot_general | solution.py:114
  239.4 53.6 %all-gather.12.cloned.1.call-done = bf16[3072,768]{1,0:T(8,128)(2,1)} async-done(((bf16[768,768]{1,0:T(8,128)(2,1)}), bf16[3072,768]{1,0:T(8,128)(2,1)}) %all-gather.12.cloned.1.call-update) | async-done | bytes 4718608 | tf_op jit(solution)/shard_map/all_gather | solution.py:86
  292.9 12.6 %fusion.41 = (bf16[3072]{0:T(1024)(128)(2,1)}, bf16[985,3072]{1,0:T(8,128)(2,1)S(1)}) fusion(f32[985,3072]{1,0:T(8,128)} %get-tuple-element.69, f32[3072]{0:T(1024)} %bitcast.72, bf16[3072,768]{1,0:T(8,128)(2,1)} %all-gather.12.cloned.1.call-done, f32[985,768]{1,0:T(8,128)} %reshape.173, f32[985]{0:T(1024)S(1)} %mul.194), kind=kOutput, calls=%fused_computation.107 | convolution fusion | flops 4685634048 | bytes 25922404 | tf_op jit(solution)/shard_map/rd,fd->rf/dot_general | solution.py:132
  305.6 6.1 multiply_reduce_fusion.3
  311.7 1.9 convert_reduce_fusion.1
  315.2 2.4 convolution_convert_fusion.4
  317.8 3.6 convolution_convert_fusion.3
  321.3 4.3 reshape.227
  325.6 6.2 copy.60
  331.9 12.8 %multiply_reduce_fusion = (f32[5,12,197]{2,1,0:T(8,128)S(1)}, f32[5,12,197,197]{2,3,1,0:T(8,128)}) fusion(f32[5,12,197,197]{2,3,1,0:T(8,128)} %copy-done, f32[5,12,197]{2,1,0:T(8,128)S(1)} %copy-done.17, bf16[5,197,12,64]{1,3,2,0:T(8,128)(2,1)} %copy.60, bf16[5,197,1,12,64]{1,4,3,0,2:T(8,128)(2,1)S(1)} %copy.74), kind=kOutput, calls=%fused_computation.3 | convolution fusion | flops 307355456 | bytes 21748800 | tf_op jit(solution)/shard_map/bqhd,bkhd->bhqk/dot_general | solution.py:152
  344.7 9.7 %multiply_convert_fusion = bf16[5,12,197,197]{2,3,1,0:T(8,128)(2,1)S(1)} fusion(f32[5,12,197,197]{2,3,1,0:T(8,128)} %get-tuple-element.72, f32[5,12,197,197]{2,3,1,0:T(8,128)} %copy-done, f32[5,12,197]{2,1,0:T(8,128)S(1)} %get-tuple-element.71, f32[5,12,197]{2,1,0:T(8,128)S(1)} %copy-done.17), kind=kLoop, calls=%fused_computation.2 | loop fusion | flops 11642700 | bytes 23379960 | tf_op jit(solution)/shard_map/convert_element_type | solution.py:154
  354.4 2.6 multiply_bitcast_fusion.1
  357.0 3.4 multiply_bitcast_fusion
  360.4 2.1 convolution_bitcast_fusion
  362.6 2.0 fusion.36
  364.5 8.8 %copy.65 = bf16[5,197,3,12,64]{1,0,4,3,2:T(8,128)(2,1)} copy(bf16[5,197,3,12,64]{1,4,3,0,2:T(8,128)(2,1)S(1)} %get-tuple-element.56) | data formatting | bytes 9077760 | tf_op jit(solution)/shard_map/convert_element_type | solution.py:162
  373.3 13.9 %convert_element_type.230 = bf16[985,2304]{0,1:T(8,128)(2,1)} reshape(bf16[5,197,3,12,64]{1,0,4,3,2:T(8,128)(2,1)} %copy.65) | data formatting | bytes 9077760 | tf_op jit(solution)/shard_map/convert_element_type | solution.py:162
  387.2 7.8 convolution_convert_fusion.2
  396.8 9.9 %convolution_convert_fusion.1 = bf16[768,3072]{1,0:T(8,128)(2,1)} fusion(bf16[985,3072]{1,0:T(8,128)(2,1)} %copy-done.42, f32[985,768]{1,0:T(8,128)S(1)} %copy-done.8, f32[768]{0:T(1024)S(1)} %copy-done.26, f32[768]{0:T(1024)S(1)} %convert_element_type.214, f32[985]{0:T(1024)S(1)} %add_rsqrt_fusion.1, f32[985]{0:T(1024)S(1)} %broadcast_multiply_fusion.5), kind=kOutput, calls=%fused_computation.36 | convolution fusion | flops 4653955072 | bytes 13810376 | tf_op jit(solution)/shard_map/rd,rf->df/dot_general | solution.py:135
  406.8 10.0 %convolution_convert_fusion = bf16[3072,768]{1,0:T(8,128)(2,1)} fusion(bf16[985,3072]{1,0:T(8,128)(2,1)} %get-tuple-element.68, f32[985,768]{1,0:T(8,128)} %reshape.173, f32[985]{0:T(1024)S(1)} %mul.194), kind=kOutput, calls=%fused_computation.35 | convolution fusion | flops 4651685376 | bytes 13800292 | tf_op jit(solution)/shard_map/rf,rd->fd/dot_general | solution.py:131
  420.5 9.5 %multiply_reduce_fusion.4 = (bf16[768]{0:T(1024)(128)(2,1)S(1)}, f32[985]{0:T(1024)S(1)}, f32[985]{0:T(1024)S(1)}, bf16[768]{0:T(1024)(128)(2,1)S(1)}, f32[985,768]{1,0:T(8,128)S(1)}) fusion(f32[985,768]{1,0:T(8,128)} %reshape.172, f32[985]{0:T(1024)S(1)} %copy-done.23, f32[985]{0:T(1024)S(1)} %copy-done.21, f32[768]{0:T(1024)S(1)} %copy-done.19, ...), kind=kOutput, calls=%fused_computation.44 | convolution fusion | flops 3492664576 | bytes 14151568 | tf_op jit(solution)/shard_map/re,de->rd/dot_general | solution.py:167
  430.1 2.1 add_convert_fusion.2
  432.1 2.9 reshape.171
  435.1 19.4 %all-reduce.18 = (bf16[768]{0:T(1024)(128)(2,1)S(1)}, bf16[768]{0:T(1024)(128)(2,1)S(1)}, bf16[768]{0:T(1024)(128)(2,1)S(1)}, bf16[768]{0:T(1024)(128)(2,1)S(1)}...) all-reduce(bf16[768]{0:T(1024)(128)(2,1)S(1)} %dynamic-update-slice, ...), channel_id=1, replica_groups=mesh['rep'=8,'shard'=4] {'shard'}, use_global_device_ids=true, to_apply=%add.7 | all-reduce | flops 9984 | bytes 39936
  454.5 10.2 %multiply_convert_fusion.2 = bf16[985,768]{1,0:T(8,128)(2,1)} fusion(f32[985,768]{1,0:T(8,128)S(1)} %copy-done.8, bf16[985,3072]{1,0:T(8,128)(2,1)} %get-tuple-element.68, bf16[3072,768]{1,0:T(8,128)(2,1)} %all-gather.12.cloned.1.call-done, f32[985]{0:T(1024)S(1)} %mul.194, f32[768]{0:T(1024)S(1)} %convert_element_type.219), kind=kOutput, calls=%fused_computation.49 | convolution fusion | flops 4650840064 | bytes 15316324 | tf_op jit(solution)/shard_map/dot_general | solution.py:117
  464.7 2.9 reshape.169
  468.3 80.5 %reduce-scatter.9.cloned.1.call-done = bf16[192,3072]{1,0:T(8,128)(2,1)} async-done(((bf16[768,3072]{1,0:T(8,128)(2,1)}), bf16[192,3072]{1,0:T(8,128)(2,1)}) %reduce-scatter.9.cloned.1.call-update) | async-done | bytes 1179664 | tf_op jit(solution)/shard_map/reduce_scatter | solution.py:203
  548.9 88.1 %reduce-scatter.11.cloned.1.call-done = bf16[768,768]{1,0:T(8,128)(2,1)} async-done(((bf16[3072,768]{1,0:T(8,128)(2,1)}), bf16[768,768]{1,0:T(8,128)(2,1)}) %reduce-scatter.11.cloned.1.call-update) | async-done | bytes 1179664 | tf_op jit(solution)/shard_map/reduce_scatter | solution.py:209
  637.0 144.6 %all-reduce.21 = (f32[192,2304]{1,0:T(8,128)}, f32[192]{0:T(256)}, f32[192]{0:T(256)}, f32[192,768]{1,0:T(8,128)}, f32[192]{0:T(256)}, /*index=5*/f32[192]{0:T(2...) all-reduce(bf16[192,2304]{1,0:T(8,128)(2,1)} %reduce-scatter.5.clon, ...), channel_id=1, replica_groups=mesh['rep'=8,'shard'=4] {'rep'}, use_global_device_ids=true, to_apply=%region_12.0 | all-reduce | flops 1771776 | bytes 10635264 | tf_op jit(solution)/shard_map/psum | solution.py:174
  (170 shorter events, 21.3 us)
Async XLA Ops:
  7.2 2.9 copy-start.4
  7.2 75.5 %all-gather.6.cloned.1.call-start = ((), (), s32[]{:S(2)}) async-start(), calls=%async_computation.4 | async-start | bytes 4423680 | tf_op jit(solution)/shard_map/all_gather | solution.py:75
  7.9 149.8 %all-gather.8.cloned.1.call-start = ((), (), s32[]{:S(2)}) async-start(), calls=%async_computation.5 | async-start | bytes 1474560 | tf_op jit(solution)/shard_map/all_gather | solution.py:78
  8.7 194.9 %all-gather.10.cloned.1.call-start = ((), (), s32[]{:S(2)}) async-start(), calls=%async_computation.6 | async-start | bytes 5898240 | tf_op jit(solution)/shard_map/all_gather | solution.py:84
  9.4 283.5 %all-gather.12.cloned.1.call-start = ((), (), s32[]{:S(2)}) async-start(), calls=%async_computation.7 | async-start | bytes 5898240 | tf_op jit(solution)/shard_map/all_gather | solution.py:86
  10.0 458.3 %reduce-scatter.7.cloned.1.call-start = ((), (), s32[]{:S(2)}) async-start(), calls=%async_computation.9 | async-start | bytes 1474560 | tf_op jit(solution)/shard_map/reduce_scatter | solution.py:185
  10.1 3.1 copy-start.31
  10.1 4.3 copy-start.34
  10.1 4.6 copy-start.35
  10.1 4.8 copy-start.36
  10.1 5.0 copy-start.37
  10.1 5.2 copy-start.38
  10.1 5.5 copy-start.39
  10.1 5.7 copy-start.40
  10.4 27.6 %copy-start.32 = (bf16[768]{0:T(1024)(128)(2,1)S(1)}, bf16[768]{0:T(1024)(128)(2,1)}, u32[]{:S(2)}) copy-start(bf16[768]{0:T(1024)(128)(2,1)} %param.28) | copy-start | bytes 4612
  10.4 42.9 %copy-start.15 = (bf16[5,197,768]{2,1,0:T(8,128)(2,1)S(1)}, bf16[5,197,768]{2,1,0:T(8,128)(2,1)}, u32[]{:S(2)}) copy-start(bf16[5,197,768]{2,1,0:T(8,128)(2,1)} %param.31) | copy-start | bytes 4538884
  11.1 71.6 %copy-start.20 = (f32[985]{0:T(1024)}, f32[985]{0:T(1024)S(1)}, u32[]{:S(2)}) copy-start(f32[985]{0:T(1024)S(1)} %div.35) | copy-start | bytes 11824
  37.2 45.5 %copy-start.18 = (f32[768]{0:T(1024)}, f32[768]{0:T(1024)S(1)}, u32[]{:S(2)}) copy-start(f32[768]{0:T(1024)S(1)} %convert_element_type.203) | copy-start | bytes 9220
  37.4 45.4 %copy-start.22 = (f32[985]{0:T(1024)}, f32[985]{0:T(1024)S(1)}, u32[]{:S(2)}) copy-start(f32[985]{0:T(1024)S(1)} %rsqrt.21) | copy-start | bytes 11824
  126.8 4.1 copy-start.1
  130.9 4.5 copy-start
  292.9 12.6 %copy-start.7 = (f32[985,768]{1,0:T(8,128)S(1)}, f32[985,768]{1,0:T(8,128)}, u32[]{:S(2)}) copy-start(f32[985,768]{1,0:T(8,128)} %copy-done.6) | copy-start | bytes 9077764
  292.9 12.6 %copy-start.33 = (bf16[768,3072]{1,0:T(8,128)(2,1)S(1)}, bf16[768,3072]{1,0:T(8,128)(2,1)}, u32[]{:S(2)}) copy-start(bf16[768,3072]{1,0:T(8,128)(2,1)} %all-gather.10.cloned.1.call-done) | copy-start | bytes 14155780
  305.6 6.1 copy-start.42
  305.6 6.1 copy-start.12
  317.7 150.6 %reduce-scatter.5.cloned.1.call-start = ((), (), s32[]{:S(2)}) async-start(), calls=%async_computation.8 | async-start | bytes 4423680 | tf_op jit(solution)/shard_map/reduce_scatter | solution.py:176
  325.6 6.2 copy-start.17
  331.9 28.5 %slice-start = ((s8[6144000]{0:T(1024)(128)(4,1)}), s8[1949696]{0:T(1024)(128)(4,1)S(1)}, s32[]{:S(2)}) async-start(s8[6144000]{0:T(1024)(128)(4,1)} %bitcast.69), calls=%async_computation.12 | async-start | bytes 3899392
  344.7 9.7 %copy-start.2 = (bf16[5,197,1,12,64]{1,4,3,0,2:T(8,128)(2,1)S(1)}, bf16[5,197,1,12,64]{1,4,3,0,2:T(8,128)(2,1)}, u32[]{:S(2)}) copy-start(bf16[5,197,1,12,64]{1,4,3,0,2:T(8,128)(2,1)} %copy-done.1) | copy-start | bytes 4538884
  344.7 15.7 %slice-start.1 = ((s8[6144000]{0:T(1024)(128)(4,1)}), s8[4194304]{0:T(1024)(128)(4,1)S(1)}, s32[]{:S(2)}) async-start(s8[6144000]{0:T(1024)(128)(4,1)} %bitcast.69), calls=%async_computation.13 | async-start | bytes 8388608
  354.4 2.6 copy-start.3
  357.0 3.4 copy-start.5
  360.4 2.1 copy-start.13
  360.4 2.1 copy-start.14
  373.3 13.9 %copy-start.16 = (bf16[985,768]{1,0:T(8,128)(2,1)S(1)}, bf16[985,768]{1,0:T(8,128)(2,1)}, u32[]{:S(2)}) copy-start(bf16[985,768]{1,0:T(8,128)(2,1)} %convert_element_type.233) | copy-start | bytes 4538884
  395.0 1.9 copy-start.8
  395.0 1.9 copy-start.26
  395.0 153.9 %reduce-scatter.9.cloned.1.call-start = ((), (), s32[]{:S(2)}) async-start(), calls=%async_computation.10 | async-start | bytes 5898240 | tf_op jit(solution)/shard_map/reduce_scatter | solution.py:203
  406.7 230.3 %reduce-scatter.11.cloned.1.call-start = ((), (), s32[]{:S(2)}) async-start(), calls=%async_computation.11 | async-start | bytes 5898240 | tf_op jit(solution)/shard_map/reduce_scatter | solution.py:209
  416.8 3.7 copy-start.19
  416.8 3.7 copy-start.21
  416.8 3.6 copy-start.23
  420.4 9.6 %copy-start.10 = (f32[985,768]{1,0:T(8,128)S(1)}, f32[985,768]{1,0:T(8,128)}, u32[]{:S(2)}) copy-start(f32[985,768]{1,0:T(8,128)} %copy-done.9) | copy-start | bytes 9077764
  420.4 9.6 %copy-start.11 = (f32[985,768]{1,0:T(8,128)S(1)}, f32[985,768]{1,0:T(8,128)}, u32[]{:S(2)}) copy-start(f32[985,768]{1,0:T(8,128)} %reshape.172) | copy-start | bytes 9077764
  430.0 5.0 copy-start.24
  430.0 5.0 copy-start.25
  430.0 5.0 copy-start.29
  430.0 5.0 copy-start.30
  (5 other events, 6.8 us)
Sparse Core Ops, SparseCore 0:
  9.6 73.0 all-gather.5
  84.3 29.1 all-gather.7
  115.0 88.5 all-gather.9
  205.0 87.8 all-gather.11
  317.8 27.6 reduce-scatter.6
  395.1 65.7 reduce-scatter.4
  463.2 85.5 reduce-scatter.8
  551.2 85.7 reduce-scatter.10
where the time goes:
time: 797 us; the launch traced here: 789 us
  waiting for transfers between devices  290 us (36%)
  blocking collectives  199 us (25%)
  matrix products  150 us (19%)
  local copies, waits for them, and re-layouts  103 us (13%)
  other arithmetic  29.4 us (4%)
  between operations  17.5 us (2%)
    psum x1, blocking collectives, per_device(): lax.psum((lax.psum_scatter(grad_qkv_w.astype(jnp.bfloat16), 'shard', scat...  145 us
    reduce_scatter x1, waiting for transfers between devices, per_device(): lax.psum_scatter(grad_down_w.astype(jnp.bfloat16), 'shard', scatter_dimen...  88.1 us
    reduce_scatter x1, waiting for transfers between devices, per_device(): lax.psum_scatter(grad_up_w.astype(jnp.bfloat16), 'shard', scatter_dimensi...  80.5 us
    all_gather x1, waiting for transfers between devices, per_device(): lax.all_gather(w_down, 'shard', axis=0, tiled=True)  53.6 us
    unnamed x2, blocking collectives  40.6 us
    all_gather x1, waiting for transfers between devices, per_device(): lax.all_gather(w_up, 'shard', axis=0, tiled=True)  39.9 us
    dot_general x1, matrix products, per_device(): jnp.dot(normed_two, up_full, preferred_element_type=f32)  35.7 us
    unnamed x111, local copies, waits for them, and re-layouts  26 us
  transfers between devices with their start and end apart: 8, of which 5 were waited for; matrix products, arithmetic and copies ran while one was open for 32% of the time, Pallas kernels for 0%

commit v1 on v0

v1 whole, which is shorter than its diff:
```python
import functools
import math

import jax
import jax.numpy as jnp
from jax import lax
from jax.experimental import pallas as pl
from jax.experimental.pallas import tpu as pltpu
from jax.sharding import Mesh, PartitionSpec as P

H = 12
HD = 64
EPSILON = 1e-06
ROOT_HALF = 1.0 / math.sqrt(2.0)
INV_ROOT_TAU = 1.0 / math.sqrt(2.0 * math.pi)
f32 = jnp.float32
bf16 = jnp.bfloat16
SWAP = [(0, 1), (1, 0)]


def norm_parts(values_in):
    row_mean = jnp.mean(values_in, axis=-1, keepdims=True)
    centred = values_in - row_mean
    inverse = lax.rsqrt(jnp.mean(centred * centred, axis=-1, keepdims=True) + EPSILON)
    return (centred * inverse, inverse)


def norm_back(grad_normal, normal_rows, inverse_rows):
    first_mean = jnp.mean(grad_normal, axis=-1, keepdims=True)
    second_mean = jnp.mean(grad_normal * normal_rows, axis=-1, keepdims=True)
    return inverse_rows * (grad_normal - first_mean - normal_rows * second_mean)


def dot_nt(a, b):
    return lax.dot_general(a, b, (((1,), (1,)), ((), ())), preferred_element_type=f32)


def dot_tn(a, b):
    return lax.dot_general(a, b, (((0,), (0,)), ((), ())), preferred_element_type=f32)


def dot_nn(a, b):
    return jnp.dot(a, b, preferred_element_type=f32)


def attention_kernel(length, qkv_ref, out_ref, prob_ref):
    rows = qkv_ref.shape[1]
    width = H * HD
    first = lax.broadcasted_iota(jnp.int32, (1, 2 * HD), 1) < HD
    key_live = lax.broadcasted_iota(jnp.int32, (rows, 1), 0) < length
    for pair in range(H // 2):
        lanes = pl.ds(pair * 2 * HD, 2 * HD)
        q2 = qkv_ref[0, :, pl.ds(pair * 2 * HD, 2 * HD)] * jnp.asarray(HD ** (-0.5), bf16)
        k2 = qkv_ref[0, :, pl.ds(width + pair * 2 * HD, 2 * HD)]
        v2 = qkv_ref[0, :, pl.ds(2 * width + pair * 2 * HD, 2 * HD)]
        total = None
        for half in range(2):
            mask = first if half == 0 else jnp.logical_not(first)
            scores = dot_nt(jnp.where(mask, k2, jnp.zeros_like(k2)), q2)
            scores = jnp.where(key_live, scores, -1e30)
            expo = jnp.exp(scores - jnp.max(scores, axis=0, keepdims=True))
            probs = (expo * (1.0 / jnp.sum(expo, axis=0, keepdims=True))).astype(bf16)
            prob_ref[0, 2 * pair + half] = probs
            part = dot_tn(probs, jnp.where(mask, v2, jnp.zeros_like(v2)))
            total = part if total is None else total + part
        out_ref[0, :, lanes] = total.astype(bf16)


def attention_back_kernel(qkv_ref, prob_ref, grad_ref, out_ref, sums_ref):
    width = H * HD
    first = lax.broadcasted_iota(jnp.int32, (1, 2 * HD), 1) < HD
    scale = jnp.asarray(HD ** (-0.5), f32)

    @pl.when(pl.program_id(0) == 0)
    def _():
        sums_ref[...] = jnp.zeros_like(sums_ref)

    for pair in range(H // 2):
        spots = [pl.ds(part * width + pair * 2 * HD, 2 * HD) for part in range(3)]
        q2 = qkv_ref[0, :, spots[0]]
        k2 = qkv_ref[0, :, spots[1]]
        v2 = qkv_ref[0, :, spots[2]]
        g2 = grad_ref[0, :, spots[0]]
        totals = [None, None, None]
        for half in range(2):
            mask = first if half == 0 else jnp.logical_not(first)

            def keep(v):
                return jnp.where(mask, v, jnp.zeros_like(v))

            probs = prob_ref[0, 2 * pair + half]
            g_half = keep(g2)
            grad_probs = dot_nt(v2, g_half)
            probs_wide = probs.astype(f32)
            delta = jnp.sum(grad_probs * probs_wide, axis=0, keepdims=True)
            grad_scores = (probs_wide * (grad_probs - delta)).astype(bf16)
            parts = (
                dot_tn(grad_scores, keep(k2)),
                dot_nn(grad_scores, keep(q2)),
                dot_nn(probs, g_half),
            )
            totals = [p if t is None else t + p for t, p in zip(totals, parts)]
        for part in range(3):
            value = totals[part] if part == 2 else totals[part] * scale
            value = value.astype(bf16)
            out_ref[0, :, spots[part]] = value
            sums_ref[:, spots[part]] += jnp.sum(value.astype(f32), axis=0, keepdims=True)


def attention(qkv, length):
    slots, rows, wide = qkv.shape
    width = wide // 3
    return pl.pallas_call(
        functools.partial(attention_kernel, length),
        grid=(slots,),
        in_specs=[pl.BlockSpec((1, rows, wide), lambda i: (i, 0, 0))],
        out_specs=[
            pl.BlockSpec((1, rows, width), lambda i: (i, 0, 0)),
            pl.BlockSpec((1, H, rows, rows), lambda i: (i, 0, 0, 0)),
        ],
        out_shape=[
            jax.ShapeDtypeStruct((slots, rows, width), bf16),
            jax.ShapeDtypeStruct((slots, H, rows, rows), bf16),
        ],
        compiler_params=pltpu.CompilerParams(vmem_limit_bytes=28 * 2**20),
        cost_estimate=pl.CostEstimate(
            flops=slots * H * 4 * rows * rows * 256, bytes_accessed=30000000, transcendentals=0
        ),
        name="attention",
    )(qkv)


def attention_back(qkv, probs, grad):
    slots, rows, wide = qkv.shape
    width = wide // 3
    return pl.pallas_call(
        attention_back_kernel,
        grid=(slots,),
        in_specs=[
            pl.BlockSpec((1, rows, wide), lambda i: (i, 0, 0)),
            pl.BlockSpec((1, H, rows, rows), lambda i: (i, 0, 0, 0)),
            pl.BlockSpec((1, rows, width), lambda i: (i, 0, 0)),
        ],
        out_specs=[
            pl.BlockSpec((1, rows, wide), lambda i: (i, 0, 0)),
            pl.BlockSpec((1, wide), lambda i: (0, 0)),
        ],
        out_shape=[
            jax.ShapeDtypeStruct((slots, rows, wide), bf16),
            jax.ShapeDtypeStruct((1, wide), f32),
        ],
        compiler_params=pltpu.CompilerParams(vmem_limit_bytes=28 * 2**20),
        cost_estimate=pl.CostEstimate(
            flops=slots * H * 8 * rows * rows * 256, bytes_accessed=60000000, transcendentals=0
        ),
        name="attention_back",
    )(qkv, probs, grad)


class Net:
    def __init__(self, rep_bits, shard_bits):
        self.core, self.x, self.y = rep_bits[-1], rep_bits[-2], rep_bits[-3]
        self.extra = tuple(rep_bits[:-3])
        self.rep = tuple(rep_bits)
        self.shard = tuple(shard_bits)
        self.dims = self.shard + (self.x, self.y)
        self.bit = {name: lax.axis_index(name) for name in self.rep + self.shard}

    def place(self, mine, other, name, spot):
        bit = self.bit[name]
        low = jnp.where(bit == 0, mine, other)
        high = jnp.where(bit == 0, other, mine)
        return low, high, spot

    def grow(self, piece, have, name):
        other = lax.ppermute(piece, name, SWAP)
        have = tuple(d for d in self.dims if d in have or d == name)
        low, high, spot = self.place(piece, other, name, have.index(name))
        return jnp.stack([low, high], axis=spot), have

    def halve(self, piece, have, name):
        spot = have.index(name)
        bit = self.bit[name]
        send = lax.dynamic_index_in_dim(piece, 1 - bit, spot, keepdims=False)
        keep = lax.dynamic_index_in_dim(piece, bit, spot, keepdims=False)
        other = lax.ppermute(send, name, SWAP)
        piece = (keep.astype(f32) + other.astype(f32)).astype(bf16)
        return piece, tuple(d for d in have if d != name)

    def gather(self, weight, streams):
        rows, columns = weight.shape
        half, fine = columns // 2, rows // 4
        mine = lax.dynamic_slice_in_dim(weight, self.bit[self.core] * half, half, 1)
        mine = mine.reshape(2, 2, fine, half)
        mine = lax.dynamic_index_in_dim(mine, self.bit[self.x], 0, keepdims=False)
        mine = lax.dynamic_index_in_dim(mine, self.bit[self.y], 0, keepdims=False)
        done = []
        for start, stop, order in streams(self, half):
            piece, have = mine[:, start:stop], ()
            for name in order:
                piece, have = self.grow(piece, have, name)
            other = lax.ppermute(piece, self.core, SWAP)
            low, high, _ = self.place(piece, other, self.core, None)
            done.append((low, high))
        full = jnp.concatenate([d[0] for d in done] + [d[1] for d in done], axis=-1)
        return full.reshape(-1, columns)

    def reduce(self, left, right, streams):
        columns = right.shape[1]
        half = columns // 2
        core = self.bit[self.core]
        send = lax.dynamic_slice_in_dim(right, (1 - core) * half, half, 1)
        keep = lax.dynamic_slice_in_dim(right, core * half, half, 1)
        other = lax.ppermute(dot_tn(left, send).astype(bf16), self.core, SWAP)
        total = (dot_tn(left, keep) + other.astype(f32)).astype(bf16)
        count = len(self.dims)
        total = total.reshape((2,) * count + (-1, half))
        done = []
        for start, stop, order in streams(self, half):
            piece, have = total[..., start:stop], self.dims
            for name in order:
                piece, have = self.halve(piece, have, name)
            for name in self.extra:
                piece = (piece.astype(f32) + lax.ppermute(piece, name, SWAP).astype(f32)).astype(bf16)
            have = ()
            for name in reversed([n for n in order if n in (self.x, self.y)]):
                piece, have = self.grow(piece, have, name)
            other = lax.ppermute(piece, self.core, SWAP)
            low, high, _ = self.place(piece, other, self.core, None)
            done.append((low, high))
        full = jnp.concatenate([d[0] for d in done] + [d[1] for d in done], axis=-1)
        return full.reshape(-1, columns).astype(f32)

    def rotations(self, pick):
        count = 2 ** len(self.shard)
        got = [pick(0)]
        for k in range(1, count):
            got.append(
                lax.ppermute(pick(k), self.shard, [(i, (i + k) % count) for i in range(count)])
            )
        return got

    def place_in_group(self):
        me = 0
        for name in self.shard:
            me = 2 * me + self.bit[name]
        return me

    def gather_small(self, small):
        got = jnp.stack(self.rotations(lambda k: small))
        count = got.shape[0]
        me = self.place_in_group()
        rows = [
            lax.dynamic_index_in_dim(got, (me + count - s) % count, 0, keepdims=False)
            for s in range(count)
        ]
        return jnp.stack(rows)

    def reduce_small(self, values):
        count = values.shape[0]
        me = self.place_in_group()
        got = self.rotations(
            lambda k: lax.dynamic_index_in_dim(values, (me + k) % count, 0, keepdims=False)
        )
        total = functools.reduce(jnp.add, got)
        for name in reversed(self.rep):
            total = total + lax.ppermute(total, name, SWAP)
        return total


def both_ways(net, half):
    cut = (half // 256) * 128
    z = net.shard
    return [(0, cut, z + (net.x, net.y)), (cut, half, z + (net.y, net.x))]


def x_way(net, half):
    return [(0, half, net.shard + (net.x, net.y))]


def y_way(net, half):
    return [(0, half, net.shard + (net.y, net.x))]


def down_along(net, half):
    return [(0, half, net.shard[::-1] + (net.x, net.y))]


def down_across(net, half):
    return [(0, half, (net.x, net.y) + net.shard[::-1])]


def down_across_y(net, half):
    return [(0, half, (net.y, net.x) + net.shard[::-1])]


def down_both(net, half):
    cut = (half // 256) * 128
    z = net.shard[::-1]
    return [(0, cut, z + (net.x, net.y)), (cut, half, (net.y, net.x) + z)]


def per_device(
    rep_bits,
    shard_bits,
    tokens,
    counts,
    w_qkv,
    b_query,
    b_value,
    w_proj,
    b_proj,
    gain_one,
    bias_one,
    gain_two,
    bias_two,
    w_up,
    b_up,
    w_down,
    b_down,
    out_grad,
):
    net = Net(rep_bits, shard_bits)
    group = 2 ** len(shard_bits)
    slot_count, length, width = tokens.shape
    padded = -(-length // 16) * 16
    row_count = slot_count * padded
    wide = w_up.shape[1]
    part = width // group
    fill = ((0, 0), (0, padded - length), (0, 0))

    small = jnp.stack(
        [b_query, b_value, b_proj, gain_one, bias_one, gain_two, bias_two, b_down]
    )
    small = jnp.concatenate([small, b_up.reshape(-1, part)], axis=0)
    small = net.gather_small(small).astype(f32)
    rows = small[:, :8].transpose(1, 0, 2).reshape(8, width)
    query_bias, value_bias, proj_bias, gain_1, bias_1, gain_2, bias_2, down_bias = (
        rows[i] for i in range(8)
    )
    up_bias = small[:, 8:].reshape(wide)

    qkv_full = net.gather(w_qkv, both_ways)
    proj_full = net.gather(w_proj, x_way)
    up_full = net.gather(w_up, x_way)
    down_full = net.gather(w_down, y_way)

    live_slots = (jnp.arange(slot_count, dtype=jnp.int32) < counts[0]).astype(f32)
    live_rows = jnp.repeat(live_slots, padded)[:, None]
    inputs = jnp.pad(tokens, fill).reshape(row_count, width).astype(f32)
    normal_one, inverse_one = norm_parts(inputs)
    normed_one = (normal_one * gain_1 + bias_1).astype(bf16)
    qkv_bias = jnp.concatenate([query_bias, jnp.zeros_like(query_bias), value_bias])
    joined = (dot_nn(normed_one, qkv_full) + qkv_bias).astype(bf16)
    joined = joined.reshape(slot_count, padded, 3 * width)
    mixed, probs = attention(joined, length)
    mixed = mixed.reshape(row_count, width)
    middle = inputs + (dot_nn(mixed, proj_full) + proj_bias)
    normal_two, inverse_two = norm_parts(middle)
    normed_two = (normal_two * gain_2 + bias_2).astype(bf16)
    hidden = dot_nn(normed_two, up_full) + up_bias
    share = 0.5 * (1.0 + lax.erf(hidden * ROOT_HALF))
    active = (hidden * share).astype(bf16)
    slope = (share + hidden * jnp.exp(-0.5 * hidden * hidden) * INV_ROOT_TAU).astype(bf16)
    result = middle + (dot_nn(active, down_full) + down_bias)
    layer_out = (result * live_rows).astype(bf16)
    layer_out = layer_out.reshape(slot_count, padded, width)[:, :length]

    grad_branch = jnp.pad(out_grad, fill).reshape(row_count, width)
    grad_branch = grad_branch * live_rows.astype(bf16)
    grad_down_b = jnp.sum(grad_branch.astype(f32), axis=0)
    grad_down_w = net.reduce(active, grad_branch, down_along)
    grad_active = dot_nt(grad_branch, down_full)
    grad_hidden = (grad_active * slope.astype(f32)).astype(bf16)
    grad_up_b = jnp.sum(grad_hidden.astype(f32), axis=0)
    grad_up_w = net.reduce(normed_two, grad_hidden, down_across)
    grad_normed_two = dot_nt(grad_hidden, up_full)
    grad_gain_two = jnp.sum(grad_normed_two * normal_two, axis=0)
    grad_bias_two = jnp.sum(grad_normed_two, axis=0)
    grad_middle = grad_branch.astype(f32) + norm_back(
        grad_normed_two * gain_2, normal_two, inverse_two
    )
    grad_attn = grad_middle.astype(bf16)
    grad_proj_b = jnp.sum(grad_attn.astype(f32), axis=0)
    grad_proj_w = net.reduce(mixed, grad_attn, down_across_y)
    grad_mixed = dot_nt(grad_attn, proj_full).astype(bf16)
    grad_joined, joined_sums = attention_back(
        joined, probs, grad_mixed.reshape(slot_count, padded, width)
    )
    grad_joined = grad_joined.reshape(row_count, 3 * width)
    grad_query_b = joined_sums[0, :width]
    grad_value_b = joined_sums[0, 2 * width :]
    grad_qkv_w = net.reduce(normed_one, grad_joined, down_both)
    grad_normed_one = dot_nt(grad_joined, qkv_full)
    grad_gain_one = jnp.sum(grad_normed_one * normal_one, axis=0)
    grad_bias_one = jnp.sum(grad_normed_one, axis=0)
    grad_inputs = grad_middle + norm_back(grad_normed_one * gain_1, normal_one, inverse_one)
    grad_tokens = grad_inputs.astype(bf16).reshape(slot_count, padded, width)[:, :length]

    def by_owner(vectors):
        return jnp.stack(vectors).reshape(len(vectors), group, -1).transpose(1, 0, 2)

    early = by_owner([grad_proj_b, grad_gain_two, grad_bias_two, grad_down_b])
    early_up = grad_up_b.reshape(group, -1, part)
    early = net.reduce_small(jnp.concatenate([early, early_up], axis=1))
    late = net.reduce_small(by_owner([grad_query_b, grad_value_b, grad_gain_one, grad_bias_one]))
    return (
        layer_out,
        grad_tokens,
        grad_qkv_w,
        late[0],
        late[1],
        grad_proj_w,
        early[0],
        late[2],
        late[3],
        early[1],
        early[2],
        grad_up_w,
        early[4:].reshape(-1),
        grad_down_w,
        early[3],
    )


def solution(mesh):
    rep, shard = mesh.shape["rep"], mesh.shape["shard"]
    rep_bits = tuple(f"r{i}" for i in range(rep.bit_length() - 1))
    shard_bits = tuple(f"s{i}" for i in range(shard.bit_length() - 1))
    fine = Mesh(mesh.devices.reshape((2,) * (len(rep_bits) + len(shard_bits))), rep_bits + shard_bits)
    every = P(rep_bits + shard_bits, None, None)
    matrix = P(shard_bits, None)
    vector = P(shard_bits)
    return jax.shard_map(
        functools.partial(per_device, rep_bits, shard_bits),
        mesh=fine,
        in_specs=(
            every,
            P(rep_bits + shard_bits),
            matrix,
            vector,
            vector,
            matrix,
            vector,
            vector,
            vector,
            vector,
            vector,
            matrix,
            vector,
            matrix,
            vector,
            every,
        ),
        out_specs=(
            every,
            every,
            matrix,
            vector,
            vector,
            matrix,
            vector,
            vector,
            vector,
            vector,
            vector,
            matrix,
            vector,
            matrix,
            vector,
        ),
        check_vma=False,
    )
```

time: 797 us -> 413 us (0.52)
  blocking collectives: 199 us -> 0 us
  waiting for transfers between devices: 290 us -> 126 us
  starting transfers between devices: 0.32 us -> 84.4 us
  local copies, waits for them, and re-layouts: 103 us -> 40.7 us
  matrix products: 150 us -> 94.7 us
  Pallas kernels: 0 us -> 20.5 us
  between operations: 17.5 us -> 3.39 us
    reduce_scatter x4 -> x0, waiting for transfers between devices: 169 us -> none  [the longest x1 88.1 us: per_device(): lax.psum_scatter(grad_down_w.astype(jnp.bfloat16), 'shard', scatter_dimen...]
    psum x1 -> x0, blocking collectives: 145 us -> none  [per_device(): lax.psum((lax.psum_scatter(grad_qkv_w.astype(jnp.bfloat16), 'shard', scat...]
    ppermute x0 -> x79, waiting for transfers between devices: none -> 126 us  [the longest x20 79.3 us: halve(): other = lax.ppermute(send, name, SWAP)]
    all_gather x4 -> x0, waiting for transfers between devices: 119 us -> none  [the longest x1 53.6 us: per_device(): lax.all_gather(w_down, 'shard', axis=0, tiled=True)]
    ppermute x0 -> x79, starting transfers between devices: none -> 84.4 us  [the longest x30 39.2 us: grow(): other = lax.ppermute(piece, name, SWAP)]
    dot_general x18 -> x16, matrix products: 150 us -> 94.7 us  [the longest x4 36.8 us: dot_nt(): lax.dot_general(a, b, (((1,), (1,)), ((), ())), preferred_element_type=f32)]
    unnamed x2 -> x0, blocking collectives: 40.6 us -> none
    convert_element_type x9 -> x2, local copies, waits for them, and re-layouts: 36.5 us -> 2.19 us  [reduce(): return full.reshape(-1, columns).astype(f32)]
  transfers between devices with their start and end apart: 8 -> 79, of which waited for: 5 -> 29; matrix products, arithmetic and copies ran while one was open for 32% -> 24% of each run, Pallas kernels for 0% -> 5%
where the time goes in v1:
time: 413 us; the launch traced here: 405 us
  waiting for transfers between devices  126 us (31%)
  matrix products  94.7 us (23%)
  starting transfers between devices  84.4 us (20%)
  local copies, waits for them, and re-layouts  40.7 us (10%)
  other arithmetic  35.2 us (9%)
  Pallas kernels  20.5 us (5%)
    ppermute x20, waiting for transfers between devices, halve(): other = lax.ppermute(send, name, SWAP)  79.3 us
    ppermute x30, waiting for transfers between devices, grow(): other = lax.ppermute(piece, name, SWAP)  43 us
    ppermute x30, starting transfers between devices, grow(): other = lax.ppermute(piece, name, SWAP)  39.2 us
    dot_general x4, matrix products, dot_nt(): lax.dot_general(a, b, (((1,), (1,)), ((), ())), preferred_element_type=f32)  36.8 us
    dot_general x8, matrix products, dot_tn(): lax.dot_general(a, b, (((0,), (0,)), ((), ())), preferred_element_type=f32)  32.2 us
    dot_general x4, matrix products, dot_nn(): return jnp.dot(a, b, preferred_element_type=f32)  25.7 us
    ppermute x20, starting transfers between devices, halve(): other = lax.ppermute(send, name, SWAP)  22.2 us
    ppermute x9, starting transfers between devices, rotations(): lax.ppermute(pick(k), self.shard, [(i, (i + k) % count) for i in range(co...  16 us
  transfers between devices with their start and end apart: 79, of which 29 were waited for; matrix products, arithmetic and copies ran while one was open for 24% of the time, Pallas kernels for 5%

profile of v1, /device:TPU:0, one launch (start us, length us, event | category | flops | bytes accessed | tf_op | source)
XLA Modules:
  0.0 405.4 jit_solution(571043899642979805)
XLA Ops:
  6.9 3.1 collective-permute-start
  10.0 2.6 collective-permute-start.1
  16.0 2.8 collective-permute-start.18
  24.1 3.1 convert_reduce_fusion.1
  28.0 2.6 pad.8
  31.6 2.8 collective-permute-start.3
  53.5 3.1 collective-permute-done.5
  56.7 2.7 collective-permute-start.6
  66.8 8.2 %collective-permute-done.6 = bf16[2,2,2,48,512]{4,3,0,1,2:T(8,128)(2,1)S(1)} collective-permute-done((bf16[2,2,2,48,512]{4,3,0,1,2:T(8,128)(2,1)S(1)}, bf16[2,2,2,48,512]{4,3,0,1,2:T(8,128)(2,1)S(1)}, u32[]{:S(2)}, u32[]{:S(2)}) %collective-permute-start.6) | collective-permute-done | bytes 393248 | tf_op jit(solution)/shard_map/ppermute | solution.py:176
  76.0 7.2 %collective-permute-done.25 = bf16[2,2,192,384]{3,2,1,0:T(8,128)(2,1)S(1)} collective-permute-done((bf16[2,2,192,384]{3,2,1,0:T(8,128)(2,1)S(1)}, bf16[2,2,192,384]{3,2,1,0:T(8,128)(2,1)S(1)}, u32[]{:S(2)}, u32[]{:S(2)}) %collective-permute-start.25) | collective-permute-done | bytes 589856 | tf_op jit(solution)/shard_map/ppermute | solution.py:176
  83.5 2.3 collective-permute-start.26
  89.7 4.1 %fusion.6 = bf16[1040,2304]{1,0:T(8,128)(2,1)S(1)} fusion(bf16[1040,768]{1,0:T(8,128)(2,1)S(1)} %bitcast.398, bf16[768,2304]{1,0:T(8,128)(2,1)S(1)} %bitcast.388, f32[2304]{0:T(1024)S(1)} %pad_maximum_fusion.37), kind=kOutput, calls=%fused_computation.13 | convolution fusion | flops 3685294080 | bytes 9937920 | tf_op jit(solution)/shard_map/dot_general | solution.py:43
  93.9 7.6 %attention.1 = (bf16[5,208,768]{2,1,0:T(8,128)(2,1)S(1)}, bf16[5,12,208,208]{3,2,1,0:T(8,128)(2,1)S(1)}) custom-call(bf16[5,208,2304]{2,1,0:T(8,128)(2,1)S(1)} %bitcast.373), custom_call_target="tpu_custom_call" | custom-call | flops 2658140160 | bytes 30000000 | tf_op jit(solution)/shard_map/attention/pallas_call | solution.py:113
  101.5 2.6 copy-done.7
  115.4 12.3 %multiply_convert_fusion = (bf16[1040,3072]{1,0:T(8,128)(2,1)}, f32[1040,3072]{1,0:T(8,128)}) fusion(f32[3072]{0:T(1024)S(1)} %copy-done.31, bf16[1040,768]{1,0:T(8,128)(2,1)} %add_convert_fusion.5, bf16[768,3072]{1,0:T(8,128)(2,1)S(1)} %bitcast.386), kind=kOutput, calls=%fused_computation.10 | convolution fusion | flops 4926504960 | bytes 25497600 | tf_op jit(solution)/shard_map/dot_general | solution.py:43
  127.7 13.7 %convert_reduce_fusion = (f32[3072]{0:T(1024)S(1)}, bf16[1040,3072]{1,0:T(8,128)(2,1)}) fusion(f32[1040,3072]{1,0:T(8,128)} %get-tuple-element.151, bf16[1040,768]{1,0:T(8,128)(2,1)S(1)} %bitcast.397, bf16[3072,768]{1,0:T(8,128)(2,1)S(1)} %bitcast.382), kind=kOutput, calls=%fused_computation.9 | convolution fusion | flops 4952060928 | bytes 25497600 | tf_op jit(solution)/shard_map/dot_general | solution.py:35
  141.5 9.0 %multiply_reduce_fusion = (f32[768]{0:T(1024)S(1)}, f32[1040]{0:T(1024)S(1)}, f32[1040]{0:T(1024)S(1)}, f32[768]{0:T(1024)S(1)}, f32[1040,768]{1,0:T(8,128)S(1)}) fusion(f32[1040,768]{1,0:T(8,128)S(1)} %get-tuple-element.149, f32[1040]{0:T(1024)S(1)} %add_rsqrt_fusion, f32[1040]{0:T(1024)S(1)} %broadcast_multiply_fusion.5, f32[768]{0:T(1024)S(1)} %mul.208, ...), kind=kOutput, calls=%fused_computation.34 | convolution fusion | flops 4914520064 | bytes 17523968 | tf_op jit(solution)/shard_map/dot_general | solution.py:35
  150.6 3.2 convert_reduce_fusion.2
  153.8 2.6 convolution_convert_fusion.3
  157.6 5.5 %convolution_convert_fusion = bf16[3072,384]{1,0:T(8,128)(2,1)} fusion(bf16[1040,3072]{1,0:T(8,128)(2,1)S(1)} %bitcast.429, bf16[1040,768]{1,0:T(8,128)(2,1)S(1)} %get-tuple-element.44, s32[]{:T(128)S(6)} %select_n.748), kind=kOutput, calls=%fused_computation.18 | convolution fusion | flops 2454847488 | bytes 9547780 | tf_op jit(solution)/shard_map/dot_general | solution.py:39
  165.2 2.4 copy-done.5
  169.0 2.8 copy-done.8
  171.8 12.9 %attention_back.1 = (bf16[5,208,2304]{2,1,0:T(8,128)(2,1)S(1)}, f32[1,2304]{1,0:T(1,128)S(1)}) custom-call(bf16[5,208,2304]{2,1,0:T(8,128)(2,1)S(1)} %bitcast.374, bf16[5,12,208,208]{3,2,1,0:T(8,128)(2,1)S(1)} %copy-done.8, bf16[5,208,768]{2,1,0:T(8,128)(2,1)S(1)} %bitcast.378), custom_call_target="tpu_custom_call" | custom-call | flops 5316280320 | bytes 60000000 | tf_op jit(solution)/shard_map/attention_back/pallas_call | solution.py:136
  187.1 11.4 %multiply_reduce_fusion.1 = (f32[768]{0:T(1024)S(1)}, f32[1040]{0:T(1024)S(1)}, f32[1040]{0:T(1024)S(1)}, f32[768]{0:T(1024)S(1)}, f32[1040,768]{1,0:T(8,128)}) fusion(f32[1040]{0:T(1024)S(1)} %div.33, f32[1040]{0:T(1024)S(1)} %copy-done.29, f32[5,208,768]{2,1,0:T(8,128)} %pad_convert_fusion, f32[1040,768]{1,0:T(8,128)} %bitcast.379, f32[768]{0:T(1024)S(1)} %mul.200, ...), kind=kOutput, calls=%fused_computation.36 | convolution fusion | flops 3689284096 | bytes 17941760 | tf_op jit(solution)/shard_map/dot_general | solution.py:35
  201.7 4.6 %add_convert_fusion.3 = (bf16[1040,768]{1,0:T(8,128)(2,1)S(1)}, bf16[1040,768]{1,0:T(8,128)(2,1)S(1)}) fusion(f32[768]{0:T(1024)S(1)} %add.431, f32[1040]{0:T(1024)S(1)} %div.33, f32[768]{0:T(1024)S(1)} %mul.200, f32[1040]{0:T(1024)S(1)} %copy-done.29, f32[5,208,768]{2,1,0:T(8,128)} %pad_convert_fusion, f32[1040,768]{1,0:T(8,128)} %get-tuple-element.43, ...), kind=kLoop, calls=%fused_computation.37 | loop fusion | flops 9584640 | bytes 12802304 | tf_op jit(solution)/shard_map/convert_element_type | solution.py:352
  206.4 2.4 add_convert_fusion.7
  210.5 2.7 convolution_convert_fusion.2
  213.2 4.3 %collective-permute-done.50 = bf16[2,2,2,48,384]{4,3,2,1,0:T(8,128)(2,1)S(1)} collective-permute-done((bf16[2,2,2,48,384]{4,3,2,1,0:T(8,128)(2,1)S(1)}, bf16[2,2,2,48,384]{4,3,2,1,0:T(8,128)(2,1)S(1)}, u32[]{:S(2)}, u32[]{:S(2)}) %collective-permute-start.50) | collective-permute-done | bytes 294944 | tf_op jit(solution)/shard_map/ppermute | solution.py:186
  217.5 2.5 collective-permute-start.45
  223.6 3.7 collective-permute-done.51
  228.6 2.4 collective-permute-done.46
  234.4 7.7 %fusion.10 = bf16[1040,768]{1,0:T(8,128)(2,1)S(1)} fusion(f32[1040,768]{1,0:T(8,128)S(1)} %copy-done.10, bf16[1040,3072]{1,0:T(8,128)(2,1)} %get-tuple-element.150, bf16[3072,768]{1,0:T(8,128)(2,1)S(1)} %bitcast.385, f32[1040]{0:T(1024)S(1)} %mul.217, f32[768]{0:T(1024)S(1)} %copy-done.32), kind=kOutput, calls=%fused_computation.26 | convolution fusion | flops 4910530560 | bytes 15907904 | tf_op jit(solution)/shard_map/dot_general | solution.py:43
  245.9 4.6 %convolution_convert_fusion.1 = bf16[768,1536]{1,0:T(8,128)(2,1)} fusion(bf16[1040,768]{1,0:T(8,128)(2,1)S(1)} %copy-done.18, bf16[1040,3072]{1,0:T(8,128)(2,1)S(1)} %bitcast.425, s32[]{:T(128)S(6)} %select_n.758), kind=kOutput, calls=%fused_computation.27 | convolution fusion | flops 2454847488 | bytes 7151620 | tf_op jit(solution)/shard_map/dot_general | solution.py:39
  258.3 2.8 add_convert_fusion.2
  268.6 5.6 %collective-permute-done.29 = bf16[2,2,2,48,512]{4,3,2,1,0:T(8,128)(2,1)S(1)} collective-permute-done((bf16[2,2,2,48,512]{4,3,2,1,0:T(8,128)(2,1)S(1)}, bf16[2,2,2,48,512]{4,3,2,1,0:T(8,128)(2,1)S(1)}, u32[]{:S(2)}, u32[]{:S(2)}) %collective-permute-start.29) | collective-permute-done | bytes 393248 | tf_op jit(solution)/shard_map/ppermute | solution.py:186
  275.8 4.6 %collective-permute-done.36 = bf16[2,2,2,48,640]{4,3,2,1,0:T(8,128)(2,1)S(1)} collective-permute-done((bf16[2,2,2,48,640]{4,3,2,1,0:T(8,128)(2,1)S(1)}, bf16[2,2,2,48,640]{4,3,2,1,0:T(8,128)(2,1)S(1)}, u32[]{:S(2)}, u32[]{:S(2)}) %collective-permute-start.36) | collective-permute-done | bytes 491552 | tf_op jit(solution)/shard_map/ppermute | solution.py:186
  282.0 7.9 %add_convert_fusion = bf16[3072,384]{1,0:T(8,128)(2,1)S(1)} fusion(bf16[3072,384]{1,0:T(8,128)(2,1)} %collective-permute-done.71, bf16[1040,3072]{1,0:T(8,128)(2,1)} %get-tuple-element.150, bf16[1040,768]{1,0:T(8,128)(2,1)S(1)} %copy-done.22, s32[]{:T(128)S(6)} %select_n.676), kind=kOutput, calls=%fused_computation.16 | convolution fusion | flops 2457206784 | bytes 11907076 | tf_op jit(solution)/shard_map/dot_general | solution.py:39
  291.4 5.1 %add_convert_fusion.1 = bf16[768,1536]{1,0:T(8,128)(2,1)S(1)} fusion(bf16[768,1536]{1,0:T(8,128)(2,1)} %collective-permute-done.63, bf16[1040,768]{1,0:T(8,128)(2,1)S(1)} %copy-done.19, bf16[1040,3072]{1,0:T(8,128)(2,1)S(1)} %bitcast.427, s32[]{:T(128)S(6)} %select_n.692), kind=kOutput, calls=%fused_computation.17 | convolution fusion | flops 2457206784 | bytes 9510916 | tf_op jit(solution)/shard_map/dot_general | solution.py:39
  303.7 16.1 %collective-permute-done.38 = bf16[2,48,640]{2,1,0:T(8,128)(2,1)S(1)} collective-permute-done((bf16[2,48,640]{2,1,0:T(8,128)(2,1)S(1)}, bf16[2,48,640]{2,1,0:T(8,128)(2,1)S(1)}, u32[]{:S(2)}, u32[]{:S(2)}) %collective-permute-start.38) | collective-permute-done | bytes 122912 | tf_op jit(solution)/shard_map/ppermute | solution.py:186
  320.2 5.4 %collective-permute-done.39 = bf16[48,640]{1,0:T(8,128)(2,1)S(1)} collective-permute-done((bf16[48,640]{1,0:T(8,128)(2,1)S(1)}, bf16[48,640]{1,0:T(8,128)(2,1)S(1)}, u32[]{:S(2)}, u32[]{:S(2)}) %collective-permute-start.39) | collective-permute-done | bytes 61472 | tf_op jit(solution)/shard_map/ppermute | solution.py:186
  331.6 3.3 collective-permute-done.41
  340.5 24.8 %collective-permute-done.73 = bf16[2,2,192,384]{3,2,1,0:T(8,128)(2,1)S(1)} collective-permute-done((bf16[2,2,192,384]{3,2,1,0:T(8,128)(2,1)S(1)}, bf16[2,2,192,384]{3,2,1,0:T(8,128)(2,1)S(1)}, u32[]{:S(2)}, u32[]{:S(2)}) %collective-permute-start.73) | collective-permute-done | bytes 589856 | tf_op jit(solution)/shard_map/ppermute | solution.py:186
  366.7 7.8 %collective-permute-done.74 = bf16[2,192,384]{2,1,0:T(8,128)(2,1)S(1)} collective-permute-done((bf16[2,192,384]{2,1,0:T(8,128)(2,1)S(1)}, bf16[2,192,384]{2,1,0:T(8,128)(2,1)S(1)}, u32[]{:S(2)}, u32[]{:S(2)}) %collective-permute-start.74) | collective-permute-done | bytes 294944 | tf_op jit(solution)/shard_map/ppermute | solution.py:186
  376.4 3.5 collective-permute-done.75
  381.5 2.8 collective-permute-done.67
  387.2 2.9 collective-permute-done.68
  391.3 4.5 %collective-permute-done.77 = bf16[2,192,384]{2,1,0:T(8,128)(2,1)S(1)} collective-permute-done((bf16[2,192,384]{2,1,0:T(8,128)(2,1)S(1)}, bf16[2,192,384]{2,1,0:T(8,128)(2,1)S(1)}, u32[]{:S(2)}, u32[]{:S(2)}) %collective-permute-start.77) | collective-permute-done | bytes 294944 | tf_op jit(solution)/shard_map/ppermute | solution.py:176
  396.1 4.7 %collective-permute-done.69 = bf16[2,48,1536]{2,1,0:T(8,128)(2,1)S(1)} collective-permute-done((bf16[2,48,1536]{2,1,0:T(8,128)(2,1)S(1)}, bf16[2,48,1536]{2,1,0:T(8,128)(2,1)S(1)}, u32[]{:S(2)}, u32[]{:S(2)}) %collective-permute-start.69) | collective-permute-done | bytes 294944 | tf_op jit(solution)/shard_map/ppermute | solution.py:176
  (435 shorter events, 134.8 us)
Async XLA Ops:
  6.9 24.5 %collective-permute-start = (bf16[12,192]{1,0:T(8,128)(2,1)S(1)}, bf16[12,192]{1,0:T(8,128)(2,1)}, u32[]{:S(2)}, u32[]{:S(2)}) collective-permute-start(bf16[12,192]{1,0:T(8,128)(2,1)S(1)} %concatenate.35), channel_id=1, source_target_pairs={{0,1},{1,2},{2,3},{3,0},{4,5},{5,6},{6,7},{7,4},{8,9},{9,10},{10,1... | collective-permute-start | bytes 13832 | tf_op jit(solution)/shard_map/ppermute | solution.py:239
  10.0 21.7 %collective-permute-start.1 = (bf16[12,192]{1,0:T(8,128)(2,1)S(1)}, bf16[12,192]{1,0:T(8,128)(2,1)}, u32[]{:S(2)}, u32[]{:S(2)}) collective-permute-start(bf16[12,192]{1,0:T(8,128)(2,1)S(1)} %concatenate.35), channel_id=1, source_target_pairs={{0,2},{1,3},{2,0},{3,1},{4,6},{5,7},{6,4},{7,5},{8,10},{9,11},{10,... | collective-permute-start | bytes 13832 | tf_op jit(solution)/shard_map/ppermute | solution.py:239
  12.6 21.8 %collective-permute-start.2 = (bf16[12,192]{1,0:T(8,128)(2,1)S(1)}, bf16[12,192]{1,0:T(8,128)(2,1)}, u32[]{:S(2)}, u32[]{:S(2)}) collective-permute-start(bf16[12,192]{1,0:T(8,128)(2,1)S(1)} %concatenate.35), channel_id=1, source_target_pairs={{0,3},{1,0},{2,1},{3,2},{4,7},{5,4},{6,5},{7,6},{8,11},{9,8},{10,9... | collective-permute-start | bytes 13832 | tf_op jit(solution)/shard_map/ppermute | solution.py:239
  14.7 32.0 %collective-permute-start.23 = (bf16[192,384]{1,0:T(8,128)(2,1)}, bf16[192,384]{1,0:T(8,128)(2,1)}, u32[]{:S(2)}, u32[]{:S(2)}) collective-permute-start(bf16[192,384]{1,0:T(8,128)(2,1)} %dynamic-slice_bitcast_fusion.14), channel_id=1, source_target_pairs={{0,2},{2,0},{1,3},{3,1},{4,6},{6,4},{5,7},{7,5},{8,10},{10,8},{9,1... | collective-permute-start | bytes 442376 | tf_op jit(solution)/shard_map/ppermute | solution.py:176
  16.0 32.6 %collective-permute-start.18 = (bf16[48,1536]{1,0:T(8,128)(2,1)S(1)}, bf16[48,1536]{1,0:T(8,128)(2,1)}, u32[]{:S(2)}, u32[]{:S(2)}) collective-permute-start(bf16[48,1536]{1,0:T(8,128)(2,1)S(1)} %dynamic-slice_bitcast_fusion.15), channel_id=1, source_target_pairs={{0,2},{2,0},{1,3},{3,1},{4,6},{6,4},{5,7},{7,5},{8,10},{10,8},{9,1... | collective-permute-start | bytes 442376 | tf_op jit(solution)/shard_map/ppermute | solution.py:176
  31.6 9.1 %collective-permute-start.3 = (bf16[48,512]{1,0:T(8,128)(2,1)S(1)}, bf16[48,512]{1,0:T(8,128)(2,1)}, u32[]{:S(2)}, u32[]{:S(2)}) collective-permute-start(bf16[48,512]{1,0:T(8,128)(2,1)S(1)} %copy-done.28), channel_id=1, source_target_pairs={{0,2},{2,0},{1,3},{3,1},{4,6},{6,4},{5,7},{7,5},{8,10},{10,8},{9,1... | collective-permute-start | bytes 147464 | tf_op jit(solution)/shard_map/ppermute | solution.py:176
  41.5 9.3 %collective-permute-start.4 = (bf16[2,48,512]{2,1,0:T(8,128)(2,1)S(1)}, bf16[2,48,512]{2,1,0:T(8,128)(2,1)S(1)}, u32[]{:S(2)}, u32[]{:S(2)}) collective-permute-start(bf16[2,48,512]{2,1,0:T(8,128)(2,1)S(1)} %pad_maximum_fusion.32), channel_id=1, source_target_pairs={{0,1},{1,0},{2,3},{3,2},{4,5},{5,4},{6,7},{7,6},{8,9},{9,8},{10,11... | collective-permute-start | bytes 294920 | tf_op jit(solution)/shard_map/ppermute | solution.py:176
  47.7 14.5 %collective-permute-start.24 = (bf16[2,192,384]{2,1,0:T(8,128)(2,1)S(1)}, bf16[2,192,384]{2,1,0:T(8,128)(2,1)S(1)}, u32[]{:S(2)}, u32[]{:S(2)}) collective-permute-start(bf16[2,192,384]{2,1,0:T(8,128)(2,1)S(1)} %pad_maximum_fusion.21), channel_id=1, source_target_pairs={{0,1},{1,0},{2,3},{3,2},{4,5},{5,4},{6,7},{7,6},{8,9},{9,8},{10,11... | collective-permute-start | bytes 884744 | tf_op jit(solution)/shard_map/ppermute | solution.py:176
  49.6 14.4 %collective-permute-start.19 = (bf16[2,48,1536]{2,1,0:T(8,128)(2,1)S(1)}, bf16[2,48,1536]{2,1,0:T(8,128)(2,1)S(1)}, u32[]{:S(2)}, u32[]{:S(2)}) collective-permute-start(bf16[2,48,1536]{2,1,0:T(8,128)(2,1)S(1)} %pad_maximum_fusion.20), channel_id=1, source_target_pairs={{0,1},{1,0},{2,3},{3,2},{4,5},{5,4},{6,7},{7,6},{8,9},{9,8},{10,11... | collective-permute-start | bytes 884744 | tf_op jit(solution)/shard_map/ppermute | solution.py:176
  51.3 9.0 %collective-permute-start.10 = (bf16[2,2,48,640]{3,2,1,0:T(8,128)(2,1)S(1)}, bf16[2,2,48,640]{3,2,1,0:T(8,128)(2,1)S(1)}, u32[]{:S(2)}, u32[]{:S(2)}) collective-permute-start(bf16[2,2,48,640]{3,2,1,0:T(8,128)(2,1)S(1)} %pad_maximum_fusion.24), channel_id=1, source_target_pairs={{0,16},{16,0},{1,17},{17,1},{2,18},{18,2},{3,19},{19,3},{4,20},{20... | collective-permute-start | bytes 737288 | tf_op jit(solution)/shard_map/ppermute | solution.py:176
  53.2 13.3 %collective-permute-start.16 = (bf16[2,2,2,48,384]{4,3,2,1,0:T(8,128)(2,1)S(1)}, bf16[2,2,2,48,384]{4,3,2,1,0:T(8,128)(2,1)S(1)}, u32[]{:S(2)}, u32[]{:S(2)}) collective-permute-start(bf16[2,2,2,48,384]{4,3,2,1,0:T(8,128)(2,1)S(1)} %pad_maximum_fusion.19), channel_id=1, source_target_pairs={{0,16},{16,0},{1,17},{17,1},{2,18},{18,2},{3,19},{19,3},{4,20},{20... | collective-permute-start | bytes 884744 | tf_op jit(solution)/shard_map/ppermute | solution.py:176
  56.7 18.3 %collective-permute-start.6 = (bf16[2,2,2,48,512]{4,3,0,1,2:T(8,128)(2,1)S(1)}, bf16[2,2,2,48,512]{4,3,0,1,2:T(8,128)(2,1)S(1)}, u32[]{:S(2)}, u32[]{:S(2)}) collective-permute-start(bf16[2,2,2,48,512]{4,3,0,1,2:T(8,128)(2,1)S(1)} %pad_maximum_fusion.18), channel_id=1, source_target_pairs={{0,16},{16,0},{1,17},{17,1},{2,18},{18,2},{3,19},{19,3},{4,20},{20... | collective-permute-start | bytes 1179656 | tf_op jit(solution)/shard_map/ppermute | solution.py:176
  60.4 14.8 %collective-permute-start.11 = (bf16[2,2,2,48,640]{4,3,2,1,0:T(8,128)(2,1)S(1)}, bf16[2,2,2,48,640]{4,3,2,1,0:T(8,128)(2,1)S(1)}, u32[]{:S(2)}, u32[]{:S(2)}) collective-permute-start(bf16[2,2,2,48,640]{4,3,2,1,0:T(8,128)(2,1)S(1)} %pad_maximum_fusion.17), channel_id=1, source_target_pairs={{0,8},{8,0},{1,9},{9,1},{2,10},{10,2},{3,11},{11,3},{4,12},{12,4},... | collective-permute-start | bytes 1474568 | tf_op jit(solution)/shard_map/ppermute | solution.py:176
  62.4 20.8 %collective-permute-start.25 = (bf16[2,2,192,384]{3,2,1,0:T(8,128)(2,1)S(1)}, bf16[2,2,192,384]{3,2,1,0:T(8,128)(2,1)S(1)}, u32[]{:S(2)}, u32[]{:S(2)}) collective-permute-start(bf16[2,2,192,384]{3,2,1,0:T(8,128)(2,1)S(1)} %pad_maximum_fusion.14), channel_id=1, source_target_pairs={{0,16},{16,0},{1,17},{17,1},{2,18},{18,2},{3,19},{19,3},{4,20},{20... | collective-permute-start | bytes 1769480 | tf_op jit(solution)/shard_map/ppermute | solution.py:176
  64.1 21.8 %collective-permute-start.20 = (bf16[2,2,48,1536]{3,2,1,0:T(8,128)(2,1)S(1)}, bf16[2,2,48,1536]{3,2,1,0:T(8,128)(2,1)S(1)}, u32[]{:S(2)}, u32[]{:S(2)}) collective-permute-start(bf16[2,2,48,1536]{3,2,1,0:T(8,128)(2,1)S(1)} %pad_maximum_fusion.13), channel_id=1, source_target_pairs={{0,8},{8,0},{1,9},{9,1},{2,10},{10,2},{3,11},{11,3},{4,12},{12,4},... | collective-permute-start | bytes 1769480 | tf_op jit(solution)/shard_map/ppermute | solution.py:176
  66.7 20.9 %collective-permute-start.17 = (bf16[2,2,2,2,48,384]{5,4,3,2,1,0:T(8,128)(2,1)S(1)}, bf16[2,2,2,2,48,384]{5,4,3,2,1,0:T(8,128)(2,1)S(1)}, u32[]{:S(2)}, u32[]{:S(2)}) collective-permute-start(bf16[2,2,2,2,48,384]{5,4,3,2,1,0:T(8,128)(2,1)S(1)} %pad_maximum_fusion.12), channel_id=1, source_target_pairs={{0,4},{4,0},{1,5},{5,1},{2,6},{6,2},{3,7},{7,3},{8,12},{12,8},{9,1... | collective-permute-start | bytes 1769480 | tf_op jit(solution)/shard_map/ppermute | solution.py:202
  75.1 12.8 %collective-permute-start.7 = (bf16[2,2,2,2,48,512]{5,4,0,1,2,3:T(8,128)(2,1)S(1)}, bf16[2,2,2,2,48,512]{5,4,0,1,2,3:T(8,128)(2,1)S(1)}, u32[]{:S(2)}, u32[]{:S(2)}) collective-permute-start(bf16[2,2,2,2,48,512]{5,4,0,1,2,3:T(8,128)(2,1)S(1)} %pad_maximum_fusion.11), channel_id=1, source_target_pairs={{0,4},{4,0},{1,5},{5,1},{2,6},{6,2},{3,7},{7,3},{8,12},{12,8},{9,1... | collective-permute-start | bytes 2359304 | tf_op jit(solution)/shard_map/ppermute | solution.py:202
  75.4 12.6 %collective-permute-start.12 = (bf16[2,2,2,2,48,640]{5,4,3,2,1,0:T(8,128)(2,1)S(1)}, bf16[2,2,2,2,48,640]{5,4,3,2,1,0:T(8,128)(2,1)S(1)}, u32[]{:S(2)}, u32[]{:S(2)}) collective-permute-start(bf16[2,2,2,2,48,640]{5,4,3,2,1,0:T(8,128)(2,1)S(1)} %pad_maximum_fusion.10), channel_id=1, source_target_pairs={{0,4},{4,0},{1,5},{5,1},{2,6},{6,2},{3,7},{7,3},{8,12},{12,8},{9,1... | collective-permute-start | bytes 2949128 | tf_op jit(solution)/shard_map/ppermute | solution.py:202
  83.5 21.7 %collective-permute-start.26 = (bf16[2,2,2,192,384]{4,3,2,1,0:T(8,128)(2,1)S(1)}, bf16[2,2,2,192,384]{4,3,2,1,0:T(8,128)(2,1)S(1)}, u32[]{:S(2)}, u32[]{:S(2)}) collective-permute-start(bf16[2,2,2,192,384]{4,3,2,1,0:T(8,128)(2,1)S(1)} %pad_maximum_fusion.7), channel_id=1, source_target_pairs={{0,8},{8,0},{1,9},{9,1},{2,10},{10,2},{3,11},{11,3},{4,12},{12,4},... | collective-permute-start | bytes 3538952 | tf_op jit(solution)/shard_map/ppermute | solution.py:176
  86.0 21.3 %collective-permute-start.21 = (bf16[2,2,2,48,1536]{4,3,2,1,0:T(8,128)(2,1)S(1)}, bf16[2,2,2,48,1536]{4,3,2,1,0:T(8,128)(2,1)S(1)}, u32[]{:S(2)}, u32[]{:S(2)}) collective-permute-start(bf16[2,2,2,48,1536]{4,3,2,1,0:T(8,128)(2,1)S(1)} %pad_maximum_fusion.6), channel_id=1, source_target_pairs={{0,16},{16,0},{1,17},{17,1},{2,18},{18,2},{3,19},{19,3},{4,20},{20... | collective-permute-start | bytes 3538952 | tf_op jit(solution)/shard_map/ppermute | solution.py:176
  163.1 118.9 %collective-permute-start.71 = (bf16[3072,384]{1,0:T(8,128)(2,1)}, bf16[3072,384]{1,0:T(8,128)(2,1)}, u32[]{:S(2)}, u32[]{:S(2)}) collective-permute-start(bf16[3072,384]{1,0:T(8,128)(2,1)} %convolution_convert_fusion), channel_id=1, source_target_pairs={{0,4},{4,0},{1,5},{5,1},{2,6},{6,2},{3,7},{7,3},{8,12},{12,8},{9,1... | collective-permute-start | bytes 7077896 | tf_op jit(solution)/shard_map/ppermute | solution.py:214
  163.4 63.9 %collective-permute-start.57 = (f32[8,192]{1,0:T(8,128)S(1)}, f32[8,192]{1,0:T(8,128)S(1)}, u32[]{:S(2)}, u32[]{:S(2)}) collective-permute-start(f32[8,192]{1,0:T(8,128)S(1)} %get-tuple-element.129), channel_id=1, source_target_pairs={{0,1},{1,2},{2,3},{3,0},{4,5},{5,6},{6,7},{7,4},{8,9},{9,10},{10,1... | collective-permute-start | bytes 18440 | tf_op jit(solution)/shard_map/ppermute | solution.py:239
  165.0 41.4 %collective-permute-start.49 = (bf16[768,384]{1,0:T(8,128)(2,1)S(1)}, bf16[768,384]{1,0:T(8,128)(2,1)}, u32[]{:S(2)}, u32[]{:S(2)}) collective-permute-start(bf16[768,384]{1,0:T(8,128)(2,1)S(1)} %convolution_convert_fusion.4), channel_id=1, source_target_pairs={{0,4},{4,0},{1,5},{5,1},{2,6},{6,2},{3,7},{7,3},{8,12},{12,8},{9,1... | collective-permute-start | bytes 1769480 | tf_op jit(solution)/shard_map/ppermute | solution.py:214
  198.7 21.4 %collective-permute-start.43 = (f32[4,192]{1,0:T(4,128)S(1)}, f32[4,192]{1,0:T(4,128)S(1)}, u32[]{:S(2)}, u32[]{:S(2)}) collective-permute-start(f32[4,192]{1,0:T(4,128)S(1)} %bitcast.415), channel_id=1, source_target_pairs={{0,1},{1,2},{2,3},{3,0},{4,5},{5,6},{6,7},{7,4},{8,9},{9,10},{10,1... | collective-permute-start | bytes 9224 | tf_op jit(solution)/shard_map/ppermute | solution.py:239
  200.6 20.1 %collective-permute-start.44 = (f32[4,192]{1,0:T(4,128)S(1)}, f32[4,192]{1,0:T(4,128)S(1)}, u32[]{:S(2)}, u32[]{:S(2)}) collective-permute-start(f32[4,192]{1,0:T(4,128)S(1)} %bitcast.414), channel_id=1, source_target_pairs={{0,2},{1,3},{2,0},{3,1},{4,6},{5,7},{6,4},{7,5},{8,10},{9,11},{10,... | collective-permute-start | bytes 9224 | tf_op jit(solution)/shard_map/ppermute | solution.py:239
  208.8 8.7 %collective-permute-start.50 = (bf16[2,2,2,48,384]{4,3,2,1,0:T(8,128)(2,1)S(1)}, bf16[2,2,2,48,384]{4,3,2,1,0:T(8,128)(2,1)S(1)}, u32[]{:S(2)}, u32[]{:S(2)}) collective-permute-start(bf16[2,2,2,48,384]{4,3,2,1,0:T(8,128)(2,1)S(1)} %dynamic-slice_bitcast_fusion.8), channel_id=1, source_target_pairs={{0,16},{16,0},{1,17},{17,1},{2,18},{18,2},{3,19},{19,3},{4,20},{20... | collective-permute-start | bytes 884744 | tf_op jit(solution)/shard_map/ppermute | solution.py:186
  227.3 31.1 %collective-permute-start.28 = (bf16[768,1152]{1,0:T(8,128)(2,1)S(1)}, bf16[768,1152]{1,0:T(8,128)(2,1)S(1)}, u32[]{:S(2)}, u32[]{:S(2)}) collective-permute-start(bf16[768,1152]{1,0:T(8,128)(2,1)S(1)} %convolution_convert_fusion.2), channel_id=1, source_target_pairs={{0,4},{4,0},{1,5},{5,1},{2,6},{6,2},{3,7},{7,3},{8,12},{12,8},{9,1... | collective-permute-start | bytes 5308424 | tf_op jit(solution)/shard_map/ppermute | solution.py:214
  228.5 15.3 %collective-permute-start.60 = (f32[8,192]{1,0:T(8,128)S(1)}, f32[8,192]{1,0:T(8,128)S(1)}, u32[]{:S(2)}, u32[]{:S(2)}) collective-permute-start(f32[8,192]{1,0:T(8,128)S(1)} %fusion.65), channel_id=1, source_target_pairs={{0,4},{4,0},{1,5},{5,1},{2,6},{6,2},{3,7},{7,3},{8,12},{12,8},{9,1... | collective-permute-start | bytes 18440 | tf_op jit(solution)/shard_map/ppermute | solution.py:267
  231.0 11.2 %collective-permute-start.47 = (f32[4,192]{1,0:T(4,128)S(1)}, f32[4,192]{1,0:T(4,128)S(1)}, u32[]{:S(2)}, u32[]{:S(2)}) collective-permute-start(f32[4,192]{1,0:T(4,128)S(1)} %add.484), channel_id=1, source_target_pairs={{0,8},{8,0},{1,9},{9,1},{2,10},{10,2},{3,11},{11,3},{4,12},{12,4},... | collective-permute-start | bytes 9224 | tf_op jit(solution)/shard_map/ppermute | solution.py:267
  232.5 12.7 %collective-permute-start.53 = (bf16[48,384]{1,0:T(8,128)(2,1)S(1)}, bf16[48,384]{1,0:T(8,128)(2,1)S(1)}, u32[]{:S(2)}, u32[]{:S(2)}) collective-permute-start(bf16[48,384]{1,0:T(8,128)(2,1)S(1)} %dynamic-slice_bitcast_fusion.22), channel_id=1, source_target_pairs={{0,2},{2,0},{1,3},{3,1},{4,6},{6,4},{5,7},{7,5},{8,10},{10,8},{9,1... | collective-permute-start | bytes 110600 | tf_op jit(solution)/shard_map/ppermute | solution.py:186
  242.2 10.8 %collective-permute-start.48 = (f32[4,192]{1,0:T(4,128)S(1)}, f32[4,192]{1,0:T(4,128)S(1)}, u32[]{:S(2)}, u32[]{:S(2)}) collective-permute-start(f32[4,192]{1,0:T(4,128)S(1)} %add.485), channel_id=1, source_target_pairs={{0,16},{16,0},{1,17},{17,1},{2,18},{18,2},{3,19},{19,3},{4,20},{20... | collective-permute-start | bytes 9224 | tf_op jit(solution)/shard_map/ppermute | solution.py:267
  243.8 9.2 %collective-permute-start.61 = (f32[8,192]{1,0:T(8,128)S(1)}, f32[8,192]{1,0:T(8,128)S(1)}, u32[]{:S(2)}, u32[]{:S(2)}) collective-permute-start(f32[8,192]{1,0:T(8,128)S(1)} %add.496), channel_id=1, source_target_pairs={{0,8},{8,0},{1,9},{9,1},{2,10},{10,2},{3,11},{11,3},{4,12},{12,4},... | collective-permute-start | bytes 18440 | tf_op jit(solution)/shard_map/ppermute | solution.py:267
  253.0 38.4 %collective-permute-start.63 = (bf16[768,1536]{1,0:T(8,128)(2,1)}, bf16[768,1536]{1,0:T(8,128)(2,1)}, u32[]{:S(2)}, u32[]{:S(2)}) collective-permute-start(bf16[768,1536]{1,0:T(8,128)(2,1)} %convolution_convert_fusion.1), channel_id=1, source_target_pairs={{0,4},{4,0},{1,5},{5,1},{2,6},{6,2},{3,7},{7,3},{8,12},{12,8},{9,1... | collective-permute-start | bytes 7077896 | tf_op jit(solution)/shard_map/ppermute | solution.py:214
  258.2 10.3 %collective-permute-start.56 = (bf16[2,2,48,384]{3,2,0,1:T(8,128)(2,1)S(1)}, bf16[2,2,48,384]{3,2,0,1:T(8,128)(2,1)S(1)}, u32[]{:S(2)}, u32[]{:S(2)}) collective-permute-start(bf16[2,2,48,384]{3,2,0,1:T(8,128)(2,1)S(1)} %pad_maximum_fusion.29), channel_id=1, source_target_pairs={{0,4},{4,0},{1,5},{5,1},{2,6},{6,2},{3,7},{7,3},{8,12},{12,8},{9,1... | collective-permute-start | bytes 442376 | tf_op jit(solution)/shard_map/ppermute | solution.py:228
  262.5 11.7 %collective-permute-start.29 = (bf16[2,2,2,48,512]{4,3,2,1,0:T(8,128)(2,1)S(1)}, bf16[2,2,2,48,512]{4,3,2,1,0:T(8,128)(2,1)S(1)}, u32[]{:S(2)}, u32[]{:S(2)}) collective-permute-start(bf16[2,2,2,48,512]{4,3,2,1,0:T(8,128)(2,1)S(1)} %dynamic-slice_bitcast_fusion.5), channel_id=1, source_target_pairs={{0,1},{1,0},{2,3},{3,2},{4,5},{5,4},{6,7},{7,6},{8,9},{9,8},{10,11... | collective-permute-start | bytes 1179656 | tf_op jit(solution)/shard_map/ppermute | solution.py:186
  267.0 13.4 %collective-permute-start.36 = (bf16[2,2,2,48,640]{4,3,2,1,0:T(8,128)(2,1)S(1)}, bf16[2,2,2,48,640]{4,3,2,1,0:T(8,128)(2,1)S(1)}, u32[]{:S(2)}, u32[]{:S(2)}) collective-permute-start(bf16[2,2,2,48,640]{4,3,2,1,0:T(8,128)(2,1)S(1)} %dynamic-slice_bitcast_fusion.4), channel_id=1, source_target_pairs={{0,16},{16,0},{1,17},{17,1},{2,18},{18,2},{3,19},{19,3},{4,20},{20... | collective-permute-start | bytes 1474568 | tf_op jit(solution)/shard_map/ppermute | solution.py:186
  274.4 16.1 %collective-permute-start.30 = (bf16[2,2,48,512]{3,2,1,0:T(8,128)(2,1)S(1)}, bf16[2,2,48,512]{3,2,1,0:T(8,128)(2,1)S(1)}, u32[]{:S(2)}, u32[]{:S(2)}) collective-permute-start(bf16[2,2,48,512]{3,2,1,0:T(8,128)(2,1)S(1)} %dynamic-slice_bitcast_fusion.10), channel_id=1, source_target_pairs={{0,2},{2,0},{1,3},{3,1},{4,6},{6,4},{5,7},{7,5},{8,10},{10,8},{9,1... | collective-permute-start | bytes 589832 | tf_op jit(solution)/shard_map/ppermute | solution.py:186
  280.6 18.9 %collective-permute-start.37 = (bf16[2,2,48,640]{3,2,1,0:T(8,128)(2,1)S(1)}, bf16[2,2,48,640]{3,2,1,0:T(8,128)(2,1)S(1)}, u32[]{:S(2)}, u32[]{:S(2)}) collective-permute-start(bf16[2,2,48,640]{3,2,1,0:T(8,128)(2,1)S(1)} %dynamic-slice_bitcast_fusion.9), channel_id=1, source_target_pairs={{0,8},{8,0},{1,9},{9,1},{2,10},{10,2},{3,11},{11,3},{4,12},{12,4},... | collective-permute-start | bytes 737288 | tf_op jit(solution)/shard_map/ppermute | solution.py:186
  290.1 46.5 %collective-permute-start.72 = (bf16[2,2,2,192,384]{4,3,2,1,0:T(8,128)(2,1)S(1)}, bf16[2,2,2,192,384]{4,3,2,1,0:T(8,128)(2,1)S(1)}, u32[]{:S(2)}, u32[]{:S(2)}) collective-permute-start(bf16[2,2,2,192,384]{4,3,2,1,0:T(8,128)(2,1)S(1)} %dynamic-slice_bitcast_fusion), channel_id=1, source_target_pairs={{0,1},{1,0},{2,3},{3,2},{4,5},{5,4},{6,7},{7,6},{8,9},{9,8},{10,11... | collective-permute-start | bytes 3538952 | tf_op jit(solution)/shard_map/ppermute | solution.py:186
  296.6 40.4 %collective-permute-start.64 = (bf16[2,2,2,48,1536]{4,3,2,1,0:T(8,128)(2,1)S(1)}, bf16[2,2,2,48,1536]{4,3,2,1,0:T(8,128)(2,1)S(1)}, u32[]{:S(2)}, u32[]{:S(2)}) collective-permute-start(bf16[2,2,2,48,1536]{4,3,2,1,0:T(8,128)(2,1)S(1)} %dynamic-slice_bitcast_fusion.1), channel_id=1, source_target_pairs={{0,8},{8,0},{1,9},{9,1},{2,10},{10,2},{3,11},{11,3},{4,12},{12,4},... | collective-permute-start | bytes 3538952 | tf_op jit(solution)/shard_map/ppermute | solution.py:186
  299.6 20.1 %collective-permute-start.38 = (bf16[2,48,640]{2,1,0:T(8,128)(2,1)S(1)}, bf16[2,48,640]{2,1,0:T(8,128)(2,1)S(1)}, u32[]{:S(2)}, u32[]{:S(2)}) collective-permute-start(bf16[2,48,640]{2,1,0:T(8,128)(2,1)S(1)} %dynamic-slice_bitcast_fusion.16), channel_id=1, source_target_pairs={{0,1},{1,0},{2,3},{3,2},{4,5},{5,4},{6,7},{7,6},{8,9},{9,8},{10,11... | collective-permute-start | bytes 368648 | tf_op jit(solution)/shard_map/ppermute | solution.py:186
  302.2 18.0 %collective-permute-start.33 = (bf16[48,512]{1,0:T(8,128)(2,1)S(1)}, bf16[48,512]{1,0:T(8,128)(2,1)S(1)}, u32[]{:S(2)}, u32[]{:S(2)}) collective-permute-start(bf16[48,512]{1,0:T(8,128)(2,1)S(1)} %fusion.49), channel_id=1, source_target_pairs={{0,16},{16,0},{1,17},{17,1},{2,18},{18,2},{3,19},{19,3},{4,20},{20... | collective-permute-start | bytes 147464 | tf_op jit(solution)/shard_map/ppermute | solution.py:176
  337.0 28.4 %collective-permute-start.73 = (bf16[2,2,192,384]{3,2,1,0:T(8,128)(2,1)S(1)}, bf16[2,2,192,384]{3,2,1,0:T(8,128)(2,1)S(1)}, u32[]{:S(2)}, u32[]{:S(2)}) collective-permute-start(bf16[2,2,192,384]{3,2,1,0:T(8,128)(2,1)S(1)} %dynamic-slice_bitcast_fusion.2), channel_id=1, source_target_pairs={{0,2},{2,0},{1,3},{3,1},{4,6},{6,4},{5,7},{7,5},{8,10},{10,8},{9,1... | collective-permute-start | bytes 1769480 | tf_op jit(solution)/shard_map/ppermute | solution.py:186
  337.4 29.0 %collective-permute-start.65 = (bf16[2,2,48,1536]{3,2,1,0:T(8,128)(2,1)S(1)}, bf16[2,2,48,1536]{3,2,1,0:T(8,128)(2,1)S(1)}, u32[]{:S(2)}, u32[]{:S(2)}) collective-permute-start(bf16[2,2,48,1536]{3,2,1,0:T(8,128)(2,1)S(1)} %dynamic-slice_bitcast_fusion.3), channel_id=1, source_target_pairs={{0,16},{16,0},{1,17},{17,1},{2,18},{18,2},{3,19},{19,3},{4,20},{20... | collective-permute-start | bytes 1769480 | tf_op jit(solution)/shard_map/ppermute | solution.py:186
  365.5 9.0 %collective-permute-start.74 = (bf16[2,192,384]{2,1,0:T(8,128)(2,1)S(1)}, bf16[2,192,384]{2,1,0:T(8,128)(2,1)S(1)}, u32[]{:S(2)}, u32[]{:S(2)}) collective-permute-start(bf16[2,192,384]{2,1,0:T(8,128)(2,1)S(1)} %dynamic-slice_bitcast_fusion.6), channel_id=1, source_target_pairs={{0,8},{8,0},{1,9},{9,1},{2,10},{10,2},{3,11},{11,3},{4,12},{12,4},... | collective-permute-start | bytes 884744 | tf_op jit(solution)/shard_map/ppermute | solution.py:186
  366.6 9.6 %collective-permute-start.66 = (bf16[2,48,1536]{2,1,0:T(8,128)(2,1)S(1)}, bf16[2,48,1536]{2,1,0:T(8,128)(2,1)S(1)}, u32[]{:S(2)}, u32[]{:S(2)}) collective-permute-start(bf16[2,48,1536]{2,1,0:T(8,128)(2,1)S(1)} %dynamic-slice_bitcast_fusion.7), channel_id=1, source_target_pairs={{0,1},{1,0},{2,3},{3,2},{4,5},{5,4},{6,7},{7,6},{8,9},{9,8},{10,11... | collective-permute-start | bytes 884744 | tf_op jit(solution)/shard_map/ppermute | solution.py:186
  385.9 10.0 %collective-permute-start.77 = (bf16[2,192,384]{2,1,0:T(8,128)(2,1)S(1)}, bf16[2,192,384]{2,1,0:T(8,128)(2,1)S(1)}, u32[]{:S(2)}, u32[]{:S(2)}) collective-permute-start(bf16[2,192,384]{2,1,0:T(8,128)(2,1)S(1)} %pad_maximum_fusion.23), channel_id=1, source_target_pairs={{0,8},{8,0},{1,9},{9,1},{2,10},{10,2},{3,11},{11,3},{4,12},{12,4},... | collective-permute-start | bytes 884744 | tf_op jit(solution)/shard_map/ppermute | solution.py:176
  390.1 10.7 %collective-permute-start.69 = (bf16[2,48,1536]{2,1,0:T(8,128)(2,1)S(1)}, bf16[2,48,1536]{2,1,0:T(8,128)(2,1)S(1)}, u32[]{:S(2)}, u32[]{:S(2)}) collective-permute-start(bf16[2,48,1536]{2,1,0:T(8,128)(2,1)S(1)} %pad_maximum_fusion.22), channel_id=1, source_target_pairs={{0,8},{8,0},{1,9},{9,1},{2,10},{10,2},{3,11},{11,3},{4,12},{12,4},... | collective-permute-start | bytes 884744 | tf_op jit(solution)/shard_map/ppermute | solution.py:176
  (73 other events, 582.1 us)

commit v2 on v1

v2 whole, which is shorter than its diff:
```python
import functools
import math

import jax
import jax.numpy as jnp
from jax import lax
from jax.experimental import pallas as pl
from jax.experimental.pallas import tpu as pltpu
from jax.sharding import Mesh, PartitionSpec as P

H = 12
HD = 64
EPSILON = 1e-06
ROOT_HALF = 1.0 / math.sqrt(2.0)
INV_ROOT_TAU = 1.0 / math.sqrt(2.0 * math.pi)
f32 = jnp.float32
bf16 = jnp.bfloat16
SWAP = [(0, 1), (1, 0)]
FREE = pl.CostEstimate(flops=0, bytes_accessed=0, transcendentals=0)


def norm_parts(values_in):
    row_mean = jnp.mean(values_in, axis=-1, keepdims=True)
    centred = values_in - row_mean
    inverse = lax.rsqrt(jnp.mean(centred * centred, axis=-1, keepdims=True) + EPSILON)
    return (centred * inverse, inverse)


def norm_back(grad_normal, normal_rows, inverse_rows):
    first_mean = jnp.mean(grad_normal, axis=-1, keepdims=True)
    second_mean = jnp.mean(grad_normal * normal_rows, axis=-1, keepdims=True)
    return inverse_rows * (grad_normal - first_mean - normal_rows * second_mean)


def dot_nt(a, b):
    return lax.dot_general(a, b, (((1,), (1,)), ((), ())), preferred_element_type=f32)


def dot_tn(a, b):
    return lax.dot_general(a, b, (((0,), (0,)), ((), ())), preferred_element_type=f32)


def dot_nn(a, b):
    return jnp.dot(a, b, preferred_element_type=f32)


def attention_kernel(length, qkv_ref, out_ref, prob_ref):
    rows = qkv_ref.shape[1]
    width = H * HD
    first = lax.broadcasted_iota(jnp.int32, (1, 2 * HD), 1) < HD
    key_live = lax.broadcasted_iota(jnp.int32, (rows, 1), 0) < length
    for pair in range(H // 2):
        lanes = pl.ds(pair * 2 * HD, 2 * HD)
        q2 = qkv_ref[0, :, pl.ds(pair * 2 * HD, 2 * HD)] * jnp.asarray(HD ** (-0.5), bf16)
        k2 = qkv_ref[0, :, pl.ds(width + pair * 2 * HD, 2 * HD)]
        v2 = qkv_ref[0, :, pl.ds(2 * width + pair * 2 * HD, 2 * HD)]
        total = None
        for half in range(2):
            mask = first if half == 0 else jnp.logical_not(first)
            scores = dot_nt(jnp.where(mask, k2, jnp.zeros_like(k2)), q2)
            scores = jnp.where(key_live, scores, -1e30)
            expo = jnp.exp(scores - jnp.max(scores, axis=0, keepdims=True))
            probs = (expo * (1.0 / jnp.sum(expo, axis=0, keepdims=True))).astype(bf16)
            prob_ref[0, 2 * pair + half] = probs
            part = dot_tn(probs, jnp.where(mask, v2, jnp.zeros_like(v2)))
            total = part if total is None else total + part
        out_ref[0, :, lanes] = total.astype(bf16)


def attention_back_kernel(qkv_ref, prob_ref, grad_ref, out_ref, sums_ref):
    width = H * HD
    first = lax.broadcasted_iota(jnp.int32, (1, 2 * HD), 1) < HD
    scale = jnp.asarray(HD ** (-0.5), f32)

    @pl.when(pl.program_id(0) == 0)
    def _():
        sums_ref[...] = jnp.zeros_like(sums_ref)

    for pair in range(H // 2):
        spots = [pl.ds(part * width + pair * 2 * HD, 2 * HD) for part in range(3)]
        q2 = qkv_ref[0, :, spots[0]]
        k2 = qkv_ref[0, :, spots[1]]
        v2 = qkv_ref[0, :, spots[2]]
        g2 = grad_ref[0, :, spots[0]]
        totals = [None, None, None]
        for half in range(2):
            mask = first if half == 0 else jnp.logical_not(first)

            def keep(v):
                return jnp.where(mask, v, jnp.zeros_like(v))

            probs = prob_ref[0, 2 * pair + half]
            g_half = keep(g2)
            grad_probs = dot_nt(v2, g_half)
            probs_wide = probs.astype(f32)
            delta = jnp.sum(grad_probs * probs_wide, axis=0, keepdims=True)
            grad_scores = (probs_wide * (grad_probs - delta)).astype(bf16)
            parts = (
                dot_tn(grad_scores, keep(k2)),
                dot_nn(grad_scores, keep(q2)),
                dot_nn(probs, g_half),
            )
            totals = [p if t is None else t + p for t, p in zip(totals, parts)]
        for part in range(3):
            value = totals[part] if part == 2 else totals[part] * scale
            value = value.astype(bf16)
            out_ref[0, :, spots[part]] = value
            sums_ref[:, spots[part]] += jnp.sum(value.astype(f32), axis=0, keepdims=True)


def attention(qkv, length):
    slots, rows, wide = qkv.shape
    width = wide // 3
    return pl.pallas_call(
        functools.partial(attention_kernel, length),
        grid=(slots,),
        in_specs=[pl.BlockSpec((1, rows, wide), lambda i: (i, 0, 0))],
        out_specs=[
            pl.BlockSpec((1, rows, width), lambda i: (i, 0, 0)),
            pl.BlockSpec((1, H, rows, rows), lambda i: (i, 0, 0, 0)),
        ],
        out_shape=[
            jax.ShapeDtypeStruct((slots, rows, width), bf16),
            pltpu.HBM((slots, H, rows, rows), bf16),
        ],
        compiler_params=pltpu.CompilerParams(vmem_limit_bytes=28 * 2**20),
        cost_estimate=FREE,
        name="attention",
    )(qkv)


def attention_back(qkv, probs, grad):
    slots, rows, wide = qkv.shape
    width = wide // 3
    return pl.pallas_call(
        attention_back_kernel,
        grid=(slots,),
        in_specs=[
            pl.BlockSpec((1, rows, wide), lambda i: (i, 0, 0)),
            pl.BlockSpec((1, H, rows, rows), lambda i: (i, 0, 0, 0)),
            pl.BlockSpec((1, rows, width), lambda i: (i, 0, 0)),
        ],
        out_specs=[
            pl.BlockSpec((1, rows, wide), lambda i: (i, 0, 0)),
            pl.BlockSpec((1, wide), lambda i: (0, 0)),
        ],
        out_shape=[
            jax.ShapeDtypeStruct((slots, rows, wide), bf16),
            jax.ShapeDtypeStruct((1, wide), f32),
        ],
        compiler_params=pltpu.CompilerParams(vmem_limit_bytes=28 * 2**20),
        cost_estimate=FREE,
        name="attention_back",
    )(qkv, probs, grad)


def hidden_back_kernel(grad_ref, weight_ref, slope_ref, out_ref, sums_ref):
    grad = dot_nt(grad_ref[...], weight_ref[...]) * slope_ref[...].astype(f32)
    grad = grad.astype(bf16)
    out_ref[...] = grad
    sums_ref[...] = jnp.sum(grad.astype(f32), axis=0, keepdims=True)


def hidden_back(grad, weight, slope):
    rows, width = grad.shape
    wide = weight.shape[0]
    tile = 512
    return pl.pallas_call(
        hidden_back_kernel,
        grid=(wide // tile,),
        in_specs=[
            pl.BlockSpec((rows, width), lambda i: (0, 0)),
            pl.BlockSpec((tile, width), lambda i: (i, 0)),
            pl.BlockSpec((rows, tile), lambda i: (0, i)),
        ],
        out_specs=[
            pl.BlockSpec((rows, tile), lambda i: (0, i)),
            pl.BlockSpec((1, tile), lambda i: (0, i)),
        ],
        out_shape=[
            jax.ShapeDtypeStruct((rows, wide), bf16),
            jax.ShapeDtypeStruct((1, wide), f32),
        ],
        compiler_params=pltpu.CompilerParams(vmem_limit_bytes=28 * 2**20),
        cost_estimate=FREE,
        name="hidden_back",
    )(grad, weight, slope)


def norm_back_kernel(grad_ref, weight_ref, value_ref, gain_ref, past_ref, out_ref, low_ref, sums_ref):
    upstream = dot_nt(grad_ref[...], weight_ref[...])
    normal, inverse = norm_parts(value_ref[...].astype(f32))

    @pl.when(pl.program_id(0) == 0)
    def _():
        sums_ref[...] = jnp.zeros_like(sums_ref)

    sums_ref[0:1] += jnp.sum(upstream * normal, axis=0, keepdims=True)
    sums_ref[1:2] += jnp.sum(upstream, axis=0, keepdims=True)
    total = past_ref[...].astype(f32) + norm_back(upstream * gain_ref[...], normal, inverse)
    low = total.astype(bf16)
    out_ref[...] = total
    low_ref[...] = low
    sums_ref[2:3] += jnp.sum(low.astype(f32), axis=0, keepdims=True)


def norm_back_low_kernel(grad_ref, weight_ref, value_ref, gain_ref, past_ref, low_ref, sums_ref):
    upstream = dot_nt(grad_ref[...], weight_ref[...])
    normal, inverse = norm_parts(value_ref[...].astype(f32))

    @pl.when(pl.program_id(0) == 0)
    def _():
        sums_ref[...] = jnp.zeros_like(sums_ref)

    sums_ref[0:1] += jnp.sum(upstream * normal, axis=0, keepdims=True)
    sums_ref[1:2] += jnp.sum(upstream, axis=0, keepdims=True)
    total = past_ref[...].astype(f32) + norm_back(upstream * gain_ref[...], normal, inverse)
    low_ref[...] = total.astype(bf16)


def matmul_norm_back(grad, weight, values, gain, past, count, both):
    rows, wide = grad.shape
    width = weight.shape[0]
    tile = rows // count
    tall = pl.BlockSpec((tile, width), lambda i: (i, 0))
    outs = [jax.ShapeDtypeStruct((rows, width), f32)] if both else []
    outs += [jax.ShapeDtypeStruct((rows, width), bf16), jax.ShapeDtypeStruct((8, width), f32)]
    return pl.pallas_call(
        norm_back_kernel if both else norm_back_low_kernel,
        grid=(count,),
        in_specs=[
            pl.BlockSpec((tile, wide), lambda i: (i, 0)),
            pl.BlockSpec((width, wide), lambda i: (0, 0)),
            tall,
            pl.BlockSpec((1, width), lambda i: (0, 0)),
            tall,
        ],
        out_specs=[tall] * (len(outs) - 1) + [pl.BlockSpec((8, width), lambda i: (0, 0))],
        out_shape=outs,
        compiler_params=pltpu.CompilerParams(vmem_limit_bytes=28 * 2**20),
        cost_estimate=FREE,
        name="matmul_norm_back",
    )(grad, weight, values, gain.reshape(1, width), past)


class Net:
    def __init__(self, rep_bits, shard_bits):
        self.core, self.x, self.y = rep_bits[-1], rep_bits[-2], rep_bits[-3]
        self.extra = tuple(rep_bits[:-3])
        self.rep = tuple(rep_bits)
        self.shard = tuple(shard_bits)
        self.bit = {name: lax.axis_index(name) for name in self.rep + self.shard}

    def other_way(self, name):
        return self.y if name == self.x else self.x

    def swap(self, piece, name):
        return lax.ppermute(piece, name, SWAP)

    def place(self, mine, other, name):
        bit = self.bit[name]
        return jnp.where(bit == 0, mine, other), jnp.where(bit == 0, other, mine)

    def join(self, piece, other, name, spot):
        return jnp.stack(self.place(piece, other, name), axis=spot)

    def grow(self, piece, name, spot):
        return self.join(piece, self.swap(piece, name), name, spot)

    def part_with(self, piece, name, spot):
        bit = self.bit[name]
        send = lax.dynamic_index_in_dim(piece, 1 - bit, spot, keepdims=False)
        keep = lax.dynamic_index_in_dim(piece, bit, spot, keepdims=False)
        return keep, self.swap(send, name)

    def core_half(self, matrix, other=False):
        half = matrix.shape[1] // 2
        bit = self.bit[self.core]
        return lax.dynamic_slice_in_dim(matrix, ((1 - bit) if other else bit) * half, half, 1)

    def both_cores(self, piece):
        return self.place(piece, self.swap(piece, self.core), self.core)

    def row_half(self, matrix, name):
        rows = matrix.shape[0] // 2
        return lax.dynamic_slice_in_dim(matrix, self.bit[name] * rows, rows, 0)

    def group_up(self, values):
        for spot, name in enumerate(self.shard):
            values = self.grow(values, name, spot)
        return values

    def place_in_group(self):
        me = 0
        for name in self.shard:
            me = 2 * me + self.bit[name]
        return me


def add(pair):
    return (pair[0].astype(f32) + pair[1].astype(f32)).astype(bf16)


def together(*values):
    return lax.optimization_barrier(values)


def cut_of(columns):
    return -(-columns // 256) * 128


def per_device(
    rep_bits,
    shard_bits,
    tokens,
    counts,
    w_qkv,
    b_query,
    b_value,
    w_proj,
    b_proj,
    gain_one,
    bias_one,
    gain_two,
    bias_two,
    w_up,
    b_up,
    w_down,
    b_down,
    out_grad,
):
    net = Net(rep_bits, shard_bits)
    group = 2 ** len(shard_bits)
    slot_count, length, width = tokens.shape
    padded = -(-length // 16) * 16
    row_count = slot_count * padded
    wide = w_up.shape[1]
    part = width // group
    blocks = w_down.shape[0] // part
    fill = ((0, 0), (0, padded - length), (0, 0))
    far, near = net.shard
    half_up, half_mid = wide // 2, width // 2

    plane = (net.x, net.y)

    def ways(piece):
        cut = cut_of(piece.shape[-1])
        return [piece[..., :cut], piece[..., cut:]]

    def fetch(mine):
        return jnp.concatenate(
            [net.row_half(p, name) for p, name in zip(ways(mine), plane)], axis=1
        )

    def send_plane(piece):
        return [net.swap(p, name) for p, name in zip(ways(piece), plane)]

    def join_plane(piece, others, spot):
        pairs = zip(ways(piece), others, plane)
        return jnp.concatenate(
            [net.join(p, o, name, spot).reshape(-1, p.shape[-1]) for p, o, name in pairs], axis=1
        )

    small = jnp.stack(
        [b_query, b_value, b_proj, gain_one, bias_one, gain_two, bias_two, b_down]
    )
    small = jnp.concatenate([small, b_up.reshape(-1, part)], axis=0)
    q_way = net.grow(fetch(net.core_half(w_qkv)), far, 0)
    small = net.grow(small, far, 0)
    mid_way = fetch(jnp.concatenate([net.core_half(w_up), net.core_half(w_proj)], axis=1))
    q_way, small, mid_way = together(q_way, small, mid_way)
    q_way = net.grow(q_way, near, 1)
    small = net.grow(small, near, 1)
    mid_got = net.swap(mid_way, far)
    down_mine = net.core_half(w_down).reshape(blocks, part, half_mid)
    down_mine = jnp.concatenate([down_mine[i] for i in range(blocks)], axis=1)
    q_way, small, mid_way, down_mine, tokens = together(
        q_way, small, mid_way, down_mine, tokens
    )
    q_got = send_plane(q_way)
    mid_way = net.join(mid_way, mid_got, far, 0)
    small = small.astype(f32).reshape(group, -1, part)
    rows = small[:, :8].transpose(1, 0, 2).reshape(8, width)
    query_bias, value_bias, proj_bias, gain_1, bias_1, gain_2, bias_2, down_bias = (
        rows[i] for i in range(8)
    )
    up_bias = small[:, 8:].reshape(wide)
    mid_way, down_way = together(mid_way, fetch(down_mine))
    mid_got = net.swap(mid_way, near)
    q_way, down_way = together(join_plane(q_way, q_got, 2), down_way)
    qkv_full = jnp.concatenate(net.both_cores(q_way), axis=1)

    live_slots = (jnp.arange(slot_count, dtype=jnp.int32) < counts[0]).astype(f32)
    live_rows = jnp.repeat(live_slots, padded)[:, None]
    low_inputs = jnp.pad(tokens, fill).reshape(row_count, width)
    inputs = low_inputs.astype(f32)
    normal_one, inverse_one = norm_parts(inputs)
    normed_one = (normal_one * gain_1 + bias_1).astype(bf16)
    qkv_bias = jnp.concatenate([query_bias, jnp.zeros_like(query_bias), value_bias])
    joined = (dot_nn(normed_one, qkv_full) + qkv_bias).astype(bf16)
    joined = joined.reshape(slot_count, padded, 3 * width)
    joined, mid_way = together(joined, mid_way)
    mid_way = net.join(mid_way, mid_got, near, 1)
    joined, mid_way, down_way = together(joined, mid_way, down_way)
    mid_got = send_plane(mid_way)
    down_got = net.swap(down_way, far)
    mixed, probs = attention(joined, length)
    mixed, mid_way, down_way, out_grad = together(mixed, mid_way, down_way, out_grad)
    mid_way = join_plane(mid_way, mid_got, 2)
    down_way = net.join(down_way, down_got, far, 0)
    mixed, mid_way, down_way = together(mixed, mid_way, down_way)
    down_got = net.swap(down_way, near)
    *mid_pairs, down_way = together(*net.both_cores(mid_way), down_way)
    down_way = net.join(down_way, down_got, near, 1)
    down_got = send_plane(down_way)
    mixed = mixed.reshape(row_count, width)
    mid = mid_pairs
    up_full = jnp.concatenate([m[:, :half_up] for m in mid], axis=1)
    proj_full = jnp.concatenate([m[:, half_up:] for m in mid], axis=1)
    middle = inputs + (dot_nn(mixed, proj_full) + proj_bias)
    normal_two, inverse_two = norm_parts(middle)
    normed_two = (normal_two * gain_2 + bias_2).astype(bf16)
    hidden = dot_nn(normed_two, up_full) + up_bias
    share = 0.5 * (1.0 + lax.erf(hidden * ROOT_HALF))
    active = (hidden * share).astype(bf16)
    active, down_way = together(active, down_way)
    down_pairs = net.both_cores(join_plane(down_way, down_got, 2))
    slope = (share + hidden * jnp.exp(-0.5 * hidden * hidden) * INV_ROOT_TAU).astype(bf16)
    down = [
        jnp.stack(
            [
                d.reshape(group, part, -1)[:, :, b * half_mid : (b + 1) * half_mid]
                for b in range(blocks)
            ],
            axis=1,
        )
        for d in down_pairs
    ]
    down_full = jnp.concatenate(down, axis=3).reshape(wide, width)

    def start_sum(left, right):
        return dot_tn(left, net.core_half(right, True)).astype(bf16)

    def own_sum(left, right, other):
        total = dot_tn(left, net.core_half(right)) + other.astype(f32)
        total = total.astype(bf16)
        return total.reshape(2, 2, 2, -1, total.shape[1])

    def part_plane(piece):
        pairs = [net.part_with(p, name, 2) for p, name in zip(ways(piece), plane)]
        return [p[0] for p in pairs], [p[1] for p in pairs]

    def add_plane(keeps, others):
        return jnp.concatenate([add(pair) for pair in zip(keeps, others)], axis=-1)

    def exchange_plane(piece):
        done = []
        for p, name in zip(ways(piece), plane):
            for other in (net.other_way(name),) + net.extra:
                p = add((p, net.swap(p, other)))
            done.append(p)
        return done

    def grow_plane(pieces):
        return jnp.concatenate(
            [
                net.grow(p, name, 0).reshape(-1, p.shape[-1])
                for p, name in zip(pieces, plane)
            ],
            axis=1,
        )

    grad_branch = jnp.pad(out_grad, fill).reshape(row_count, width)
    grad_branch = grad_branch * live_rows.astype(bf16)
    grad_down_b = jnp.sum(grad_branch.astype(f32), axis=0, keepdims=True)
    branch_2, d_send = together(grad_branch, start_sum(active, grad_branch))
    d_other = net.swap(d_send, net.core)
    result = middle + (dot_nn(active, down_full) + down_bias)
    layer_out = (result * live_rows).astype(bf16)
    layer_out = layer_out.reshape(slot_count, padded, width)[:, :length]
    branch_3, layer_out = together(grad_branch, layer_out)
    d_piece = own_sum(active, branch_3, d_other)
    branch_2, d_piece = together(branch_2, d_piece)
    d_keeps, d_others = part_plane(d_piece)
    grad_hidden, up_sums = hidden_back(branch_2, down_full, slope)
    grad_hidden, u_send = together(grad_hidden, start_sum(normed_two, grad_hidden))
    u_other = net.swap(u_send, net.core)
    grad_middle, grad_attn, mid_sums = matmul_norm_back(
        grad_hidden, up_full, middle, gain_2, grad_branch, slot_count, True
    )
    grad_attn, *d_keeps = together(grad_attn, *d_keeps)
    d_piece = add_plane(d_keeps, d_others)
    grad_hidden, grad_attn, d_piece = together(grad_hidden, grad_attn, d_piece)
    d_pair = net.part_with(d_piece, near, 1)
    grad_attn, p_send = together(grad_attn, start_sum(mixed, grad_attn))
    p_other = net.swap(p_send, net.core)
    u_piece = own_sum(normed_two, grad_hidden, u_other)
    grad_attn, u_piece = together(grad_attn, u_piece)
    p_piece = own_sum(mixed, grad_attn, p_other)
    grad_attn_2, u_piece = together(grad_attn, jnp.concatenate([u_piece, p_piece], axis=-1))
    u_keeps, u_others = part_plane(u_piece)
    grad_mixed = dot_nt(grad_attn_2, proj_full).astype(bf16)
    grad_joined, joined_sums = attention_back(
        joined, probs, grad_mixed.reshape(slot_count, padded, width)
    )
    grad_joined, d_keep, *u_keeps = together(
        grad_joined.reshape(row_count, 3 * width), d_pair[0], *u_keeps
    )
    d_piece = add((d_keep, d_pair[1]))
    u_piece = add_plane(u_keeps, u_others)
    grad_joined, d_piece, u_piece = together(grad_joined, d_piece, u_piece)
    d_pair = net.part_with(d_piece, far, 0)
    u_pair = net.part_with(u_piece, near, 1)
    grad_joined, q_send = together(grad_joined, start_sum(normed_one, grad_joined))
    q_other = net.swap(q_send, net.core)
    q_piece = own_sum(normed_one, grad_joined, q_other)
    grad_joined, q_piece = together(grad_joined, q_piece)
    q_keeps, q_others = part_plane(q_piece)
    grad_tokens, first_sums = matmul_norm_back(
        grad_joined, qkv_full, low_inputs, gain_1, grad_middle, slot_count, False
    )
    grad_tokens = grad_tokens.reshape(slot_count, padded, width)[:, :length]

    vectors = [
        mid_sums[2:3],
        mid_sums[0:2],
        grad_down_b,
        joined_sums[:, :width],
        joined_sums[:, 2 * width :],
        first_sums[0:2],
    ]
    vectors += [up_sums[:, k * width : (k + 1) * width] for k in range(group)]
    vectors = jnp.concatenate(vectors, axis=0)

    vectors, u_keep, *q_keeps = together(vectors, u_pair[0], *q_keeps)
    sums = vectors + net.swap(vectors, net.core)
    q_piece = add_plane(q_keeps, q_others)
    q_piece, u_keep, d_keep, sums = together(q_piece, u_keep, d_pair[0], sums)
    q_pair = net.part_with(q_piece, near, 1)
    u_piece = add((u_keep, u_pair[1]))
    u_piece, d_keep, sums, q_keep = together(u_piece, d_keep, sums, q_pair[0])
    u_pair = net.part_with(u_piece, far, 0)
    d_piece = exchange_plane(add((d_keep, d_pair[1])))
    sums = sums + net.swap(sums, net.x)
    q_piece = add((q_keep, q_pair[1]))
    q_piece, u_keep, sums, *d_piece = together(q_piece, u_pair[0], sums, *d_piece)
    q_pair = net.part_with(q_piece, far, 0)
    down_shard = grow_plane(d_piece)
    sums = sums + net.swap(sums, net.y)
    u_piece = exchange_plane(add((u_keep, u_pair[1])))
    q_keep, sums, down_shard, *u_piece = together(q_pair[0], sums, down_shard, *u_piece)
    q_piece = add((q_keep, q_pair[1]))
    up_shard = grow_plane(u_piece)
    down_pair = net.both_cores(down_shard)
    sums = sums + net.swap(sums, far)
    q_1, q_2 = exchange_plane(q_piece)
    q_1, q_2, sums, up_shard = together(q_1, q_2, sums, up_shard)
    up_pair = net.both_cores(up_shard)
    q_pair = net.both_cores(grow_plane([q_1, q_2]))
    for name in (near,) + net.extra:
        sums = sums + net.swap(sums, name)
    me = net.place_in_group()
    owned = lax.dynamic_slice_in_dim(sums[:8], me * part, part, 1)
    owned_up = lax.dynamic_index_in_dim(sums, 8 + me, 0, keepdims=False)
    grad_down_w = jnp.concatenate(down_pair, axis=1).astype(f32)
    grad_up_w = jnp.concatenate([p[:, :half_up] for p in up_pair], axis=1).astype(f32)
    grad_proj_w = jnp.concatenate([p[:, half_up:] for p in up_pair], axis=1).astype(f32)
    grad_qkv_w = jnp.concatenate(q_pair, axis=1).astype(f32)
    return (
        layer_out,
        grad_tokens,
        grad_qkv_w,
        owned[4],
        owned[5],
        grad_proj_w,
        owned[0],
        owned[6],
        owned[7],
        owned[1],
        owned[2],
        grad_up_w,
        owned_up,
        grad_down_w,
        owned[3],
    )


def solution(mesh):
    rep, shard = mesh.shape["rep"], mesh.shape["shard"]
    rep_bits = tuple(f"r{i}" for i in range(rep.bit_length() - 1))
    shard_bits = tuple(f"s{i}" for i in range(shard.bit_length() - 1))
    fine = Mesh(mesh.devices.reshape((2,) * (len(rep_bits) + len(shard_bits))), rep_bits + shard_bits)
    every = P(rep_bits + shard_bits, None, None)
    matrix = P(shard_bits, None)
    vector = P(shard_bits)
    return jax.shard_map(
        functools.partial(per_device, rep_bits, shard_bits),
        mesh=fine,
        in_specs=(
            every,
            P(rep_bits + shard_bits),
            matrix,
            vector,
            vector,
            matrix,
            vector,
            vector,
            vector,
            vector,
            vector,
            matrix,
            vector,
            matrix,
            vector,
            every,
        ),
        out_specs=(
            every,
            every,
            matrix,
            vector,
            vector,
            matrix,
            vector,
            vector,
            vector,
            vector,
            vector,
            matrix,
            vector,
            matrix,
            vector,
        ),
        check_vma=False,
    )
```

time: 413 us -> 346 us (0.84)
  starting transfers between devices: 84.4 us -> 46.8 us
  matrix products: 94.7 us -> 60.2 us
  Pallas kernels: 20.5 us -> 47.8 us
  waiting for transfers between devices: 126 us -> 108 us
    ppermute x79 -> x53, starting transfers between devices: 84.4 us -> 46.8 us  [swap(): return lax.ppermute(piece, name, SWAP)]
    dot_general x4 -> x1, matrix products: 36.8 us -> 1.46 us  [dot_nt(): lax.dot_general(a, b, (((1,), (1,)), ((), ())), preferred_element_type=f32)]
    pallas_call x0 -> x3, Pallas kernels: none -> 26.6 us  [the longest x2 19 us: matmul_norm_back(): pl.pallas_call(norm_back_kernel if both else norm_back_low_kernel, grid=(...]
    ppermute x79 -> x53, waiting for transfers between devices: 126 us -> 108 us  [swap(): return lax.ppermute(piece, name, SWAP)]
    select_n x10 -> x6, other arithmetic: 1.69 us -> 7.7 us  [place(): return (jnp.where(bit == 0, mine, other), jnp.where(bit == 0, other, mine))]
    concatenate x6 -> x18, other arithmetic: 2 us -> 7.78 us  [the longest x3 3.35 us: join_plane(): jnp.concatenate([net.join(p, o, name, spot).reshape(-1, p.shape[-1]) for...]
    convert_element_type x2 -> x1, other arithmetic: 6.39 us -> 0.66 us  [per_device(): normed_one = (normal_one * gain_1 + bias_1).astype(bf16)]
    unnamed x90 -> x98, local copies, waits for them, and re-layouts: 15.4 us -> 9.71 us
  transfers between devices with their start and end apart: 79 -> 53, of which waited for: 29 -> 29; matrix products, arithmetic and copies ran while one was open for 24% -> 28% of each run, Pallas kernels for 5% -> 12%
where the time goes in v2:
time: 346 us; the launch traced here: 341 us
  waiting for transfers between devices  108 us (31%)
  matrix products  60.2 us (17%)
  Pallas kernels  47.8 us (14%)
  starting transfers between devices  46.8 us (14%)
  other arithmetic  38.5 us (11%)
  local copies, waits for them, and re-layouts  36.6 us (11%)
    ppermute x53, waiting for transfers between devices, swap(): return lax.ppermute(piece, name, SWAP)  108 us
    ppermute x53, starting transfers between devices, swap(): return lax.ppermute(piece, name, SWAP)  46.8 us
    dot_general x8, matrix products, dot_tn(): lax.dot_general(a, b, (((0,), (0,)), ((), ())), preferred_element_type=f32)  33.5 us
    dot_general x4, matrix products, dot_nn(): return jnp.dot(a, b, preferred_element_type=f32)  25.3 us
    pallas_call x2, Pallas kernels, matmul_norm_back(): pl.pallas_call(norm_back_kernel if both else norm_back_low_kernel, grid=(...  19 us
    pallas_call x1, Pallas kernels, attention_back(): pl.pallas_call(attention_back_kernel, grid=(slots,), in_specs=[pl.BlockSp...  12.7 us
    unnamed x98, local copies, waits for them, and re-layouts  9.71 us
    pallas_call x1, Pallas kernels, attention(): pl.pallas_call(functools.partial(attention_kernel, length), grid=(slots,)...  8.44 us
  transfers between devices with their start and end apart: 53, of which 29 were waited for; matrix products, arithmetic and copies ran while one was open for 28% of the time, Pallas kernels for 12%

profile of v2, /device:TPU:0, one launch (start us, length us, event | category | flops | bytes accessed | tf_op | source)
XLA Modules:
  0.0 341.1 jit_solution(2256247560046439962)
XLA Ops:
  2.6 4.1 %collective-permute-start = (bf16[96,1152]{1,0:T(8,128)(2,1)S(1)}, bf16[96,1152]{1,0:T(8,128)(2,1)S(1)}, u32[]{:S(2)}, u32[]{:S(2)}) collective-permute-start(bf16[96,1152]{1,0:T(8,128)(2,1)S(1)} %pad_maximum_fusion.34), channel_id=1, source_target_pairs={{0,2},{2,0},{1,3},{3,1},{4,6},{6,4},{5,7},{7,5},{8,10},{10,8},{9,1... | collective-permute-start | bytes 663560 | tf_op jit(solution)/shard_map/ppermute | solution.py:258
  15.3 2.0 collective-permute-done.1
  17.5 1.6 collective-permute-start.2
  19.7 2.1 collective-permute-start.6
  21.7 15.1 %collective-permute-done.3 = bf16[2,12,192]{2,1,0:T(8,128)(2,1)S(1)} collective-permute-done((bf16[2,12,192]{2,1,0:T(8,128)(2,1)S(1)}, bf16[2,12,192]{2,1,0:T(8,128)(2,1)S(1)}, u32[]{:S(2)}, u32[]{:S(2)}) %collective-permute-start.3) | collective-permute-done | bytes 9248 | tf_op jit(solution)/shard_map/ppermute | solution.py:258
  42.1 5.2 %collective-permute-done.5 = bf16[2,2,96,512]{3,2,0,1:T(8,128)(2,1)} collective-permute-done((bf16[2,2,96,512]{3,2,0,1:T(8,128)(2,1)}, bf16[2,2,96,512]{3,2,0,1:T(8,128)(2,1)}, u32[]{:S(2)}, u32[]{:S(2)}) %collective-permute-start.5) | collective-permute-done | bytes 393248 | tf_op jit(solution)/shard_map/ppermute | solution.py:258
  48.5 1.6 collective-permute-done.4
  55.9 2.3 broadcast_select_fusion.5
  58.3 4.6 %fusion.5 = bf16[1040,2304]{1,0:T(8,128)(2,1)S(1)} fusion(bf16[1040,768]{1,0:T(8,128)(2,1)S(1)} %fusion.12, f32[2304]{0:T(1024)S(1)} %pad_maximum_fusion.39, bf16[768,1152]{1,0:T(8,128)(2,1)S(1)} %get-tuple-element.216, bf16[768,1152]{1,0:T(8,128)(2,1)S(1)} %get-tuple-element.215), kind=kOutput, calls=%fused_computation.10 | convolution fusion | flops 3692371968 | bytes 9937920 | tf_op jit(solution)/shard_map/dot_general | solution.py:44
  62.9 9.6 %collective-permute-done.8 = bf16[2,96,1920]{2,1,0:T(8,128)(2,1)S(1)} collective-permute-done((bf16[2,96,1920]{2,1,0:T(8,128)(2,1)}, bf16[2,96,1920]{2,1,0:T(8,128)(2,1)S(1)}, u32[]{:S(2)}, u32[]{:S(2)}) %collective-permute-start.8) | collective-permute-done | bytes 737312 | tf_op jit(solution)/shard_map/ppermute | solution.py:258
  72.8 3.1 collective-permute-start.11
  76.1 8.4 %attention.1 = (bf16[5,208,768]{2,1,0:T(8,128)(2,1)S(1)}, bf16[5,12,208,208]{3,2,1,0:T(8,128)(2,1)}) custom-call(bf16[5,208,2304]{2,1,0:T(8,128)(2,1)S(1)} %bitcast.217), custom_call_target="tpu_custom_call" | custom-call | tf_op jit(solution)/shard_map/attention/pallas_call | solution.py:114
  86.6 2.7 collective-permute-done.11
  90.1 11.3 %collective-permute-done.10 = bf16[2,2,96,896]{3,2,0,1:T(8,128)(2,1)S(1)} collective-permute-done((bf16[2,2,96,896]{3,2,0,1:T(8,128)(2,1)S(1)}, bf16[2,2,96,896]{3,2,0,1:T(8,128)(2,1)S(1)}, u32[]{:S(2)}, u32[]{:S(2)}) %collective-permute-start.10) | collective-permute-done | bytes 688160 | tf_op jit(solution)/shard_map/ppermute | solution.py:258
  101.8 1.9 collective-permute-done.9
  106.3 3.7 %collective-permute-done.12 = bf16[768,1920]{1,0:T(8,128)(2,1)} collective-permute-done((bf16[768,1920]{1,0:T(8,128)(2,1)S(1)}, bf16[768,1920]{1,0:T(8,128)(2,1)}, u32[]{:S(2)}, u32[]{:S(2)}) %collective-permute-start.12) | collective-permute-done | bytes 2949152 | tf_op jit(solution)/shard_map/ppermute | solution.py:258
  110.0 2.4 broadcast_select_fusion
  113.7 1.7 copy-done.2
  116.5 1.6 fusion.55
  118.7 2.1 collective-permute-done.13
  125.7 13.9 %fusion.4 = (bf16[1040,3072]{1,0:T(8,128)(2,1)}, bf16[1040,3072]{1,0:T(8,128)(2,1)}) fusion(f32[3072]{0:T(1024)S(1)} %add.296, bf16[1040,768]{1,0:T(8,128)(2,1)S(1)} %add_convert_fusion.3, bf16[768,1536]{1,0:T(8,128)(2,1)S(1)} %slice.279, bf16[768,1536]{1,0:T(8,128)(2,1)S(1)} %slice.278), kind=kOutput, calls=%fused_computation.7 | convolution fusion | flops 4955111424 | bytes 19107840 | tf_op jit(solution)/shard_map/dot_general | solution.py:44
  140.3 1.8 pad_maximum_fusion.4
  145.0 7.6 %convolution_convert_fusion = bf16[3072,384]{1,0:T(8,128)(2,1)S(1)} fusion(bf16[1040,3072]{1,0:T(8,128)(2,1)} %get-tuple-element.140, bf16[1040,768]{1,0:T(8,128)(2,1)S(1)} %bitcast_multiply_fusion.grad_ref.past_ref, s32[]{:T(128)S(6)} %select_n.459), kind=kOutput, calls=%fused_computation.15 | convolution fusion | flops 2454847488 | bytes 9547780 | tf_op jit(solution)/shard_map/dot_general | solution.py:40
  153.2 2.6 broadcast_select_fusion.3
  159.0 5.2 %fusion.8 = bf16[1040,768]{1,0:T(8,128)(2,1)S(1)} fusion(f32[1040,768]{1,0:T(8,128)S(1)} %get-tuple-element.328.value_ref, bf16[1040,3072]{1,0:T(8,128)(2,1)S(1)} %bitcast.273, bf16[3072,768]{1,0:T(8,128)(2,1)S(1)} %bitcast.221, f32[1040]{0:T(1024)S(1)} %broadcast_in_dim_reshape.4, f32[768]{0:T(1024)S(1)} %add.301), kind=kOutput, calls=%fused_computation.26 | convolution fusion | flops 4910530560 | bytes 15907904 | tf_op jit(solution)/shard_map/dot_general | solution.py:44
  165.4 5.7 %add_convert_fusion.1 = bf16[3072,384]{1,0:T(8,128)(2,1)} fusion(bf16[3072,384]{1,0:T(8,128)(2,1)S(1)} %collective-permute-done.17, bf16[1040,3072]{1,0:T(8,128)(2,1)S(1)} %bitcast.273, bf16[1040,768]{1,0:T(8,128)(2,1)S(1)} %bitcast_multiply_fusion.grad_ref.past_ref, s32[]{:T(128)S(6)} %select_n.414), kind=kOutput, calls=%fused_computation.14 | convolution fusion | flops 2457206784 | bytes 11907076 | tf_op jit(solution)/shard_map/dot_general | solution.py:40
  171.2 7.7 %hidden_back.1 = (bf16[1040,3072]{1,0:T(8,128)(2,1)S(1)}, f32[1,3072]{1,0:T(1,128)S(1)}) custom-call(bf16[1040,768]{1,0:T(8,128)(2,1)S(1)} %bitcast_multiply_fusion.grad_ref.past_ref, bf16[3072,768]{1,0:T(8,128)(2,1)S(1)} %bitcast.222, bf16[1040,3072]{1,0:T(8,128)(2,1)S(1)} %bitcast.228), custom_call_target="tpu_custom_call" | custom-call | tf_op jit(solution)/shard_map/hidden_back/pallas_call | solution.py:168
  178.8 4.6 %convolution_convert_fusion.1 = bf16[768,1536]{1,0:T(8,128)(2,1)} fusion(bf16[1040,768]{1,0:T(8,128)(2,1)S(1)} %copy-done.32, bf16[1040,3072]{1,0:T(8,128)(2,1)S(1)} %get-tuple-element.157.grad_ref, s32[]{:T(128)S(6)} %select_n.460), kind=kOutput, calls=%fused_computation.27 | convolution fusion | flops 2454847488 | bytes 7151620 | tf_op jit(solution)/shard_map/dot_general | solution.py:40
  190.2 10.5 %matmul_norm_back.2 = (f32[1040,768]{1,0:T(8,128)S(1)}, bf16[1040,768]{1,0:T(8,128)(2,1)S(1)}, f32[8,768]{1,0:T(8,128)S(1)}) custom-call(bf16[1040,3072]{1,0:T(8,128)(2,1)S(1)} %bitcast.230, bf16[768,3072]{1,0:T(8,128)(2,1)S(1)} %pad_maximum_fusion.weight_ref, f32[1040,768]{1,0:T(8,128)S(1)} %get-tuple-element.328.value_ref, f32[1,768]{1,0:T(1,128)S(1)} %slice.295.gain_ref, ...), custom_call_target="tpu_custom_call" | custom-call | tf_op jit(solution)/shard_map/matmul_norm_back/pallas_call | solution.py:228
  202.2 4.4 %collective-permute-done.18 = bf16[2,2,384,256]{3,2,1,0:T(8,128)(2,1)S(1)} collective-permute-done((bf16[2,2,384,256]{3,2,1,0:T(8,128)(2,1)S(1)}, bf16[2,2,384,256]{3,2,1,0:T(8,128)(2,1)S(1)}, u32[]{:S(2)}, u32[]{:S(2)}) %collective-permute-start.18) | collective-permute-done | bytes 786464 | tf_op jit(solution)/shard_map/ppermute | solution.py:258
  209.9 5.3 %add_convert_fusion = bf16[768,1536]{1,0:T(8,128)(2,1)S(1)} fusion(bf16[768,1536]{1,0:T(8,128)(2,1)} %collective-permute-done.20, bf16[1040,768]{1,0:T(8,128)(2,1)S(1)} %copy-done.33, bf16[1040,3072]{1,0:T(8,128)(2,1)S(1)} %bitcast.230, s32[]{:T(128)} %select_n.413), kind=kOutput, calls=%fused_computation.13 | convolution fusion | flops 2457206784 | bytes 9510916 | tf_op jit(solution)/shard_map/dot_general | solution.py:40
  221.1 12.7 %attention_back.1 = (bf16[5,208,2304]{2,1,0:T(8,128)(2,1)S(1)}, f32[1,2304]{1,0:T(1,128)S(1)}) custom-call(bf16[5,208,2304]{2,1,0:T(8,128)(2,1)S(1)} %bitcast.220, bf16[5,12,208,208]{3,2,1,0:T(8,128)(2,1)S(1)} %bitcast.226, bf16[5,208,768]{2,1,0:T(8,128)(2,1)S(1)} %bitcast.234), custom_call_target="tpu_custom_call" | custom-call | tf_op jit(solution)/shard_map/attention_back/pallas_call | solution.py:135
  235.1 2.2 collective-permute-done.23
  237.8 3.8 %convolution_convert_fusion.2 = bf16[768,1152]{1,0:T(8,128)(2,1)} fusion(bf16[1040,768]{1,0:T(8,128)(2,1)S(1)} %copy-done.29, bf16[1040,2304]{1,0:T(8,128)(2,1)S(1)} %bitcast.231, s32[]{:T(128)S(6)} %select_n.467), kind=kOutput, calls=%fused_computation.28 | convolution fusion | flops 1841135616 | bytes 5763076 | tf_op jit(solution)/shard_map/dot_general | solution.py:40
  242.4 2.4 pad_maximum_fusion.1.weight_ref
  246.3 4.1 %add_convert_fusion.2 = bf16[768,1152]{1,0:T(8,128)(2,1)S(1)} fusion(bf16[768,1152]{1,0:T(8,128)(2,1)} %collective-permute-done.25, bf16[1040,768]{1,0:T(8,128)(2,1)S(1)} %copy-done.30, bf16[1040,2304]{1,0:T(8,128)(2,1)S(1)} %bitcast.232, s32[]{:T(128)S(6)} %select_n.405), kind=kOutput, calls=%fused_computation.25 | convolution fusion | flops 1842905088 | bytes 7532548 | tf_op jit(solution)/shard_map/dot_general | solution.py:40
  256.1 8.4 %matmul_norm_back.3 = (bf16[1040,768]{1,0:T(8,128)(2,1)S(1)}, f32[8,768]{1,0:T(8,128)S(1)}) custom-call(bf16[1040,2304]{1,0:T(8,128)(2,1)S(1)} %bitcast.233, bf16[768,2304]{1,0:T(8,128)(2,1)S(1)} %pad_maximum_fusion.1.weight_ref, bf16[1040,768]{1,0:T(8,128)(2,1)S(1)} %bitcast.224, f32[1,768]{1,0:T(1,128)S(1)} %slice.300.gain_ref, f32[1040,768]{1,0:T(8,128)S(1)} %copy-done.10), custom_call_target="tpu_custom_call" | custom-call | tf_op jit(solution)/shard_map/matmul_norm_back/pallas_call | solution.py:228
  269.9 11.1 %collective-permute-done.29 = bf16[2,96,1920]{2,1,0:T(8,128)(2,1)} collective-permute-done((bf16[2,96,1920]{2,1,0:T(8,128)(2,1)}, bf16[2,96,1920]{2,1,0:T(8,128)(2,1)}, u32[]{:S(2)}, u32[]{:S(2)}) %collective-permute-start.29) | collective-permute-done | bytes 737312 | tf_op jit(solution)/shard_map/ppermute | solution.py:258
  282.3 1.6 collective-permute-start.31
  286.5 2.2 collective-permute-done.34
  288.7 1.7 collective-permute-done.33
  290.4 2.8 collective-permute-done.30
  293.4 2.0 collective-permute-start.37
  295.4 10.4 %collective-permute-done.38 = bf16[96,1920]{1,0:T(8,128)(2,1)S(1)} collective-permute-done((bf16[96,1920]{1,0:T(8,128)(2,1)S(1)}, bf16[96,1920]{1,0:T(8,128)(2,1)S(1)}, u32[]{:S(2)}, u32[]{:S(2)}) %collective-permute-start.38) | collective-permute-done | bytes 368672 | tf_op jit(solution)/shard_map/ppermute | solution.py:258
  308.7 6.0 %collective-permute-done.40 = bf16[96,896]{1,0:T(8,128)(2,1)S(1)} collective-permute-done((bf16[96,896]{1,0:T(8,128)(2,1)S(1)}, bf16[96,896]{1,0:T(8,128)(2,1)S(1)}, u32[]{:S(2)}, u32[]{:S(2)}) %collective-permute-start.40) | collective-permute-done | bytes 172064 | tf_op jit(solution)/shard_map/ppermute | solution.py:258
  316.1 2.8 collective-permute-start.44
  322.2 3.5 %collective-permute-done.42 = bf16[96,640]{1,0:T(8,128)(2,1)S(1)} collective-permute-done((bf16[96,640]{1,0:T(8,128)(2,1)S(1)}, bf16[96,640]{1,0:T(8,128)(2,1)S(1)}, u32[]{:S(2)}, u32[]{:S(2)}) %collective-permute-start.42) | collective-permute-done | bytes 122912 | tf_op jit(solution)/shard_map/ppermute | solution.py:258
  339.2 1.7 maximum_convert_fusion
  (382 shorter events, 102.0 us)
Async XLA Ops:
  2.6 14.8 %collective-permute-start = (bf16[96,1152]{1,0:T(8,128)(2,1)S(1)}, bf16[96,1152]{1,0:T(8,128)(2,1)S(1)}, u32[]{:S(2)}, u32[]{:S(2)}) collective-permute-start(bf16[96,1152]{1,0:T(8,128)(2,1)S(1)} %pad_maximum_fusion.34), channel_id=1, source_target_pairs={{0,2},{2,0},{1,3},{3,1},{4,6},{6,4},{5,7},{7,5},{8,10},{10,8},{9,1... | collective-permute-start | bytes 663560 | tf_op jit(solution)/shard_map/ppermute | solution.py:258
  12.7 4.6 %collective-permute-start.1 = (bf16[12,192]{1,0:T(8,128)(2,1)S(1)}, bf16[12,192]{1,0:T(8,128)(2,1)S(1)}, u32[]{:S(2)}, u32[]{:S(2)}) collective-permute-start(bf16[12,192]{1,0:T(8,128)(2,1)S(1)} %concatenate.79), channel_id=1, source_target_pairs={{0,2},{2,0},{1,3},{3,1},{4,6},{6,4},{5,7},{7,5},{8,10},{10,8},{9,1... | collective-permute-start | bytes 13832 | tf_op jit(solution)/shard_map/ppermute | solution.py:258
  17.5 19.4 %collective-permute-start.2 = (bf16[2,96,1152]{2,1,0:T(8,128)(2,1)S(1)}, bf16[2,96,1152]{2,1,0:T(8,128)(2,1)S(1)}, u32[]{:S(2)}, u32[]{:S(2)}) collective-permute-start(bf16[2,96,1152]{2,1,0:T(8,128)(2,1)S(1)} %pad_maximum_fusion.26), channel_id=1, source_target_pairs={{0,1},{1,0},{2,3},{3,2},{4,5},{5,4},{6,7},{7,6},{8,9},{9,8},{10,11... | collective-permute-start | bytes 1327112 | tf_op jit(solution)/shard_map/ppermute | solution.py:258
  19.2 17.7 %collective-permute-start.3 = (bf16[2,12,192]{2,1,0:T(8,128)(2,1)S(1)}, bf16[2,12,192]{2,1,0:T(8,128)(2,1)S(1)}, u32[]{:S(2)}, u32[]{:S(2)}) collective-permute-start(bf16[2,12,192]{2,1,0:T(8,128)(2,1)S(1)} %pad_maximum_fusion.38), channel_id=1, source_target_pairs={{0,1},{1,0},{2,3},{3,2},{4,5},{5,4},{6,7},{7,6},{8,9},{9,8},{10,11... | collective-permute-start | bytes 27656 | tf_op jit(solution)/shard_map/ppermute | solution.py:258
  19.7 21.3 %collective-permute-start.6 = (bf16[96,1920]{1,0:T(8,128)(2,1)S(1)}, bf16[96,1920]{1,0:T(8,128)(2,1)S(1)}, u32[]{:S(2)}, u32[]{:S(2)}) collective-permute-start(bf16[96,1920]{1,0:T(8,128)(2,1)S(1)} %pad_maximum_fusion.30), channel_id=1, source_target_pairs={{0,2},{2,0},{1,3},{3,1},{4,6},{6,4},{5,7},{7,5},{8,10},{10,8},{9,1... | collective-permute-start | bytes 1105928 | tf_op jit(solution)/shard_map/ppermute | solution.py:258
  37.9 9.4 %collective-permute-start.5 = (bf16[2,2,96,512]{3,2,0,1:T(8,128)(2,1)}, bf16[2,2,96,512]{3,2,0,1:T(8,128)(2,1)}, u32[]{:S(2)}, u32[]{:S(2)}) collective-permute-start(bf16[2,2,96,512]{3,2,0,1:T(8,128)(2,1)} %slice.264), channel_id=1, source_target_pairs={{0,16},{16,0},{1,17},{17,1},{2,18},{18,2},{3,19},{19,3},{4,20},{20... | collective-permute-start | bytes 1179656 | tf_op jit(solution)/shard_map/ppermute | solution.py:258
  39.4 10.8 %collective-permute-start.4 = (bf16[2,2,96,640]{3,2,0,1:T(8,128)(2,1)S(1)}, bf16[2,2,96,640]{3,2,0,1:T(8,128)(2,1)S(1)}, u32[]{:S(2)}, u32[]{:S(2)}) collective-permute-start(bf16[2,2,96,640]{3,2,0,1:T(8,128)(2,1)S(1)} %slice.263), channel_id=1, source_target_pairs={{0,8},{8,0},{1,9},{9,1},{2,10},{10,2},{3,11},{11,3},{4,12},{12,4},... | collective-permute-start | bytes 1474568 | tf_op jit(solution)/shard_map/ppermute | solution.py:258
  53.6 18.9 %collective-permute-start.8 = (bf16[2,96,1920]{2,1,0:T(8,128)(2,1)}, bf16[2,96,1920]{2,1,0:T(8,128)(2,1)S(1)}, u32[]{:S(2)}, u32[]{:S(2)}) collective-permute-start(bf16[2,96,1920]{2,1,0:T(8,128)(2,1)} %pad_maximum_fusion.21), channel_id=1, source_target_pairs={{0,1},{1,0},{2,3},{3,2},{4,5},{5,4},{6,7},{7,6},{8,9},{9,8},{10,11... | collective-permute-start | bytes 2211848 | tf_op jit(solution)/shard_map/ppermute | solution.py:258
  72.8 16.4 %collective-permute-start.11 = (bf16[96,1536]{1,0:T(8,128)(2,1)S(1)}, bf16[96,1536]{1,0:T(8,128)(2,1)S(1)}, u32[]{:S(2)}, u32[]{:S(2)}) collective-permute-start(bf16[96,1536]{1,0:T(8,128)(2,1)S(1)} %pad_maximum_fusion.32), channel_id=1, source_target_pairs={{0,2},{2,0},{1,3},{3,1},{4,6},{6,4},{5,7},{7,5},{8,10},{10,8},{9,1... | collective-permute-start | bytes 884744 | tf_op jit(solution)/shard_map/ppermute | solution.py:258
  84.6 16.8 %collective-permute-start.10 = (bf16[2,2,96,896]{3,2,0,1:T(8,128)(2,1)S(1)}, bf16[2,2,96,896]{3,2,0,1:T(8,128)(2,1)S(1)}, u32[]{:S(2)}, u32[]{:S(2)}) collective-permute-start(bf16[2,2,96,896]{3,2,0,1:T(8,128)(2,1)S(1)} %slice.272), channel_id=1, source_target_pairs={{0,16},{16,0},{1,17},{17,1},{2,18},{18,2},{3,19},{19,3},{4,20},{20... | collective-permute-start | bytes 2064392 | tf_op jit(solution)/shard_map/ppermute | solution.py:258
  85.1 18.7 %collective-permute-start.9 = (bf16[2,2,96,1024]{3,2,0,1:T(8,128)(2,1)S(1)}, bf16[2,2,96,1024]{3,2,0,1:T(8,128)(2,1)S(1)}, u32[]{:S(2)}, u32[]{:S(2)}) collective-permute-start(bf16[2,2,96,1024]{3,2,0,1:T(8,128)(2,1)S(1)} %slice.270), channel_id=1, source_target_pairs={{0,8},{8,0},{1,9},{9,1},{2,10},{10,2},{3,11},{11,3},{4,12},{12,4},... | collective-permute-start | bytes 2359304 | tf_op jit(solution)/shard_map/ppermute | solution.py:258
  104.5 5.6 %collective-permute-start.12 = (bf16[768,1920]{1,0:T(8,128)(2,1)S(1)}, bf16[768,1920]{1,0:T(8,128)(2,1)}, u32[]{:S(2)}, u32[]{:S(2)}) collective-permute-start(bf16[768,1920]{1,0:T(8,128)(2,1)S(1)} %pad_maximum_fusion.2), channel_id=1, source_target_pairs={{0,4},{4,0},{1,5},{5,1},{2,6},{6,2},{3,7},{7,3},{8,12},{12,8},{9,1... | collective-permute-start | bytes 8847368 | tf_op jit(solution)/shard_map/ppermute | solution.py:258
  104.9 15.9 %collective-permute-start.13 = (bf16[2,96,1536]{2,1,0:T(8,128)(2,1)}, bf16[2,96,1536]{2,1,0:T(8,128)(2,1)S(1)}, u32[]{:S(2)}, u32[]{:S(2)}) collective-permute-start(bf16[2,96,1536]{2,1,0:T(8,128)(2,1)} %pad_maximum_fusion.24), channel_id=1, source_target_pairs={{0,1},{1,0},{2,3},{3,2},{4,5},{5,4},{6,7},{7,6},{8,9},{9,8},{10,11... | collective-permute-start | bytes 1769480 | tf_op jit(solution)/shard_map/ppermute | solution.py:258
  122.1 17.7 %collective-permute-start.14 = (bf16[2,2,96,768]{3,2,1,0:T(8,128)(2,1)S(1)}, bf16[2,2,96,768]{3,2,1,0:T(8,128)(2,1)S(1)}, u32[]{:S(2)}, u32[]{:S(2)}) collective-permute-start(bf16[2,2,96,768]{3,2,1,0:T(8,128)(2,1)S(1)} %get-tuple-element.255), channel_id=1, source_target_pairs={{0,8},{8,0},{1,9},{9,1},{2,10},{10,2},{3,11},{11,3},{4,12},{12,4},... | collective-permute-start | bytes 1769480 | tf_op jit(solution)/shard_map/ppermute | solution.py:258
  123.6 16.1 %collective-permute-start.15 = (bf16[2,2,96,768]{3,2,1,0:T(8,128)(2,1)S(1)}, bf16[2,2,96,768]{3,2,1,0:T(8,128)(2,1)S(1)}, u32[]{:S(2)}, u32[]{:S(2)}) collective-permute-start(bf16[2,2,96,768]{3,2,1,0:T(8,128)(2,1)S(1)} %get-tuple-element.256), channel_id=1, source_target_pairs={{0,16},{16,0},{1,17},{17,1},{2,18},{18,2},{3,19},{19,3},{4,20},{20... | collective-permute-start | bytes 1769480 | tf_op jit(solution)/shard_map/ppermute | solution.py:258
  142.3 10.9 %collective-permute-start.16 = (bf16[768,1536]{1,0:T(8,128)(2,1)}, bf16[768,1536]{1,0:T(8,128)(2,1)}, u32[]{:S(2)}, u32[]{:S(2)}) collective-permute-start(bf16[768,1536]{1,0:T(8,128)(2,1)} %pad_maximum_fusion.4), channel_id=1, source_target_pairs={{0,4},{4,0},{1,5},{5,1},{2,6},{6,2},{3,7},{7,3},{8,12},{12,8},{9,1... | collective-permute-start | bytes 7077896 | tf_op jit(solution)/shard_map/ppermute | solution.py:258
  152.6 12.8 %collective-permute-start.17 = (bf16[3072,384]{1,0:T(8,128)(2,1)S(1)}, bf16[3072,384]{1,0:T(8,128)(2,1)S(1)}, u32[]{:S(2)}, u32[]{:S(2)}) collective-permute-start(bf16[3072,384]{1,0:T(8,128)(2,1)S(1)} %convolution_convert_fusion), channel_id=1, source_target_pairs={{0,4},{4,0},{1,5},{5,1},{2,6},{6,2},{3,7},{7,3},{8,12},{12,8},{9,1... | collective-permute-start | bytes 7077896 | tf_op jit(solution)/shard_map/ppermute | solution.py:258
  183.5 26.4 %collective-permute-start.20 = (bf16[768,1536]{1,0:T(8,128)(2,1)}, bf16[768,1536]{1,0:T(8,128)(2,1)}, u32[]{:S(2)}, u32[]{:S(2)}) collective-permute-start(bf16[768,1536]{1,0:T(8,128)(2,1)} %convolution_convert_fusion.1), channel_id=1, source_target_pairs={{0,4},{4,0},{1,5},{5,1},{2,6},{6,2},{3,7},{7,3},{8,12},{12,8},{9,1... | collective-permute-start | bytes 7077896 | tf_op jit(solution)/shard_map/ppermute | solution.py:258
  186.6 20.0 %collective-permute-start.18 = (bf16[2,2,384,256]{3,2,1,0:T(8,128)(2,1)S(1)}, bf16[2,2,384,256]{3,2,1,0:T(8,128)(2,1)S(1)}, u32[]{:S(2)}, u32[]{:S(2)}) collective-permute-start(bf16[2,2,384,256]{3,2,1,0:T(8,128)(2,1)S(1)} %get-tuple-element.235), channel_id=1, source_target_pairs={{0,8},{8,0},{1,9},{9,1},{2,10},{10,2},{3,11},{11,3},{4,12},{12,4},... | collective-permute-start | bytes 2359304 | tf_op jit(solution)/shard_map/ppermute | solution.py:258
  187.3 13.5 %collective-permute-start.19 = (bf16[2,2,384,128]{3,2,1,0:T(8,128)(2,1)S(1)}, bf16[2,2,384,128]{3,2,1,0:T(8,128)(2,1)}, u32[]{:S(2)}, u32[]{:S(2)}) collective-permute-start(bf16[2,2,384,128]{3,2,1,0:T(8,128)(2,1)S(1)} %get-tuple-element.273), channel_id=1, source_target_pairs={{0,16},{16,0},{1,17},{17,1},{2,18},{18,2},{3,19},{19,3},{4,20},{20... | collective-permute-start | bytes 1179656 | tf_op jit(solution)/shard_map/ppermute | solution.py:258
  208.2 7.0 %collective-permute-start.21 = (bf16[768,384]{1,0:T(8,128)(2,1)S(1)}, bf16[768,384]{1,0:T(8,128)(2,1)S(1)}, u32[]{:S(2)}, u32[]{:S(2)}) collective-permute-start(bf16[768,384]{1,0:T(8,128)(2,1)S(1)} %convolution_convert_fusion.4), channel_id=1, source_target_pairs={{0,4},{4,0},{1,5},{5,1},{2,6},{6,2},{3,7},{7,3},{8,12},{12,8},{9,1... | collective-permute-start | bytes 1769480 | tf_op jit(solution)/shard_map/ppermute | solution.py:258
  208.4 25.5 %collective-permute-start.22 = (bf16[2,384,384]{2,1,0:T(8,128)(2,1)S(1)}, bf16[2,384,384]{2,1,0:T(8,128)(2,1)S(1)}, u32[]{:S(2)}, u32[]{:S(2)}) collective-permute-start(bf16[2,384,384]{2,1,0:T(8,128)(2,1)S(1)} %get-tuple-element.251), channel_id=1, source_target_pairs={{0,1},{1,0},{2,3},{3,2},{4,5},{5,4},{6,7},{7,6},{8,9},{9,8},{10,11... | collective-permute-start | bytes 1769480 | tf_op jit(solution)/shard_map/ppermute | solution.py:258
  217.1 17.8 %collective-permute-start.24 = (bf16[2,2,96,896]{3,2,1,0:T(8,128)(2,1)S(1)}, bf16[2,2,96,896]{3,2,1,0:T(8,128)(2,1)S(1)}, u32[]{:S(2)}, u32[]{:S(2)}) collective-permute-start(bf16[2,2,96,896]{3,2,1,0:T(8,128)(2,1)S(1)} %get-tuple-element.243), channel_id=1, source_target_pairs={{0,16},{16,0},{1,17},{17,1},{2,18},{18,2},{3,19},{19,3},{4,20},{20... | collective-permute-start | bytes 2064392 | tf_op jit(solution)/shard_map/ppermute | solution.py:258
  217.9 19.4 %collective-permute-start.23 = (bf16[2,2,96,1024]{3,2,1,0:T(8,128)(2,1)S(1)}, bf16[2,2,96,1024]{3,2,1,0:T(8,128)(2,1)S(1)}, u32[]{:S(2)}, u32[]{:S(2)}) collective-permute-start(bf16[2,2,96,1024]{3,2,1,0:T(8,128)(2,1)S(1)} %get-tuple-element.233), channel_id=1, source_target_pairs={{0,8},{8,0},{1,9},{9,1},{2,10},{10,2},{3,11},{11,3},{4,12},{12,4},... | collective-permute-start | bytes 2359304 | tf_op jit(solution)/shard_map/ppermute | solution.py:258
  251.5 14.4 %collective-permute-start.27 = (bf16[2,2,96,512]{3,2,1,0:T(8,128)(2,1)}, bf16[2,2,96,512]{3,2,1,0:T(8,128)(2,1)}, u32[]{:S(2)}, u32[]{:S(2)}) collective-permute-start(bf16[2,2,96,512]{3,2,1,0:T(8,128)(2,1)} %get-tuple-element.272), channel_id=1, source_target_pairs={{0,16},{16,0},{1,17},{17,1},{2,18},{18,2},{3,19},{19,3},{4,20},{20... | collective-permute-start | bytes 1179656 | tf_op jit(solution)/shard_map/ppermute | solution.py:258
  254.0 13.7 %collective-permute-start.26 = (bf16[2,2,96,640]{3,2,1,0:T(8,128)(2,1)}, bf16[2,2,96,640]{3,2,1,0:T(8,128)(2,1)}, u32[]{:S(2)}, u32[]{:S(2)}) collective-permute-start(bf16[2,2,96,640]{3,2,1,0:T(8,128)(2,1)} %get-tuple-element.263), channel_id=1, source_target_pairs={{0,8},{8,0},{1,9},{9,1},{2,10},{10,2},{3,11},{11,3},{4,12},{12,4},... | collective-permute-start | bytes 1474568 | tf_op jit(solution)/shard_map/ppermute | solution.py:258
  255.5 25.5 %collective-permute-start.29 = (bf16[2,96,1920]{2,1,0:T(8,128)(2,1)}, bf16[2,96,1920]{2,1,0:T(8,128)(2,1)}, u32[]{:S(2)}, u32[]{:S(2)}) collective-permute-start(bf16[2,96,1920]{2,1,0:T(8,128)(2,1)} %get-tuple-element.239), channel_id=1, source_target_pairs={{0,1},{1,0},{2,3},{3,2},{4,5},{5,4},{6,7},{7,6},{8,9},{9,8},{10,11... | collective-permute-start | bytes 2211848 | tf_op jit(solution)/shard_map/ppermute | solution.py:258
  264.8 19.2 %collective-permute-start.32 = (bf16[384,384]{1,0:T(8,128)(2,1)S(1)}, bf16[384,384]{1,0:T(8,128)(2,1)S(1)}, u32[]{:S(2)}, u32[]{:S(2)}) collective-permute-start(bf16[384,384]{1,0:T(8,128)(2,1)S(1)} %get-tuple-element.279), channel_id=1, source_target_pairs={{0,2},{2,0},{1,3},{3,1},{4,6},{6,4},{5,7},{7,5},{8,10},{10,8},{9,1... | collective-permute-start | bytes 884744 | tf_op jit(solution)/shard_map/ppermute | solution.py:258
  268.9 24.2 %collective-permute-start.30 = (bf16[2,96,1152]{2,1,0:T(8,128)(2,1)S(1)}, bf16[2,96,1152]{2,1,0:T(8,128)(2,1)S(1)}, u32[]{:S(2)}, u32[]{:S(2)}) collective-permute-start(bf16[2,96,1152]{2,1,0:T(8,128)(2,1)S(1)} %get-tuple-element.268), channel_id=1, source_target_pairs={{0,1},{1,0},{2,3},{3,2},{4,5},{5,4},{6,7},{7,6},{8,9},{9,8},{10,11... | collective-permute-start | bytes 1327112 | tf_op jit(solution)/shard_map/ppermute | solution.py:258
  282.3 4.2 %collective-permute-start.31 = (f32[12,768]{1,0:T(8,128)S(1)}, f32[12,768]{1,0:T(8,128)S(1)}, u32[]{:S(2)}, u32[]{:S(2)}) collective-permute-start(f32[12,768]{1,0:T(8,128)S(1)} %add.327), channel_id=1, source_target_pairs={{0,8},{8,0},{1,9},{9,1},{2,10},{10,2},{3,11},{11,3},{4,12},{12,4},... | collective-permute-start | bytes 110600 | tf_op jit(solution)/shard_map/ppermute | solution.py:258
  284.0 4.7 %collective-permute-start.34 = (bf16[384,128]{1,0:T(8,128)(2,1)S(1)}, bf16[384,128]{1,0:T(8,128)(2,1)S(1)}, u32[]{:S(2)}, u32[]{:S(2)}) collective-permute-start(bf16[384,128]{1,0:T(8,128)(2,1)S(1)} %slice.357), channel_id=1, source_target_pairs={{0,8},{8,0},{1,9},{9,1},{2,10},{10,2},{3,11},{11,3},{4,12},{12,4},... | collective-permute-start | bytes 294920 | tf_op jit(solution)/shard_map/ppermute | solution.py:258
  284.6 5.7 %collective-permute-start.33 = (bf16[384,256]{1,0:T(8,128)(2,1)S(1)}, bf16[384,256]{1,0:T(8,128)(2,1)S(1)}, u32[]{:S(2)}, u32[]{:S(2)}) collective-permute-start(bf16[384,256]{1,0:T(8,128)(2,1)S(1)} %slice.356), channel_id=1, source_target_pairs={{0,16},{16,0},{1,17},{17,1},{2,18},{18,2},{3,19},{19,3},{4,20},{20... | collective-permute-start | bytes 589832 | tf_op jit(solution)/shard_map/ppermute | solution.py:258
  285.2 20.6 %collective-permute-start.38 = (bf16[96,1920]{1,0:T(8,128)(2,1)S(1)}, bf16[96,1920]{1,0:T(8,128)(2,1)S(1)}, u32[]{:S(2)}, u32[]{:S(2)}) collective-permute-start(bf16[96,1920]{1,0:T(8,128)(2,1)S(1)} %get-tuple-element.275), channel_id=1, source_target_pairs={{0,2},{2,0},{1,3},{3,1},{4,6},{6,4},{5,7},{7,5},{8,10},{10,8},{9,1... | collective-permute-start | bytes 1105928 | tf_op jit(solution)/shard_map/ppermute | solution.py:258
  293.3 15.3 %collective-permute-start.35 = (f32[12,768]{1,0:T(8,128)S(1)}, f32[12,768]{1,0:T(8,128)S(1)}, u32[]{:S(2)}, u32[]{:S(2)}) collective-permute-start(f32[12,768]{1,0:T(8,128)S(1)} %add.330), channel_id=1, source_target_pairs={{0,16},{16,0},{1,17},{17,1},{2,18},{18,2},{3,19},{19,3},{4,20},{20... | collective-permute-start | bytes 110600 | tf_op jit(solution)/shard_map/ppermute | solution.py:258
  293.4 15.3 %collective-permute-start.37 = (bf16[384,128]{1,0:T(8,128)(2,1)S(1)}, bf16[384,128]{1,0:T(8,128)(2,1)S(1)}, u32[]{:S(2)}, u32[]{:S(2)}) collective-permute-start(bf16[384,128]{1,0:T(8,128)(2,1)S(1)} %add_convert_fusion.22), channel_id=1, source_target_pairs={{0,16},{16,0},{1,17},{17,1},{2,18},{18,2},{3,19},{19,3},{4,20},{20... | collective-permute-start | bytes 294920 | tf_op jit(solution)/shard_map/ppermute | solution.py:258
  306.0 9.0 %collective-permute-start.41 = (bf16[96,1152]{1,0:T(8,128)(2,1)S(1)}, bf16[96,1152]{1,0:T(8,128)(2,1)S(1)}, u32[]{:S(2)}, u32[]{:S(2)}) collective-permute-start(bf16[96,1152]{1,0:T(8,128)(2,1)S(1)} %get-tuple-element.286), channel_id=1, source_target_pairs={{0,2},{2,0},{1,3},{3,1},{4,6},{6,4},{5,7},{7,5},{8,10},{10,8},{9,1... | collective-permute-start | bytes 663560 | tf_op jit(solution)/shard_map/ppermute | solution.py:258
  306.1 8.7 %collective-permute-start.36 = (bf16[384,256]{1,0:T(8,128)(2,1)S(1)}, bf16[384,256]{1,0:T(8,128)(2,1)S(1)}, u32[]{:S(2)}, u32[]{:S(2)}) collective-permute-start(bf16[384,256]{1,0:T(8,128)(2,1)S(1)} %add_convert_fusion.18), channel_id=1, source_target_pairs={{0,8},{8,0},{1,9},{9,1},{2,10},{10,2},{3,11},{11,3},{4,12},{12,4},... | collective-permute-start | bytes 589832 | tf_op jit(solution)/shard_map/ppermute | solution.py:258
  307.1 7.8 %collective-permute-start.39 = (bf16[96,1024]{1,0:T(8,128)(2,1)S(1)}, bf16[96,1024]{1,0:T(8,128)(2,1)S(1)}, u32[]{:S(2)}, u32[]{:S(2)}) collective-permute-start(bf16[96,1024]{1,0:T(8,128)(2,1)S(1)} %slice.358), channel_id=1, source_target_pairs={{0,16},{16,0},{1,17},{17,1},{2,18},{18,2},{3,19},{19,3},{4,20},{20... | collective-permute-start | bytes 589832 | tf_op jit(solution)/shard_map/ppermute | solution.py:258
  308.6 6.1 %collective-permute-start.40 = (bf16[96,896]{1,0:T(8,128)(2,1)S(1)}, bf16[96,896]{1,0:T(8,128)(2,1)S(1)}, u32[]{:S(2)}, u32[]{:S(2)}) collective-permute-start(bf16[96,896]{1,0:T(8,128)(2,1)S(1)} %slice.359), channel_id=1, source_target_pairs={{0,8},{8,0},{1,9},{9,1},{2,10},{10,2},{3,11},{11,3},{4,12},{12,4},... | collective-permute-start | bytes 516104 | tf_op jit(solution)/shard_map/ppermute | solution.py:258
  315.1 7.1 %collective-permute-start.43 = (bf16[96,512]{1,0:T(8,128)(2,1)S(1)}, bf16[96,512]{1,0:T(8,128)(2,1)S(1)}, u32[]{:S(2)}, u32[]{:S(2)}) collective-permute-start(bf16[96,512]{1,0:T(8,128)(2,1)S(1)} %slice.361), channel_id=1, source_target_pairs={{0,8},{8,0},{1,9},{9,1},{2,10},{10,2},{3,11},{11,3},{4,12},{12,4},... | collective-permute-start | bytes 294920 | tf_op jit(solution)/shard_map/ppermute | solution.py:258
  316.1 6.0 %collective-permute-start.44 = (f32[12,768]{1,0:T(8,128)S(1)}, f32[12,768]{1,0:T(8,128)S(1)}, u32[]{:S(2)}, u32[]{:S(2)}) collective-permute-start(f32[12,768]{1,0:T(8,128)S(1)} %add.335), channel_id=1, source_target_pairs={{0,2},{2,0},{1,3},{3,1},{4,6},{6,4},{5,7},{7,5},{8,10},{10,8},{9,1... | collective-permute-start | bytes 110600 | tf_op jit(solution)/shard_map/ppermute | solution.py:258
  318.9 6.8 %collective-permute-start.46 = (bf16[96,896]{1,0:T(8,128)(2,1)S(1)}, bf16[96,896]{1,0:T(8,128)(2,1)S(1)}, u32[]{:S(2)}, u32[]{:S(2)}) collective-permute-start(bf16[96,896]{1,0:T(8,128)(2,1)S(1)} %add_convert_fusion.19), channel_id=1, source_target_pairs={{0,16},{16,0},{1,17},{17,1},{2,18},{18,2},{3,19},{19,3},{4,20},{20... | collective-permute-start | bytes 516104 | tf_op jit(solution)/shard_map/ppermute | solution.py:258
  320.4 5.7 %collective-permute-start.45 = (bf16[96,1024]{1,0:T(8,128)(2,1)S(1)}, bf16[96,1024]{1,0:T(8,128)(2,1)S(1)}, u32[]{:S(2)}, u32[]{:S(2)}) collective-permute-start(bf16[96,1024]{1,0:T(8,128)(2,1)S(1)} %add_convert_fusion.17), channel_id=1, source_target_pairs={{0,8},{8,0},{1,9},{9,1},{2,10},{10,2},{3,11},{11,3},{4,12},{12,4},... | collective-permute-start | bytes 589832 | tf_op jit(solution)/shard_map/ppermute | solution.py:258
  320.8 4.9 %collective-permute-start.42 = (bf16[96,640]{1,0:T(8,128)(2,1)S(1)}, bf16[96,640]{1,0:T(8,128)(2,1)S(1)}, u32[]{:S(2)}, u32[]{:S(2)}) collective-permute-start(bf16[96,640]{1,0:T(8,128)(2,1)S(1)} %slice.360), channel_id=1, source_target_pairs={{0,16},{16,0},{1,17},{17,1},{2,18},{18,2},{3,19},{19,3},{4,20},{20... | collective-permute-start | bytes 368648 | tf_op jit(solution)/shard_map/ppermute | solution.py:258
  327.9 6.9 %collective-permute-start.52 = (bf16[768,384]{1,0:T(8,128)(2,1)S(1)}, bf16[768,384]{1,0:T(8,128)(2,1)S(1)}, u32[]{:S(2)}, u32[]{:S(2)}) collective-permute-start(bf16[768,384]{1,0:T(8,128)(2,1)S(1)} %pad_maximum_fusion.25), channel_id=1, source_target_pairs={{0,4},{4,0},{1,5},{5,1},{2,6},{6,2},{3,7},{7,3},{8,12},{12,8},{9,1... | collective-permute-start | bytes 1769480 | tf_op jit(solution)/shard_map/ppermute | solution.py:258
  327.9 5.2 %collective-permute-start.48 = (bf16[96,512]{1,0:T(8,128)(2,1)S(1)}, bf16[96,512]{1,0:T(8,128)(2,1)S(1)}, u32[]{:S(2)}, u32[]{:S(2)}) collective-permute-start(bf16[96,512]{1,0:T(8,128)(2,1)S(1)} %add_convert_fusion.21), channel_id=1, source_target_pairs={{0,16},{16,0},{1,17},{17,1},{2,18},{18,2},{3,19},{19,3},{4,20},{20... | collective-permute-start | bytes 294920 | tf_op jit(solution)/shard_map/ppermute | solution.py:258
  329.1 5.5 %collective-permute-start.47 = (bf16[96,640]{1,0:T(8,128)(2,1)S(1)}, bf16[96,640]{1,0:T(8,128)(2,1)S(1)}, u32[]{:S(2)}, u32[]{:S(2)}) collective-permute-start(bf16[96,640]{1,0:T(8,128)(2,1)S(1)} %add_convert_fusion.20), channel_id=1, source_target_pairs={{0,8},{8,0},{1,9},{9,1},{2,10},{10,2},{3,11},{11,3},{4,12},{12,4},... | collective-permute-start | bytes 368648 | tf_op jit(solution)/shard_map/ppermute | solution.py:258
  330.1 7.9 %collective-permute-start.51 = (bf16[192,1920]{1,0:T(8,128)(2,1)S(1)}, bf16[192,1920]{1,0:T(8,128)(2,1)S(1)}, u32[]{:S(2)}, u32[]{:S(2)}) collective-permute-start(bf16[192,1920]{1,0:T(8,128)(2,1)S(1)} %pad_maximum_fusion.22), channel_id=1, source_target_pairs={{0,4},{4,0},{1,5},{5,1},{2,6},{6,2},{3,7},{7,3},{8,12},{12,8},{9,1... | collective-permute-start | bytes 2211848 | tf_op jit(solution)/shard_map/ppermute | solution.py:258
  (55 other events, 297.4 us)

commit v3 on v2

--- a/solution.py
+++ b/solution.py
@@ -108,6 +108,10 @@
             sums_ref[:, spots[part]] += jnp.sum(value.astype(f32), axis=0, keepdims=True)
 
 
+def stay(value):
+    return pltpu.with_memory_space_constraint(value, pltpu.HBM)
+
+
 def attention(qkv, length):
     slots, rows, wide = qkv.shape
     width = wide // 3
@@ -151,7 +155,7 @@
         compiler_params=pltpu.CompilerParams(vmem_limit_bytes=28 * 2**20),
         cost_estimate=FREE,
         name="attention_back",
-    )(qkv, probs, grad)
+    )(qkv, stay(probs), grad)
 
 
 def hidden_back_kernel(grad_ref, weight_ref, slope_ref, out_ref, sums_ref):
@@ -178,7 +182,7 @@
             pl.BlockSpec((1, tile), lambda i: (0, i)),
         ],
         out_shape=[
-            jax.ShapeDtypeStruct((rows, wide), bf16),
+            pltpu.HBM((rows, wide), bf16),
             jax.ShapeDtypeStruct((1, wide), f32),
         ],
         compiler_params=pltpu.CompilerParams(vmem_limit_bytes=28 * 2**20),
@@ -240,7 +244,7 @@
         compiler_params=pltpu.CompilerParams(vmem_limit_bytes=28 * 2**20),
         cost_estimate=FREE,
         name="matmul_norm_back",
-    )(grad, weight, values, gain.reshape(1, width), past)
+    )(*map(stay if both else (lambda v: v), (grad, weight, values)), gain.reshape(1, width), past)
 
 
 class Net:
@@ -368,27 +372,28 @@
     q_way = net.grow(fetch(net.core_half(w_qkv)), far, 0)
     small = net.grow(small, far, 0)
     mid_way = fetch(jnp.concatenate([net.core_half(w_up), net.core_half(w_proj)], axis=1))
-    q_way, small, mid_way = together(q_way, small, mid_way)
+    q_way, small = together(q_way, small)
     q_way = net.grow(q_way, near, 1)
     small = net.grow(small, near, 1)
-    mid_got = net.swap(mid_way, far)
     down_mine = net.core_half(w_down).reshape(blocks, part, half_mid)
     down_mine = jnp.concatenate([down_mine[i] for i in range(blocks)], axis=1)
     q_way, small, mid_way, down_mine, tokens = together(
         q_way, small, mid_way, down_mine, tokens
     )
     q_got = send_plane(q_way)
-    mid_way = net.join(mid_way, mid_got, far, 0)
+    mid_got = net.swap(mid_way, far)
     small = small.astype(f32).reshape(group, -1, part)
     rows = small[:, :8].transpose(1, 0, 2).reshape(8, width)
     query_bias, value_bias, proj_bias, gain_1, bias_1, gain_2, bias_2, down_bias = (
         rows[i] for i in range(8)
     )
     up_bias = small[:, 8:].reshape(wide)
-    mid_way, down_way = together(mid_way, fetch(down_mine))
+    q_way, *q_got = together(q_way, *q_got)
+    q_way, mid_way, down_way = together(join_plane(q_way, q_got, 2), mid_way, fetch(down_mine))
+    qkv_pair = net.both_cores(q_way)
+    mid_way = net.join(mid_way, mid_got, far, 0)
     mid_got = net.swap(mid_way, near)
-    q_way, down_way = together(join_plane(q_way, q_got, 2), down_way)
-    qkv_full = jnp.concatenate(net.both_cores(q_way), axis=1)
+    (qkv_full,) = together(jnp.concatenate(qkv_pair, axis=1))
 
     live_slots = (jnp.arange(slot_count, dtype=jnp.int32) < counts[0]).astype(f32)
     live_rows = jnp.repeat(live_slots, padded)[:, None]
@@ -399,16 +404,17 @@
     qkv_bias = jnp.concatenate([query_bias, jnp.zeros_like(query_bias), value_bias])
     joined = (dot_nn(normed_one, qkv_full) + qkv_bias).astype(bf16)
     joined = joined.reshape(slot_count, padded, 3 * width)
-    joined, mid_way = together(joined, mid_way)
+    mixed, probs = attention(joined, length)
+    mixed, mid_way, mid_got, down_way = together(mixed, mid_way, mid_got, down_way)
     mid_way = net.join(mid_way, mid_got, near, 1)
-    joined, mid_way, down_way = together(joined, mid_way, down_way)
+    mixed, mid_way, down_way = together(mixed, mid_way, down_way)
     mid_got = send_plane(mid_way)
     down_got = net.swap(down_way, far)
-    mixed, probs = attention(joined, length)
-    mixed, mid_way, down_way, out_grad = together(mixed, mid_way, down_way, out_grad)
-    mid_way = join_plane(mid_way, mid_got, 2)
+    mixed, mid_way, down_way, out_grad, down_got, *mid_got = together(
+        mixed, mid_way, down_way, out_grad, down_got, *mid_got
+    )
     down_way = net.join(down_way, down_got, far, 0)
-    mixed, mid_way, down_way = together(mixed, mid_way, down_way)
+    mid_way, down_way = together(join_plane(mid_way, mid_got, 2), down_way)
     down_got = net.swap(down_way, near)
     *mid_pairs, down_way = together(*net.both_cores(mid_way), down_way)
     down_way = net.join(down_way, down_got, near, 1)
@@ -417,6 +423,7 @@
     mid = mid_pairs
     up_full = jnp.concatenate([m[:, :half_up] for m in mid], axis=1)
     proj_full = jnp.concatenate([m[:, half_up:] for m in mid], axis=1)
+    up_full, proj_full = together(up_full, proj_full)
     middle = inputs + (dot_nn(mixed, proj_full) + proj_bias)
     normal_two, inverse_two = norm_parts(middle)
     normed_two = (normal_two * gain_2 + bias_2).astype(bf16)
@@ -436,7 +443,7 @@
         )
         for d in down_pairs
     ]
-    down_full = jnp.concatenate(down, axis=3).reshape(wide, width)
+    (down_full,) = together(jnp.concatenate(down, axis=3).reshape(wide, width))
 
     def start_sum(left, right):
         return dot_tn(left, net.core_half(right, True)).astype(bf16)
@@ -481,38 +488,46 @@
     branch_3, layer_out = together(grad_branch, layer_out)
     d_piece = own_sum(active, branch_3, d_other)
     branch_2, d_piece = together(branch_2, d_piece)
-    d_keeps, d_others = part_plane(d_piece)
+    fine = d_piece.shape[3] // 2
+    d_pairs = [
+        net.part_with(d_piece[:, :, :, i * fine : (i + 1) * fine], name, 2)
+        for i, name in enumerate(plane)
+    ]
+    d_keeps, d_others = [p[0] for p in d_pairs], [p[1] for p in d_pairs]
     grad_hidden, up_sums = hidden_back(branch_2, down_full, slope)
     grad_hidden, u_send = together(grad_hidden, start_sum(normed_two, grad_hidden))
     u_other = net.swap(u_send, net.core)
     grad_middle, grad_attn, mid_sums = matmul_norm_back(
         grad_hidden, up_full, middle, gain_2, grad_branch, slot_count, True
     )
-    grad_attn, *d_keeps = together(grad_attn, *d_keeps)
-    d_piece = add_plane(d_keeps, d_others)
-    grad_hidden, grad_attn, d_piece = together(grad_hidden, grad_attn, d_piece)
-    d_pair = net.part_with(d_piece, near, 1)
+    grad_attn, d_1, d_2, o_1, o_2 = together(grad_attn, *d_keeps, *d_others)
+    grad_hidden, grad_attn = together(grad_hidden, grad_attn)
     grad_attn, p_send = together(grad_attn, start_sum(mixed, grad_attn))
     p_other = net.swap(p_send, net.core)
     u_piece = own_sum(normed_two, grad_hidden, u_other)
     grad_attn, u_piece = together(grad_attn, u_piece)
     p_piece = own_sum(mixed, grad_attn, p_other)
-    grad_attn_2, u_piece = together(grad_attn, jnp.concatenate([u_piece, p_piece], axis=-1))
+    u_piece = jnp.concatenate([u_piece, p_piece], axis=-1)
+    grad_attn_2, u_piece, d_1, d_2, o_1, o_2 = together(grad_attn, u_piece, d_1, d_2, o_1, o_2)
+    d_piece = add_plane([d_1, d_2], [o_1, o_2])
+    d_pair = net.part_with(d_piece, near, 1)
     u_keeps, u_others = part_plane(u_piece)
     grad_mixed = dot_nt(grad_attn_2, proj_full).astype(bf16)
     grad_joined, joined_sums = attention_back(
         joined, probs, grad_mixed.reshape(slot_count, padded, width)
     )
-    grad_joined, d_keep, *u_keeps = together(
-        grad_joined.reshape(row_count, 3 * width), d_pair[0], *u_keeps
-    )
-    d_piece = add((d_keep, d_pair[1]))
-    u_piece = add_plane(u_keeps, u_others)
+    grad_joined, d_keep, d_other, u_1, u_2, o_1, o_2 = together(
+        grad_joined.reshape(row_count, 3 * width), *d_pair, *u_keeps, *u_others
+    )
+    grad_joined, q_send, d_keep, d_other, u_1, u_2, o_1, o_2 = together(
+        grad_joined, start_sum(normed_one, grad_joined), d_keep, d_other, u_1, u_2, o_1, o_2
+    )
+    q_other = net.swap(q_send, net.core)
+    u_piece = add_plane([u_1, u_2], [o_1, o_2])
+    d_piece = add((d_keep, d_other))
     grad_joined, d_piece, u_piece = together(grad_joined, d_piece, u_piece)
+    u_pair = net.part_with(u_piece, near, 1)
     d_pair = net.part_with(d_piece, far, 0)
-    u_pair = net.part_with(u_piece, near, 1)
-    grad_joined, q_send = together(grad_joined, start_sum(normed_one, grad_joined))
-    q_other = net.swap(q_send, net.core)
     q_piece = own_sum(normed_one, grad_joined, q_other)
     grad_joined, q_piece = together(grad_joined, q_piece)
     q_keeps, q_others = part_plane(q_piece)
@@ -532,37 +547,43 @@
     vectors += [up_sums[:, k * width : (k + 1) * width] for k in range(group)]
     vectors = jnp.concatenate(vectors, axis=0)
 
-    vectors, u_keep, *q_keeps = together(vectors, u_pair[0], *q_keeps)
+    vectors, u_keep, u_other, d_keep, d_other, q_1, q_2, o_1, o_2 = together(
+        vectors, *u_pair, *d_pair, *q_keeps, *q_others
+    )
+    q_piece = add_plane([q_1, q_2], [o_1, o_2])
+    u_piece = add((u_keep, u_other))
+    q_piece, u_piece, vectors, d_keep = together(q_piece, u_piece, vectors, d_keep)
+    q_pair = net.part_with(q_piece, near, 1)
+    u_pair = net.part_with(u_piece, far, 0)
     sums = vectors + net.swap(vectors, net.core)
-    q_piece = add_plane(q_keeps, q_others)
-    q_piece, u_keep, d_keep, sums = together(q_piece, u_keep, d_pair[0], sums)
-    q_pair = net.part_with(q_piece, near, 1)
-    u_piece = add((u_keep, u_pair[1]))
-    u_piece, d_keep, sums, q_keep = together(u_piece, d_keep, sums, q_pair[0])
-    u_pair = net.part_with(u_piece, far, 0)
-    d_piece = exchange_plane(add((d_keep, d_pair[1])))
+    d_piece = exchange_plane(add((d_keep, d_other)))
+    q_keep, q_other, u_keep, u_other, sums, *d_piece = together(*q_pair, *u_pair, sums, *d_piece)
+    q_piece = add((q_keep, q_other))
+    u_piece = add((u_keep, u_other))
+    q_piece, u_piece, sums, *d_piece = together(q_piece, u_piece, sums, *d_piece)
+    q_pair = net.part_with(q_piece, far, 0)
+    u_piece = exchange_plane(u_piece)
+    down_shard = jnp.stack(
+        [net.grow(p, name, 0) for p, name in zip(d_piece, plane)], axis=1
+    ).reshape(-1, half_mid)
     sums = sums + net.swap(sums, net.x)
-    q_piece = add((q_keep, q_pair[1]))
-    q_piece, u_keep, sums, *d_piece = together(q_piece, u_pair[0], sums, *d_piece)
-    q_pair = net.part_with(q_piece, far, 0)
-    down_shard = grow_plane(d_piece)
-    sums = sums + net.swap(sums, net.y)
-    u_piece = exchange_plane(add((u_keep, u_pair[1])))
-    q_keep, sums, down_shard, *u_piece = together(q_pair[0], sums, down_shard, *u_piece)
-    q_piece = add((q_keep, q_pair[1]))
+    q_keep, q_other, sums, down_shard, *u_piece = together(*q_pair, sums, down_shard, *u_piece)
+    q_1, q_2 = exchange_plane(add((q_keep, q_other)))
     up_shard = grow_plane(u_piece)
     down_pair = net.both_cores(down_shard)
+    sums = sums + net.swap(sums, net.y)
+    grad_down_w = jnp.concatenate(down_pair, axis=1).astype(f32)
+    q_1, q_2, sums, up_shard, grad_down_w = together(q_1, q_2, sums, up_shard, grad_down_w)
+    q_piece = grow_plane([q_1, q_2])
+    up_pair = net.both_cores(up_shard)
     sums = sums + net.swap(sums, far)
-    q_1, q_2 = exchange_plane(q_piece)
-    q_1, q_2, sums, up_shard = together(q_1, q_2, sums, up_shard)
-    up_pair = net.both_cores(up_shard)
-    q_pair = net.both_cores(grow_plane([q_1, q_2]))
+    q_piece, sums, *up_pair = together(q_piece, sums, *up_pair)
+    q_pair = net.both_cores(q_piece)
     for name in (near,) + net.extra:
         sums = sums + net.swap(sums, name)
     me = net.place_in_group()
     owned = lax.dynamic_slice_in_dim(sums[:8], me * part, part, 1)
     owned_up = lax.dynamic_index_in_dim(sums, 8 + me, 0, keepdims=False)
-    grad_down_w = jnp.concatenate(down_pair, axis=1).astype(f32)
     grad_up_w = jnp.concatenate([p[:, :half_up] for p in up_pair], axis=1).astype(f32)
     grad_proj_w = jnp.concatenate([p[:, half_up:] for p in up_pair], axis=1).astype(f32)
     grad_qkv_w = jnp.concatenate(q_pair, axis=1).astype(f32)

time: 346 us -> 339 us (0.980)
  waiting for transfers between devices: 108 us -> 79.8 us
  starting transfers between devices: 46.8 us -> 53.3 us
  Pallas kernels: 47.8 us -> 53.7 us
  local copies, waits for them, and re-layouts: 36.6 us -> 40.7 us
    ppermute x53, waiting for transfers between devices: 108 us -> 79.8 us  [swap(): return lax.ppermute(piece, name, SWAP)]
    ppermute x53, starting transfers between devices: 46.8 us -> 53.3 us  [swap(): return lax.ppermute(piece, name, SWAP)]
    squeeze x9 -> x11, local copies, waits for them, and re-layouts: 2.59 us -> 8.1 us  [part_with(): send = lax.dynamic_index_in_dim(piece, 1 - bit, spot, keepdims=False)]
    pallas_call x2, Pallas kernels: 19 us -> 22.6 us  [matmul_norm_back(): pl.pallas_call(norm_back_kernel if both else norm_back_low_kernel, grid=(...]
    convert_element_type x18 -> x17, other arithmetic: 7.44 us -> 9.83 us  [add(): return (pair[0].astype(f32) + pair[1].astype(f32)).astype(bf16)]
    unnamed x98 -> x86, local copies, waits for them, and re-layouts: 9.71 us -> 8.33 us
  transfers between devices with their start and end apart: 53 -> 53, of which waited for: 29 -> 30; matrix products, arithmetic and copies ran while one was open for 28% -> 30% of each run, Pallas kernels for 12% -> 14%
where the time goes in v3:
time: 339 us; the launch traced here: 334 us
  waiting for transfers between devices  79.8 us (24%)
  matrix products  62.5 us (18%)
  Pallas kernels  53.7 us (16%)
  starting transfers between devices  53.3 us (16%)
  other arithmetic  41 us (12%)
  local copies, waits for them, and re-layouts  40.7 us (12%)
    ppermute x53, waiting for transfers between devices, swap(): return lax.ppermute(piece, name, SWAP)  79.8 us
    ppermute x53, starting transfers between devices, swap(): return lax.ppermute(piece, name, SWAP)  53.3 us
    dot_general x8, matrix products, dot_tn(): lax.dot_general(a, b, (((0,), (0,)), ((), ())), preferred_element_type=f32)  35.7 us
    dot_general x4, matrix products, dot_nn(): return jnp.dot(a, b, preferred_element_type=f32)  23.4 us
    pallas_call x2, Pallas kernels, matmul_norm_back(): pl.pallas_call(norm_back_kernel if both else norm_back_low_kernel, grid=(...  22.6 us
    pallas_call x1, Pallas kernels, attention_back(): pl.pallas_call(attention_back_kernel, grid=(slots,), in_specs=[pl.BlockSp...  14.5 us
    convert_element_type x17, other arithmetic, add(): return (pair[0].astype(f32) + pair[1].astype(f32)).astype(bf16)  9.83 us
    select_n x6, other arithmetic, place(): return (jnp.where(bit == 0, mine, other), jnp.where(bit == 0, other, mine))  8.64 us
  transfers between devices with their start and end apart: 53, of which 30 were waited for; matrix products, arithmetic and copies ran while one was open for 30% of the time, Pallas kernels for 14%

profile of v3, /device:TPU:0, one launch (start us, length us, event | category | flops | bytes accessed | tf_op | source)
XLA Modules:
  0.0 334.0 jit_solution(15478359395772120570)
XLA Ops:
  2.6 4.1 %collective-permute-start = (bf16[96,1152]{1,0:T(8,128)(2,1)S(1)}, bf16[96,1152]{1,0:T(8,128)(2,1)S(1)}, u32[]{:S(2)}, u32[]{:S(2)}) collective-permute-start(bf16[96,1152]{1,0:T(8,128)(2,1)S(1)} %pad_maximum_fusion.30), channel_id=1, source_target_pairs={{0,2},{2,0},{1,3},{3,1},{4,6},{6,4},{5,7},{7,5},{8,10},{10,8},{9,1... | collective-permute-start | bytes 663560 | tf_op jit(solution)/shard_map/ppermute | solution.py:262
  15.1 2.3 collective-permute-done.1
  17.6 1.6 collective-permute-start.2
  19.7 9.3 %collective-permute-done.3 = bf16[2,12,192]{2,1,0:T(8,128)(2,1)S(1)} collective-permute-done((bf16[2,12,192]{2,1,0:T(8,128)(2,1)S(1)}, bf16[2,12,192]{2,1,0:T(8,128)(2,1)S(1)}, u32[]{:S(2)}, u32[]{:S(2)}) %collective-permute-start.3) | collective-permute-done | bytes 9248 | tf_op jit(solution)/shard_map/ppermute | solution.py:262
  34.3 3.4 %collective-permute-start.7 = (bf16[96,1920]{1,0:T(8,128)(2,1)S(1)}, bf16[96,1920]{1,0:T(8,128)(2,1)}, u32[]{:S(2)}, u32[]{:S(2)}) collective-permute-start(bf16[96,1920]{1,0:T(8,128)(2,1)S(1)} %pad_maximum_fusion.26), channel_id=1, source_target_pairs={{0,2},{2,0},{1,3},{3,1},{4,6},{6,4},{5,7},{7,5},{8,10},{10,8},{9,1... | collective-permute-start | bytes 1105928 | tf_op jit(solution)/shard_map/ppermute | solution.py:262
  38.4 3.2 collective-permute-done.5
  47.2 6.2 %collective-permute-done.7 = bf16[96,1920]{1,0:T(8,128)(2,1)} collective-permute-done((bf16[96,1920]{1,0:T(8,128)(2,1)S(1)}, bf16[96,1920]{1,0:T(8,128)(2,1)}, u32[]{:S(2)}, u32[]{:S(2)}) %collective-permute-start.7) | collective-permute-done | bytes 368672 | tf_op jit(solution)/shard_map/ppermute | solution.py:262
  55.3 2.3 broadcast_select_fusion.5
  57.9 4.7 %fusion.5 = bf16[1040,2304]{1,0:T(8,128)(2,1)S(1)} fusion(bf16[1040,768]{1,0:T(8,128)(2,1)S(1)} %fusion.12, bf16[768,2304]{1,0:T(8,128)(2,1)S(1)} %pad_maximum_fusion.1.weight_ref, f32[2304]{0:T(1024)S(1)} %pad_maximum_fusion.34), kind=kOutput, calls=%fused_computation.10 | convolution fusion | flops 3685294080 | bytes 9937920 | tf_op jit(solution)/shard_map/dot_general | solution.py:44
  62.6 8.4 %attention.1 = (bf16[5,208,768]{2,1,0:T(8,128)(2,1)S(1)}, bf16[5,12,208,208]{3,2,1,0:T(8,128)(2,1)}) custom-call(bf16[5,208,2304]{2,1,0:T(8,128)(2,1)S(1)} %bitcast.226), custom_call_target="tpu_custom_call" | custom-call | tf_op jit(solution)/shard_map/attention/pallas_call | solution.py:118
  73.8 3.2 collective-permute-start.9
  77.0 12.6 %collective-permute-done.9 = bf16[96,1536]{1,0:T(8,128)(2,1)S(1)} collective-permute-done((bf16[96,1536]{1,0:T(8,128)(2,1)S(1)}, bf16[96,1536]{1,0:T(8,128)(2,1)S(1)}, u32[]{:S(2)}, u32[]{:S(2)}) %collective-permute-start.9) | collective-permute-done | bytes 294944 | tf_op jit(solution)/shard_map/ppermute | solution.py:262
  89.7 1.7 collective-permute-done.10
  92.3 1.8 pad_maximum_fusion.2
  95.9 4.1 %collective-permute-done.12 = bf16[768,1920]{1,0:T(8,128)(2,1)} collective-permute-done((bf16[768,1920]{1,0:T(8,128)(2,1)}, bf16[768,1920]{1,0:T(8,128)(2,1)}, u32[]{:S(2)}, u32[]{:S(2)}) %collective-permute-start.12) | collective-permute-done | bytes 2949152 | tf_op jit(solution)/shard_map/ppermute | solution.py:262
  100.0 3.3 broadcast_select_fusion
  104.6 2.4 copy-done.11
  107.0 1.6 fusion.57
  112.4 11.8 %fusion.4 = (bf16[1040,3072]{1,0:T(8,128)(2,1)}, bf16[1040,3072]{1,0:T(8,128)(2,1)}) fusion(f32[3072]{0:T(1024)S(1)} %add.295, bf16[1040,768]{1,0:T(8,128)(2,1)S(1)} %add_convert_fusion.3, bf16[768,3072]{1,0:T(8,128)(2,1)S(1)} %pad_maximum_fusion.weight_ref), kind=kOutput, calls=%fused_computation.7 | convolution fusion | flops 4945674240 | bytes 19107840 | tf_op jit(solution)/shard_map/dot_general | solution.py:44
  126.3 1.7 pad_maximum_fusion.4
  130.8 7.6 %convolution_convert_fusion = bf16[3072,384]{1,0:T(8,128)(2,1)S(1)} fusion(bf16[1040,3072]{1,0:T(8,128)(2,1)} %get-tuple-element.182, bf16[1040,768]{1,0:T(8,128)(2,1)S(1)} %bitcast_multiply_fusion.grad_ref.past_ref, s32[]{:T(128)S(6)} %select_n.456), kind=kOutput, calls=%fused_computation.15 | convolution fusion | flops 2454847488 | bytes 9547780 | tf_op jit(solution)/shard_map/dot_general | solution.py:40
  138.9 2.7 broadcast_select_fusion.3
  144.7 5.2 %fusion.8 = bf16[1040,768]{1,0:T(8,128)(2,1)S(1)} fusion(f32[1040,768]{1,0:T(8,128)S(1)} %copy-done.15, bf16[1040,3072]{1,0:T(8,128)(2,1)S(1)} %bitcast.277, bf16[3072,768]{1,0:T(8,128)(2,1)S(1)} %bitcast.230, f32[1040]{0:T(1024)S(1)} %broadcast_in_dim_reshape.4, f32[768]{0:T(1024)S(1)} %add.300), kind=kOutput, calls=%fused_computation.26 | convolution fusion | flops 4910530560 | bytes 15907904 | tf_op jit(solution)/shard_map/dot_general | solution.py:44
  151.1 5.7 %add_convert_fusion.1 = bf16[3072,384]{1,0:T(8,128)(2,1)} fusion(bf16[3072,384]{1,0:T(8,128)(2,1)S(1)} %collective-permute-done.17, bf16[1040,3072]{1,0:T(8,128)(2,1)S(1)} %bitcast.277, bf16[1040,768]{1,0:T(8,128)(2,1)S(1)} %bitcast_multiply_fusion.grad_ref.past_ref, s32[]{:T(128)S(6)} %select_n.416), kind=kOutput, calls=%fused_computation.14 | convolution fusion | flops 2457206784 | bytes 11907076 | tf_op jit(solution)/shard_map/dot_general | solution.py:40
  156.9 8.3 %hidden_back.1 = (bf16[1040,3072]{1,0:T(8,128)(2,1)}, f32[1,3072]{1,0:T(1,128)S(1)}) custom-call(bf16[1040,768]{1,0:T(8,128)(2,1)S(1)} %bitcast_multiply_fusion.grad_ref.past_ref, bf16[3072,768]{1,0:T(8,128)(2,1)S(1)} %bitcast.231, bf16[1040,3072]{1,0:T(8,128)(2,1)S(1)} %bitcast.235), custom_call_target="tpu_custom_call" | custom-call | tf_op jit(solution)/shard_map/hidden_back/pallas_call | solution.py:172
  165.1 6.4 %convolution_convert_fusion.1 = bf16[768,1536]{1,0:T(8,128)(2,1)} fusion(bf16[1040,768]{1,0:T(8,128)(2,1)S(1)} %copy-done.26, bf16[1040,3072]{1,0:T(8,128)(2,1)} %get-tuple-element.197.grad_ref, s32[]{:T(128)S(6)} %select_n.457), kind=kOutput, calls=%fused_computation.27 | convolution fusion | flops 2454847488 | bytes 7151620 | tf_op jit(solution)/shard_map/dot_general | solution.py:40
  171.5 1.9 fusion.50
  179.0 13.8 %matmul_norm_back.2 = (f32[1040,768]{1,0:T(8,128)S(1)}, bf16[1040,768]{1,0:T(8,128)(2,1)S(1)}, f32[8,768]{1,0:T(8,128)S(1)}) custom-call(bf16[1040,3072]{1,0:T(8,128)(2,1)} %get-tuple-element.197.grad_ref, bf16[768,3072]{1,0:T(8,128)(2,1)} %copy-done.16, f32[1040,768]{1,0:T(8,128)} %copy-done.14, f32[1,768]{1,0:T(1,128)S(1)} %slice.301.gain_ref, ...), custom_call_target="tpu_custom_call" | custom-call | tf_op jit(solution)/shard_map/matmul_norm_back/pallas_call | solution.py:232
  195.6 5.7 %add_convert_fusion = bf16[768,1536]{1,0:T(8,128)(2,1)S(1)} fusion(bf16[768,1536]{1,0:T(8,128)(2,1)} %collective-permute-done.20, bf16[1040,768]{1,0:T(8,128)(2,1)S(1)} %copy-done.27, bf16[1040,3072]{1,0:T(8,128)(2,1)} %get-tuple-element.197.grad_ref, s32[]{:T(128)} %select_n.415), kind=kOutput, calls=%fused_computation.13 | convolution fusion | flops 2457206784 | bytes 9511424 | tf_op jit(solution)/shard_map/dot_general | solution.py:40
  210.2 3.3 %convolution_convert_fusion.3 = bf16[1040,768]{1,0:T(8,128)(2,1)S(1)} fusion(bf16[1040,768]{1,0:T(8,128)(2,1)} %copy-done.13, bf16[768,768]{1,0:T(8,128)(2,1)} %copy-done.28), kind=kOutput, calls=%fused_computation.29 | convolution fusion | flops 1227632640 | bytes 4374528 | tf_op jit(solution)/shard_map/dot_general | solution.py:36
  213.6 14.5 %attention_back.1 = (bf16[5,208,2304]{2,1,0:T(8,128)(2,1)S(1)}, f32[1,2304]{1,0:T(1,128)S(1)}) custom-call(bf16[5,208,2304]{2,1,0:T(8,128)(2,1)S(1)} %bitcast.229, bf16[5,12,208,208]{3,2,1,0:T(8,128)(2,1)} %get-tuple-element.185.prob_ref, bf16[5,208,768]{2,1,0:T(8,128)(2,1)S(1)} %bitcast.241), custom_call_target="tpu_custom_call" | custom-call | tf_op jit(solution)/shard_map/attention_back/pallas_call | solution.py:139
  228.1 3.8 %convolution_convert_fusion.2 = bf16[768,1152]{1,0:T(8,128)(2,1)} fusion(bf16[1040,768]{1,0:T(8,128)(2,1)S(1)} %copy-done.23, bf16[1040,2304]{1,0:T(8,128)(2,1)S(1)} %bitcast.236, s32[]{:T(128)S(6)} %select_n.464), kind=kOutput, calls=%fused_computation.28 | convolution fusion | flops 1841135616 | bytes 5763076 | tf_op jit(solution)/shard_map/dot_general | solution.py:40
  232.1 1.9 convert_reduce_fusion.1
  233.9 1.6 add_convert_fusion.6
  241.1 3.5 %collective-permute-start.27 = (bf16[192,768]{1,0:T(8,128)(2,1)}, bf16[192,768]{1,0:T(8,128)(2,1)}, u32[]{:S(2)}, u32[]{:S(2)}) collective-permute-start(bf16[192,768]{1,0:T(8,128)(2,1)} %get-tuple-element.351), channel_id=1, source_target_pairs={{0,2},{2,0},{1,3},{3,1},{4,6},{6,4},{5,7},{7,5},{8,10},{10,8},{9,1... | collective-permute-start | bytes 884744 | tf_op jit(solution)/shard_map/ppermute | solution.py:262
  244.7 4.1 %add_convert_fusion.2 = bf16[768,1152]{1,0:T(8,128)(2,1)S(1)} fusion(bf16[768,1152]{1,0:T(8,128)(2,1)} %collective-permute-done.25, bf16[1040,768]{1,0:T(8,128)(2,1)S(1)} %copy-done.24, bf16[1040,2304]{1,0:T(8,128)(2,1)S(1)} %bitcast.239, s32[]{:T(128)S(6)} %select_n.402), kind=kOutput, calls=%fused_computation.25 | convolution fusion | flops 1842905088 | bytes 7532548 | tf_op jit(solution)/shard_map/dot_general | solution.py:40
  252.7 8.7 %matmul_norm_back.3 = (bf16[1040,768]{1,0:T(8,128)(2,1)S(1)}, f32[8,768]{1,0:T(8,128)S(1)}) custom-call(bf16[1040,2304]{1,0:T(8,128)(2,1)S(1)} %bitcast.240, bf16[768,2304]{1,0:T(8,128)(2,1)S(1)} %copy-done.4, bf16[1040,768]{1,0:T(8,128)(2,1)S(1)} %bitcast.233, f32[1,768]{1,0:T(1,128)S(1)} %slice.306.gain_ref, f32[1040,768]{1,0:T(8,128)S(1)} %copy-done.7), custom_call_target="tpu_custom_call" | custom-call | tf_op jit(solution)/shard_map/matmul_norm_back/pallas_call | solution.py:232
  263.3 1.7 collective-permute-done.26
  268.8 3.6 %collective-permute-start.30 = (bf16[2,96,1152]{2,1,0:T(8,128)(2,1)S(1)}, bf16[2,96,1152]{2,1,0:T(8,128)(2,1)S(1)}, u32[]{:S(2)}, u32[]{:S(2)}) collective-permute-start(bf16[2,96,1152]{2,1,0:T(8,128)(2,1)S(1)} %get-tuple-element.341), channel_id=1, source_target_pairs={{0,1},{1,0},{2,3},{3,2},{4,5},{5,4},{6,7},{7,6},{8,9},{9,8},{10,11... | collective-permute-start | bytes 1327112 | tf_op jit(solution)/shard_map/ppermute | solution.py:262
  280.2 13.6 %collective-permute-done.31 = bf16[96,1920]{1,0:T(8,128)(2,1)S(1)} collective-permute-done((bf16[96,1920]{1,0:T(8,128)(2,1)S(1)}, bf16[96,1920]{1,0:T(8,128)(2,1)S(1)}, u32[]{:S(2)}, u32[]{:S(2)}) %collective-permute-start.31) | collective-permute-done | bytes 368672 | tf_op jit(solution)/shard_map/ppermute | solution.py:262
  299.3 2.0 collective-permute-done.38
  302.2 2.0 collective-permute-done.40
  310.7 2.6 collective-permute-done.41
  313.3 2.3 collective-permute-done.45
  316.0 1.6 maximum_convert_fusion
  318.3 2.1 collective-permute-start.49
  323.9 2.6 collective-permute-done.47
  327.1 1.7 maximum_convert_fusion.1
  (366 shorter events, 106.5 us)
Async XLA Ops:
  2.6 14.8 %collective-permute-start = (bf16[96,1152]{1,0:T(8,128)(2,1)S(1)}, bf16[96,1152]{1,0:T(8,128)(2,1)S(1)}, u32[]{:S(2)}, u32[]{:S(2)}) collective-permute-start(bf16[96,1152]{1,0:T(8,128)(2,1)S(1)} %pad_maximum_fusion.30), channel_id=1, source_target_pairs={{0,2},{2,0},{1,3},{3,1},{4,6},{6,4},{5,7},{7,5},{8,10},{10,8},{9,1... | collective-permute-start | bytes 663560 | tf_op jit(solution)/shard_map/ppermute | solution.py:262
  17.6 11.5 %collective-permute-start.2 = (bf16[2,96,1152]{2,1,0:T(8,128)(2,1)S(1)}, bf16[2,96,1152]{2,1,0:T(8,128)(2,1)S(1)}, u32[]{:S(2)}, u32[]{:S(2)}) collective-permute-start(bf16[2,96,1152]{2,1,0:T(8,128)(2,1)S(1)} %pad_maximum_fusion.23), channel_id=1, source_target_pairs={{0,1},{1,0},{2,3},{3,2},{4,5},{5,4},{6,7},{7,6},{8,9},{9,8},{10,11... | collective-permute-start | bytes 1327112 | tf_op jit(solution)/shard_map/ppermute | solution.py:262
  19.2 9.8 %collective-permute-start.3 = (bf16[2,12,192]{2,1,0:T(8,128)(2,1)S(1)}, bf16[2,12,192]{2,1,0:T(8,128)(2,1)S(1)}, u32[]{:S(2)}, u32[]{:S(2)}) collective-permute-start(bf16[2,12,192]{2,1,0:T(8,128)(2,1)S(1)} %pad_maximum_fusion.33), channel_id=1, source_target_pairs={{0,1},{1,0},{2,3},{3,2},{4,5},{5,4},{6,7},{7,6},{8,9},{9,8},{10,11... | collective-permute-start | bytes 27656 | tf_op jit(solution)/shard_map/ppermute | solution.py:262
  31.3 11.4 %collective-permute-start.4 = (bf16[2,2,96,640]{3,2,0,1:T(8,128)(2,1)}, bf16[2,2,96,640]{3,2,0,1:T(8,128)(2,1)S(1)}, u32[]{:S(2)}, u32[]{:S(2)}) collective-permute-start(bf16[2,2,96,640]{3,2,0,1:T(8,128)(2,1)} %slice.267), channel_id=1, source_target_pairs={{0,8},{8,0},{1,9},{9,1},{2,10},{10,2},{3,11},{11,3},{4,12},{12,4},... | collective-permute-start | bytes 1474568 | tf_op jit(solution)/shard_map/ppermute | solution.py:262
  32.7 8.9 %collective-permute-start.5 = (bf16[2,2,96,512]{3,2,0,1:T(8,128)(2,1)}, bf16[2,2,96,512]{3,2,0,1:T(8,128)(2,1)S(1)}, u32[]{:S(2)}, u32[]{:S(2)}) collective-permute-start(bf16[2,2,96,512]{3,2,0,1:T(8,128)(2,1)} %slice.268), channel_id=1, source_target_pairs={{0,16},{16,0},{1,17},{17,1},{2,18},{18,2},{3,19},{19,3},{4,20},{20... | collective-permute-start | bytes 1179656 | tf_op jit(solution)/shard_map/ppermute | solution.py:262
  34.3 19.1 %collective-permute-start.7 = (bf16[96,1920]{1,0:T(8,128)(2,1)S(1)}, bf16[96,1920]{1,0:T(8,128)(2,1)}, u32[]{:S(2)}, u32[]{:S(2)}) collective-permute-start(bf16[96,1920]{1,0:T(8,128)(2,1)S(1)} %pad_maximum_fusion.26), channel_id=1, source_target_pairs={{0,2},{2,0},{1,3},{3,1},{4,6},{6,4},{5,7},{7,5},{8,10},{10,8},{9,1... | collective-permute-start | bytes 1105928 | tf_op jit(solution)/shard_map/ppermute | solution.py:262
  44.6 10.6 %collective-permute-start.6 = (bf16[768,1152]{1,0:T(8,128)(2,1)}, bf16[768,1152]{1,0:T(8,128)(2,1)}, u32[]{:S(2)}, u32[]{:S(2)}) collective-permute-start(bf16[768,1152]{1,0:T(8,128)(2,1)} %pad_maximum_fusion.5), channel_id=1, source_target_pairs={{0,4},{4,0},{1,5},{5,1},{2,6},{6,2},{3,7},{7,3},{8,12},{12,8},{9,1... | collective-permute-start | bytes 5308424 | tf_op jit(solution)/shard_map/ppermute | solution.py:262
  54.6 17.5 %collective-permute-start.8 = (bf16[2,96,1920]{2,1,0:T(8,128)(2,1)S(1)}, bf16[2,96,1920]{2,1,0:T(8,128)(2,1)S(1)}, u32[]{:S(2)}, u32[]{:S(2)}) collective-permute-start(bf16[2,96,1920]{2,1,0:T(8,128)(2,1)S(1)} %pad_maximum_fusion.18), channel_id=1, source_target_pairs={{0,1},{1,0},{2,3},{3,2},{4,5},{5,4},{6,7},{7,6},{8,9},{9,8},{10,11... | collective-permute-start | bytes 2211848 | tf_op jit(solution)/shard_map/ppermute | solution.py:262
  72.6 18.9 %collective-permute-start.10 = (bf16[2,2,96,1024]{3,2,0,1:T(8,128)(2,1)S(1)}, bf16[2,2,96,1024]{3,2,0,1:T(8,128)(2,1)S(1)}, u32[]{:S(2)}, u32[]{:S(2)}) collective-permute-start(bf16[2,2,96,1024]{3,2,0,1:T(8,128)(2,1)S(1)} %slice.275), channel_id=1, source_target_pairs={{0,8},{8,0},{1,9},{9,1},{2,10},{10,2},{3,11},{11,3},{4,12},{12,4},... | collective-permute-start | bytes 2359304 | tf_op jit(solution)/shard_map/ppermute | solution.py:262
  73.2 16.5 %collective-permute-start.11 = (bf16[2,2,96,896]{3,2,0,1:T(8,128)(2,1)S(1)}, bf16[2,2,96,896]{3,2,0,1:T(8,128)(2,1)S(1)}, u32[]{:S(2)}, u32[]{:S(2)}) collective-permute-start(bf16[2,2,96,896]{3,2,0,1:T(8,128)(2,1)S(1)} %slice.276), channel_id=1, source_target_pairs={{0,16},{16,0},{1,17},{17,1},{2,18},{18,2},{3,19},{19,3},{4,20},{20... | collective-permute-start | bytes 2064392 | tf_op jit(solution)/shard_map/ppermute | solution.py:262
  73.8 15.8 %collective-permute-start.9 = (bf16[96,1536]{1,0:T(8,128)(2,1)S(1)}, bf16[96,1536]{1,0:T(8,128)(2,1)S(1)}, u32[]{:S(2)}, u32[]{:S(2)}) collective-permute-start(bf16[96,1536]{1,0:T(8,128)(2,1)S(1)} %pad_maximum_fusion.28), channel_id=1, source_target_pairs={{0,2},{2,0},{1,3},{3,1},{4,6},{6,4},{5,7},{7,5},{8,10},{10,8},{9,1... | collective-permute-start | bytes 884744 | tf_op jit(solution)/shard_map/ppermute | solution.py:262
  94.2 5.8 %collective-permute-start.12 = (bf16[768,1920]{1,0:T(8,128)(2,1)}, bf16[768,1920]{1,0:T(8,128)(2,1)}, u32[]{:S(2)}, u32[]{:S(2)}) collective-permute-start(bf16[768,1920]{1,0:T(8,128)(2,1)} %pad_maximum_fusion.2), channel_id=1, source_target_pairs={{0,4},{4,0},{1,5},{5,1},{2,6},{6,2},{3,7},{7,3},{8,12},{12,8},{9,1... | collective-permute-start | bytes 8847368 | tf_op jit(solution)/shard_map/ppermute | solution.py:262
  94.6 15.7 %collective-permute-start.13 = (bf16[2,96,1536]{2,1,0:T(8,128)(2,1)S(1)}, bf16[2,96,1536]{2,1,0:T(8,128)(2,1)S(1)}, u32[]{:S(2)}, u32[]{:S(2)}) collective-permute-start(bf16[2,96,1536]{2,1,0:T(8,128)(2,1)S(1)} %pad_maximum_fusion.21), channel_id=1, source_target_pairs={{0,1},{1,0},{2,3},{3,2},{4,5},{5,4},{6,7},{7,6},{8,9},{9,8},{10,11... | collective-permute-start | bytes 1769480 | tf_op jit(solution)/shard_map/ppermute | solution.py:262
  110.5 15.0 %collective-permute-start.14 = (bf16[2,2,96,768]{3,2,1,0:T(8,128)(2,1)S(1)}, bf16[2,2,96,768]{3,2,1,0:T(8,128)(2,1)S(1)}, u32[]{:S(2)}, u32[]{:S(2)}) collective-permute-start(bf16[2,2,96,768]{3,2,1,0:T(8,128)(2,1)S(1)} %get-tuple-element.329), channel_id=1, source_target_pairs={{0,8},{8,0},{1,9},{9,1},{2,10},{10,2},{3,11},{11,3},{4,12},{12,4},... | collective-permute-start | bytes 1769480 | tf_op jit(solution)/shard_map/ppermute | solution.py:262
  111.1 14.7 %collective-permute-start.15 = (bf16[2,2,96,768]{3,2,1,0:T(8,128)(2,1)S(1)}, bf16[2,2,96,768]{3,2,1,0:T(8,128)(2,1)S(1)}, u32[]{:S(2)}, u32[]{:S(2)}) collective-permute-start(bf16[2,2,96,768]{3,2,1,0:T(8,128)(2,1)S(1)} %get-tuple-element.330), channel_id=1, source_target_pairs={{0,16},{16,0},{1,17},{17,1},{2,18},{18,2},{3,19},{19,3},{4,20},{20... | collective-permute-start | bytes 1769480 | tf_op jit(solution)/shard_map/ppermute | solution.py:262
  128.1 10.9 %collective-permute-start.16 = (bf16[768,1536]{1,0:T(8,128)(2,1)}, bf16[768,1536]{1,0:T(8,128)(2,1)}, u32[]{:S(2)}, u32[]{:S(2)}) collective-permute-start(bf16[768,1536]{1,0:T(8,128)(2,1)} %pad_maximum_fusion.4), channel_id=1, source_target_pairs={{0,4},{4,0},{1,5},{5,1},{2,6},{6,2},{3,7},{7,3},{8,12},{12,8},{9,1... | collective-permute-start | bytes 7077896 | tf_op jit(solution)/shard_map/ppermute | solution.py:262
  138.4 12.8 %collective-permute-start.17 = (bf16[3072,384]{1,0:T(8,128)(2,1)S(1)}, bf16[3072,384]{1,0:T(8,128)(2,1)S(1)}, u32[]{:S(2)}, u32[]{:S(2)}) collective-permute-start(bf16[3072,384]{1,0:T(8,128)(2,1)S(1)} %convolution_convert_fusion), channel_id=1, source_target_pairs={{0,4},{4,0},{1,5},{5,1},{2,6},{6,2},{3,7},{7,3},{8,12},{12,8},{9,1... | collective-permute-start | bytes 7077896 | tf_op jit(solution)/shard_map/ppermute | solution.py:262
  171.5 23.4 %collective-permute-start.20 = (bf16[768,1536]{1,0:T(8,128)(2,1)}, bf16[768,1536]{1,0:T(8,128)(2,1)}, u32[]{:S(2)}, u32[]{:S(2)}) collective-permute-start(bf16[768,1536]{1,0:T(8,128)(2,1)} %convolution_convert_fusion.1), channel_id=1, source_target_pairs={{0,4},{4,0},{1,5},{5,1},{2,6},{6,2},{3,7},{7,3},{8,12},{12,8},{9,1... | collective-permute-start | bytes 7077896 | tf_op jit(solution)/shard_map/ppermute | solution.py:262
  174.4 18.5 %collective-permute-start.18 = (bf16[2,2,192,384]{3,2,1,0:T(8,128)(2,1)}, bf16[2,2,192,384]{3,2,1,0:T(8,128)(2,1)S(1)}, u32[]{:S(2)}, u32[]{:S(2)}) collective-permute-start(bf16[2,2,192,384]{3,2,1,0:T(8,128)(2,1)} %get-tuple-element.325), channel_id=1, source_target_pairs={{0,8},{8,0},{1,9},{9,1},{2,10},{10,2},{3,11},{11,3},{4,12},{12,4},... | collective-permute-start | bytes 1769480 | tf_op jit(solution)/shard_map/ppermute | solution.py:262
  177.0 15.9 %collective-permute-start.19 = (bf16[2,2,192,384]{3,2,1,0:T(8,128)(2,1)}, bf16[2,2,192,384]{3,2,1,0:T(8,128)(2,1)S(1)}, u32[]{:S(2)}, u32[]{:S(2)}) collective-permute-start(bf16[2,2,192,384]{3,2,1,0:T(8,128)(2,1)} %get-tuple-element.323), channel_id=1, source_target_pairs={{0,16},{16,0},{1,17},{17,1},{2,18},{18,2},{3,19},{19,3},{4,20},{20... | collective-permute-start | bytes 1769480 | tf_op jit(solution)/shard_map/ppermute | solution.py:262
  194.9 6.4 %collective-permute-start.21 = (bf16[768,384]{1,0:T(8,128)(2,1)S(1)}, bf16[768,384]{1,0:T(8,128)(2,1)S(1)}, u32[]{:S(2)}, u32[]{:S(2)}) collective-permute-start(bf16[768,384]{1,0:T(8,128)(2,1)S(1)} %convolution_convert_fusion.4), channel_id=1, source_target_pairs={{0,4},{4,0},{1,5},{5,1},{2,6},{6,2},{3,7},{7,3},{8,12},{12,8},{9,1... | collective-permute-start | bytes 1769480 | tf_op jit(solution)/shard_map/ppermute | solution.py:262
  205.4 22.7 %collective-permute-start.23 = (bf16[2,2,96,1024]{3,2,1,0:T(8,128)(2,1)}, bf16[2,2,96,1024]{3,2,1,0:T(8,128)(2,1)}, u32[]{:S(2)}, u32[]{:S(2)}) collective-permute-start(bf16[2,2,96,1024]{3,2,1,0:T(8,128)(2,1)} %get-tuple-element.305), channel_id=1, source_target_pairs={{0,8},{8,0},{1,9},{9,1},{2,10},{10,2},{3,11},{11,3},{4,12},{12,4},... | collective-permute-start | bytes 2359304 | tf_op jit(solution)/shard_map/ppermute | solution.py:262
  206.0 22.0 %collective-permute-start.24 = (bf16[2,2,96,896]{3,2,1,0:T(8,128)(2,1)}, bf16[2,2,96,896]{3,2,1,0:T(8,128)(2,1)}, u32[]{:S(2)}, u32[]{:S(2)}) collective-permute-start(bf16[2,2,96,896]{3,2,1,0:T(8,128)(2,1)} %get-tuple-element.313), channel_id=1, source_target_pairs={{0,16},{16,0},{1,17},{17,1},{2,18},{18,2},{3,19},{19,3},{4,20},{20... | collective-permute-start | bytes 2064392 | tf_op jit(solution)/shard_map/ppermute | solution.py:262
  208.9 19.1 %collective-permute-start.22 = (bf16[2,192,768]{2,1,0:T(8,128)(2,1)}, bf16[2,192,768]{2,1,0:T(8,128)(2,1)}, u32[]{:S(2)}, u32[]{:S(2)}) collective-permute-start(bf16[2,192,768]{2,1,0:T(8,128)(2,1)} %get-tuple-element.321), channel_id=1, source_target_pairs={{0,1},{1,0},{2,3},{3,2},{4,5},{5,4},{6,7},{7,6},{8,9},{9,8},{10,11... | collective-permute-start | bytes 1769480 | tf_op jit(solution)/shard_map/ppermute | solution.py:262
  232.0 12.7 %collective-permute-start.25 = (bf16[768,1152]{1,0:T(8,128)(2,1)}, bf16[768,1152]{1,0:T(8,128)(2,1)}, u32[]{:S(2)}, u32[]{:S(2)}) collective-permute-start(bf16[768,1152]{1,0:T(8,128)(2,1)} %convolution_convert_fusion.2), channel_id=1, source_target_pairs={{0,4},{4,0},{1,5},{5,1},{2,6},{6,2},{3,7},{7,3},{8,12},{12,8},{9,1... | collective-permute-start | bytes 5308424 | tf_op jit(solution)/shard_map/ppermute | solution.py:262
  239.5 25.5 %collective-permute-start.26 = (bf16[2,96,1920]{2,1,0:T(8,128)(2,1)}, bf16[2,96,1920]{2,1,0:T(8,128)(2,1)}, u32[]{:S(2)}, u32[]{:S(2)}) collective-permute-start(bf16[2,96,1920]{2,1,0:T(8,128)(2,1)} %get-tuple-element.309), channel_id=1, source_target_pairs={{0,1},{1,0},{2,3},{3,2},{4,5},{5,4},{6,7},{7,6},{8,9},{9,8},{10,11... | collective-permute-start | bytes 2211848 | tf_op jit(solution)/shard_map/ppermute | solution.py:262
  241.1 22.2 %collective-permute-start.27 = (bf16[192,768]{1,0:T(8,128)(2,1)}, bf16[192,768]{1,0:T(8,128)(2,1)}, u32[]{:S(2)}, u32[]{:S(2)}) collective-permute-start(bf16[192,768]{1,0:T(8,128)(2,1)} %get-tuple-element.351), channel_id=1, source_target_pairs={{0,2},{2,0},{1,3},{3,1},{4,6},{6,4},{5,7},{7,5},{8,10},{10,8},{9,1... | collective-permute-start | bytes 884744 | tf_op jit(solution)/shard_map/ppermute | solution.py:262
  249.9 15.1 %collective-permute-start.28 = (bf16[2,2,96,640]{3,2,1,0:T(8,128)(2,1)}, bf16[2,2,96,640]{3,2,1,0:T(8,128)(2,1)}, u32[]{:S(2)}, u32[]{:S(2)}) collective-permute-start(bf16[2,2,96,640]{3,2,1,0:T(8,128)(2,1)} %get-tuple-element.337), channel_id=1, source_target_pairs={{0,8},{8,0},{1,9},{9,1},{2,10},{10,2},{3,11},{11,3},{4,12},{12,4},... | collective-permute-start | bytes 1474568 | tf_op jit(solution)/shard_map/ppermute | solution.py:262
  252.2 12.8 %collective-permute-start.29 = (bf16[2,2,96,512]{3,2,1,0:T(8,128)(2,1)}, bf16[2,2,96,512]{3,2,1,0:T(8,128)(2,1)}, u32[]{:S(2)}, u32[]{:S(2)}) collective-permute-start(bf16[2,2,96,512]{3,2,1,0:T(8,128)(2,1)} %get-tuple-element.345), channel_id=1, source_target_pairs={{0,16},{16,0},{1,17},{17,1},{2,18},{18,2},{3,19},{19,3},{4,20},{20... | collective-permute-start | bytes 1179656 | tf_op jit(solution)/shard_map/ppermute | solution.py:262
  268.8 25.0 %collective-permute-start.30 = (bf16[2,96,1152]{2,1,0:T(8,128)(2,1)S(1)}, bf16[2,96,1152]{2,1,0:T(8,128)(2,1)S(1)}, u32[]{:S(2)}, u32[]{:S(2)}) collective-permute-start(bf16[2,96,1152]{2,1,0:T(8,128)(2,1)S(1)} %get-tuple-element.341), channel_id=1, source_target_pairs={{0,1},{1,0},{2,3},{3,2},{4,5},{5,4},{6,7},{7,6},{8,9},{9,8},{10,11... | collective-permute-start | bytes 1327112 | tf_op jit(solution)/shard_map/ppermute | solution.py:262
  273.4 5.3 %collective-permute-start.34 = (bf16[192,384]{1,0:T(8,128)(2,1)S(1)}, bf16[192,384]{1,0:T(8,128)(2,1)S(1)}, u32[]{:S(2)}, u32[]{:S(2)}) collective-permute-start(bf16[192,384]{1,0:T(8,128)(2,1)S(1)} %get-tuple-element.371), channel_id=1, source_target_pairs={{0,8},{8,0},{1,9},{9,1},{2,10},{10,2},{3,11},{11,3},{4,12},{12,4},... | collective-permute-start | bytes 442376 | tf_op jit(solution)/shard_map/ppermute | solution.py:262
  275.0 5.1 %collective-permute-start.33 = (bf16[192,384]{1,0:T(8,128)(2,1)S(1)}, bf16[192,384]{1,0:T(8,128)(2,1)S(1)}, u32[]{:S(2)}, u32[]{:S(2)}) collective-permute-start(bf16[192,384]{1,0:T(8,128)(2,1)S(1)} %get-tuple-element.372), channel_id=1, source_target_pairs={{0,16},{16,0},{1,17},{17,1},{2,18},{18,2},{3,19},{19,3},{4,20},{20... | collective-permute-start | bytes 442376 | tf_op jit(solution)/shard_map/ppermute | solution.py:262
  275.5 18.3 %collective-permute-start.31 = (bf16[96,1920]{1,0:T(8,128)(2,1)S(1)}, bf16[96,1920]{1,0:T(8,128)(2,1)S(1)}, u32[]{:S(2)}, u32[]{:S(2)}) collective-permute-start(bf16[96,1920]{1,0:T(8,128)(2,1)S(1)} %get-tuple-element.347), channel_id=1, source_target_pairs={{0,2},{2,0},{1,3},{3,1},{4,6},{6,4},{5,7},{7,5},{8,10},{10,8},{9,1... | collective-permute-start | bytes 1105928 | tf_op jit(solution)/shard_map/ppermute | solution.py:262
  294.1 4.7 %collective-permute-start.36 = (f32[12,768]{1,0:T(8,128)S(1)}, f32[12,768]{1,0:T(8,128)S(1)}, u32[]{:S(2)}, u32[]{:S(2)}) collective-permute-start(f32[12,768]{1,0:T(8,128)S(1)} %add.328), channel_id=1, source_target_pairs={{0,8},{8,0},{1,9},{9,1},{2,10},{10,2},{3,11},{11,3},{4,12},{12,4},... | collective-permute-start | bytes 110600 | tf_op jit(solution)/shard_map/ppermute | solution.py:262
  294.7 6.7 %collective-permute-start.38 = (bf16[192,384]{1,0:T(8,128)(2,1)S(1)}, bf16[192,384]{1,0:T(8,128)(2,1)S(1)}, u32[]{:S(2)}, u32[]{:S(2)}) collective-permute-start(bf16[192,384]{1,0:T(8,128)(2,1)S(1)} %get-tuple-element.262), channel_id=1, source_target_pairs={{0,16},{16,0},{1,17},{17,1},{2,18},{18,2},{3,19},{19,3},{4,20},{20... | collective-permute-start | bytes 442376 | tf_op jit(solution)/shard_map/ppermute | solution.py:262
  296.3 8.3 %collective-permute-start.35 = (bf16[96,1152]{1,0:T(8,128)(2,1)S(1)}, bf16[96,1152]{1,0:T(8,128)(2,1)S(1)}, u32[]{:S(2)}, u32[]{:S(2)}) collective-permute-start(bf16[96,1152]{1,0:T(8,128)(2,1)S(1)} %get-tuple-element.357), channel_id=1, source_target_pairs={{0,2},{2,0},{1,3},{3,1},{4,6},{6,4},{5,7},{7,5},{8,10},{10,8},{9,1... | collective-permute-start | bytes 663560 | tf_op jit(solution)/shard_map/ppermute | solution.py:262
  296.4 5.6 %collective-permute-start.37 = (bf16[192,384]{1,0:T(8,128)(2,1)S(1)}, bf16[192,384]{1,0:T(8,128)(2,1)S(1)}, u32[]{:S(2)}, u32[]{:S(2)}) collective-permute-start(bf16[192,384]{1,0:T(8,128)(2,1)S(1)} %get-tuple-element.261), channel_id=1, source_target_pairs={{0,8},{8,0},{1,9},{9,1},{2,10},{10,2},{3,11},{11,3},{4,12},{12,4},... | collective-permute-start | bytes 442376 | tf_op jit(solution)/shard_map/ppermute | solution.py:262
  297.9 6.3 %collective-permute-start.39 = (bf16[96,1024]{1,0:T(8,128)(2,1)S(1)}, bf16[96,1024]{1,0:T(8,128)(2,1)S(1)}, u32[]{:S(2)}, u32[]{:S(2)}) collective-permute-start(bf16[96,1024]{1,0:T(8,128)(2,1)S(1)} %slice.321), channel_id=1, source_target_pairs={{0,16},{16,0},{1,17},{17,1},{2,18},{18,2},{3,19},{19,3},{4,20},{20... | collective-permute-start | bytes 589832 | tf_op jit(solution)/shard_map/ppermute | solution.py:262
  298.8 5.4 %collective-permute-start.40 = (bf16[96,896]{1,0:T(8,128)(2,1)S(1)}, bf16[96,896]{1,0:T(8,128)(2,1)S(1)}, u32[]{:S(2)}, u32[]{:S(2)}) collective-permute-start(bf16[96,896]{1,0:T(8,128)(2,1)S(1)} %slice.322), channel_id=1, source_target_pairs={{0,8},{8,0},{1,9},{9,1},{2,10},{10,2},{3,11},{11,3},{4,12},{12,4},... | collective-permute-start | bytes 516104 | tf_op jit(solution)/shard_map/ppermute | solution.py:262
  304.7 6.0 %collective-permute-start.42 = (bf16[96,512]{1,0:T(8,128)(2,1)S(1)}, bf16[96,512]{1,0:T(8,128)(2,1)S(1)}, u32[]{:S(2)}, u32[]{:S(2)}) collective-permute-start(bf16[96,512]{1,0:T(8,128)(2,1)S(1)} %slice.365), channel_id=1, source_target_pairs={{0,8},{8,0},{1,9},{9,1},{2,10},{10,2},{3,11},{11,3},{4,12},{12,4},... | collective-permute-start | bytes 294920 | tf_op jit(solution)/shard_map/ppermute | solution.py:262
  306.8 6.4 %collective-permute-start.41 = (bf16[96,640]{1,0:T(8,128)(2,1)S(1)}, bf16[96,640]{1,0:T(8,128)(2,1)S(1)}, u32[]{:S(2)}, u32[]{:S(2)}) collective-permute-start(bf16[96,640]{1,0:T(8,128)(2,1)S(1)} %slice.364), channel_id=1, source_target_pairs={{0,16},{16,0},{1,17},{17,1},{2,18},{18,2},{3,19},{19,3},{4,20},{20... | collective-permute-start | bytes 368648 | tf_op jit(solution)/shard_map/ppermute | solution.py:262
  308.1 7.5 %collective-permute-start.45 = (bf16[96,896]{1,0:T(8,128)(2,1)S(1)}, bf16[96,896]{1,0:T(8,128)(2,1)S(1)}, u32[]{:S(2)}, u32[]{:S(2)}) collective-permute-start(bf16[96,896]{1,0:T(8,128)(2,1)S(1)} %add_convert_fusion.17), channel_id=1, source_target_pairs={{0,16},{16,0},{1,17},{17,1},{2,18},{18,2},{3,19},{19,3},{4,20},{20... | collective-permute-start | bytes 516104 | tf_op jit(solution)/shard_map/ppermute | solution.py:262
  308.9 6.8 %collective-permute-start.44 = (bf16[96,1024]{1,0:T(8,128)(2,1)S(1)}, bf16[96,1024]{1,0:T(8,128)(2,1)S(1)}, u32[]{:S(2)}, u32[]{:S(2)}) collective-permute-start(bf16[96,1024]{1,0:T(8,128)(2,1)S(1)} %add_convert_fusion.16), channel_id=1, source_target_pairs={{0,8},{8,0},{1,9},{9,1},{2,10},{10,2},{3,11},{11,3},{4,12},{12,4},... | collective-permute-start | bytes 589832 | tf_op jit(solution)/shard_map/ppermute | solution.py:262
  310.6 5.2 %collective-permute-start.46 = (bf16[768,384]{1,0:T(8,128)(2,1)S(1)}, bf16[768,384]{1,0:T(8,128)(2,1)S(1)}, u32[]{:S(2)}, u32[]{:S(2)}) collective-permute-start(bf16[768,384]{1,0:T(8,128)(2,1)S(1)} %bitcast.256), channel_id=1, source_target_pairs={{0,4},{4,0},{1,5},{5,1},{2,6},{6,2},{3,7},{7,3},{8,12},{12,8},{9,1... | collective-permute-start | bytes 1769480 | tf_op jit(solution)/shard_map/ppermute | solution.py:262
  317.6 6.3 %collective-permute-start.48 = (bf16[96,512]{1,0:T(8,128)(2,1)S(1)}, bf16[96,512]{1,0:T(8,128)(2,1)S(1)}, u32[]{:S(2)}, u32[]{:S(2)}) collective-permute-start(bf16[96,512]{1,0:T(8,128)(2,1)S(1)} %add_convert_fusion.21), channel_id=1, source_target_pairs={{0,16},{16,0},{1,17},{17,1},{2,18},{18,2},{3,19},{19,3},{4,20},{20... | collective-permute-start | bytes 294920 | tf_op jit(solution)/shard_map/ppermute | solution.py:262
  318.3 5.5 %collective-permute-start.49 = (f32[12,768]{1,0:T(8,128)S(1)}, f32[12,768]{1,0:T(8,128)S(1)}, u32[]{:S(2)}, u32[]{:S(2)}) collective-permute-start(f32[12,768]{1,0:T(8,128)S(1)} %add.340), channel_id=1, source_target_pairs={{0,2},{2,0},{1,3},{3,1},{4,6},{6,4},{5,7},{7,5},{8,10},{10,8},{9,1... | collective-permute-start | bytes 110600 | tf_op jit(solution)/shard_map/ppermute | solution.py:262
  321.6 4.9 %collective-permute-start.47 = (bf16[96,640]{1,0:T(8,128)(2,1)S(1)}, bf16[96,640]{1,0:T(8,128)(2,1)S(1)}, u32[]{:S(2)}, u32[]{:S(2)}) collective-permute-start(bf16[96,640]{1,0:T(8,128)(2,1)S(1)} %add_convert_fusion.20), channel_id=1, source_target_pairs={{0,8},{8,0},{1,9},{9,1},{2,10},{10,2},{3,11},{11,3},{4,12},{12,4},... | collective-permute-start | bytes 368648 | tf_op jit(solution)/shard_map/ppermute | solution.py:262
  326.9 5.5 %collective-permute-start.51 = (bf16[192,1152]{1,0:T(8,128)(2,1)S(1)}, bf16[192,1152]{1,0:T(8,128)(2,1)S(1)}, u32[]{:S(2)}, u32[]{:S(2)}) collective-permute-start(bf16[192,1152]{1,0:T(8,128)(2,1)S(1)} %pad_maximum_fusion.24), channel_id=1, source_target_pairs={{0,4},{4,0},{1,5},{5,1},{2,6},{6,2},{3,7},{7,3},{8,12},{12,8},{9,1... | collective-permute-start | bytes 1327112 | tf_op jit(solution)/shard_map/ppermute | solution.py:262
  (49 other events, 271.0 us)

commit v4 on v3

--- a/solution.py
+++ b/solution.py
@@ -479,7 +479,6 @@
 
     grad_branch = jnp.pad(out_grad, fill).reshape(row_count, width)
     grad_branch = grad_branch * live_rows.astype(bf16)
-    grad_down_b = jnp.sum(grad_branch.astype(f32), axis=0, keepdims=True)
     branch_2, d_send = together(grad_branch, start_sum(active, grad_branch))
     d_other = net.swap(d_send, net.core)
     result = middle + (dot_nn(active, down_full) + down_bias)
@@ -536,6 +535,17 @@
     )
     grad_tokens = grad_tokens.reshape(slot_count, padded, width)[:, :length]
 
+    first_sums, u_keep, u_other, d_keep, d_other, q_1, q_2, o_1, o_2 = together(
+        first_sums, *u_pair, *d_pair, *q_keeps, *q_others
+    )
+    q_piece = add_plane([q_1, q_2], [o_1, o_2])
+    u_piece = add((u_keep, u_other))
+    q_piece, u_piece, first_sums, d_keep, branch_4 = together(
+        q_piece, u_piece, first_sums, d_keep, grad_branch
+    )
+    q_pair = net.part_with(q_piece, near, 1)
+    u_pair = net.part_with(u_piece, far, 0)
+    grad_down_b = jnp.sum(branch_4.astype(f32), axis=0, keepdims=True)
     vectors = [
         mid_sums[2:3],
         mid_sums[0:2],
@@ -546,15 +556,6 @@
     ]
     vectors += [up_sums[:, k * width : (k + 1) * width] for k in range(group)]
     vectors = jnp.concatenate(vectors, axis=0)
-
-    vectors, u_keep, u_other, d_keep, d_other, q_1, q_2, o_1, o_2 = together(
-        vectors, *u_pair, *d_pair, *q_keeps, *q_others
-    )
-    q_piece = add_plane([q_1, q_2], [o_1, o_2])
-    u_piece = add((u_keep, u_other))
-    q_piece, u_piece, vectors, d_keep = together(q_piece, u_piece, vectors, d_keep)
-    q_pair = net.part_with(q_piece, near, 1)
-    u_pair = net.part_with(u_piece, far, 0)
     sums = vectors + net.swap(vectors, net.core)
     d_piece = exchange_plane(add((d_keep, d_other)))
     q_keep, q_other, u_keep, u_other, sums, *d_piece = together(*q_pair, *u_pair, sums, *d_piece)

time: 339 us -> 339 us (level)
    unnamed x86 -> x88, local copies, waits for them, and re-layouts: 8.33 us -> 8.11 us
  transfers between devices with their start and end apart: 53 -> 53, of which waited for: 30 -> 26; matrix products, arithmetic and copies ran while one was open for 30% -> 30% of each run, Pallas kernels for 14% -> 14%
where the time goes in v4:
time: 339 us; the launch traced here: 334 us
  waiting for transfers between devices  77.8 us (23%)
  matrix products  61.7 us (18%)
  starting transfers between devices  55.4 us (16%)
  Pallas kernels  53.6 us (16%)
  other arithmetic  41.6 us (12%)
  local copies, waits for them, and re-layouts  40.8 us (12%)
    ppermute x53, waiting for transfers between devices, swap(): return lax.ppermute(piece, name, SWAP)  77.8 us
    ppermute x53, starting transfers between devices, swap(): return lax.ppermute(piece, name, SWAP)  55.4 us
    dot_general x8, matrix products, dot_tn(): lax.dot_general(a, b, (((0,), (0,)), ((), ())), preferred_element_type=f32)  35.2 us
    dot_general x4, matrix products, dot_nn(): return jnp.dot(a, b, preferred_element_type=f32)  23.3 us
    pallas_call x2, Pallas kernels, matmul_norm_back(): pl.pallas_call(norm_back_kernel if both else norm_back_low_kernel, grid=(...  22.5 us
    pallas_call x1, Pallas kernels, attention_back(): pl.pallas_call(attention_back_kernel, grid=(slots,), in_specs=[pl.BlockSp...  14.4 us
    convert_element_type x17, other arithmetic, add(): return (pair[0].astype(f32) + pair[1].astype(f32)).astype(bf16)  10 us
    select_n x6, other arithmetic, place(): return (jnp.where(bit == 0, mine, other), jnp.where(bit == 0, other, mine))  8.69 us
  transfers between devices with their start and end apart: 53, of which 26 were waited for; matrix products, arithmetic and copies ran while one was open for 30% of the time, Pallas kernels for 14%

profile of v4, /device:TPU:0, one launch (start us, length us, event | category | flops | bytes accessed | tf_op | source)
XLA Modules:
  0.0 334.3 jit_solution(15729914759641294757)
XLA Ops:
  2.6 4.1 %collective-permute-start = (bf16[96,1152]{1,0:T(8,128)(2,1)S(1)}, bf16[96,1152]{1,0:T(8,128)(2,1)S(1)}, u32[]{:S(2)}, u32[]{:S(2)}) collective-permute-start(bf16[96,1152]{1,0:T(8,128)(2,1)S(1)} %pad_maximum_fusion.30), channel_id=1, source_target_pairs={{0,2},{2,0},{1,3},{3,1},{4,6},{6,4},{5,7},{7,5},{8,10},{10,8},{9,1... | collective-permute-start | bytes 663560 | tf_op jit(solution)/shard_map/ppermute | solution.py:262
  15.1 2.3 collective-permute-done.1
  17.6 1.6 collective-permute-start.2
  19.7 9.3 %collective-permute-done.3 = bf16[2,12,192]{2,1,0:T(8,128)(2,1)S(1)} collective-permute-done((bf16[2,12,192]{2,1,0:T(8,128)(2,1)S(1)}, bf16[2,12,192]{2,1,0:T(8,128)(2,1)S(1)}, u32[]{:S(2)}, u32[]{:S(2)}) %collective-permute-start.3) | collective-permute-done | bytes 9248 | tf_op jit(solution)/shard_map/ppermute | solution.py:262
  34.9 3.4 %collective-permute-start.7 = (bf16[96,1920]{1,0:T(8,128)(2,1)S(1)}, bf16[96,1920]{1,0:T(8,128)(2,1)}, u32[]{:S(2)}, u32[]{:S(2)}) collective-permute-start(bf16[96,1920]{1,0:T(8,128)(2,1)S(1)} %pad_maximum_fusion.26), channel_id=1, source_target_pairs={{0,2},{2,0},{1,3},{3,1},{4,6},{6,4},{5,7},{7,5},{8,10},{10,8},{9,1... | collective-permute-start | bytes 1105928 | tf_op jit(solution)/shard_map/ppermute | solution.py:262
  39.7 2.5 collective-permute-done.5
  50.9 3.2 collective-permute-done.7
  55.8 2.3 broadcast_select_fusion.5
  58.4 4.6 %fusion.5 = bf16[1040,2304]{1,0:T(8,128)(2,1)S(1)} fusion(bf16[1040,768]{1,0:T(8,128)(2,1)S(1)} %fusion.12, bf16[768,2304]{1,0:T(8,128)(2,1)S(1)} %pad_maximum_fusion.1.weight_ref, f32[2304]{0:T(1024)S(1)} %pad_maximum_fusion.34), kind=kOutput, calls=%fused_computation.10 | convolution fusion | flops 3685294080 | bytes 9937920 | tf_op jit(solution)/shard_map/dot_general | solution.py:44
  63.1 8.4 %attention.1 = (bf16[5,208,768]{2,1,0:T(8,128)(2,1)S(1)}, bf16[5,12,208,208]{3,2,1,0:T(8,128)(2,1)}) custom-call(bf16[5,208,2304]{2,1,0:T(8,128)(2,1)S(1)} %bitcast.226), custom_call_target="tpu_custom_call" | custom-call | tf_op jit(solution)/shard_map/attention/pallas_call | solution.py:118
  74.8 4.8 %collective-permute-start.9 = (bf16[96,1536]{1,0:T(8,128)(2,1)S(1)}, bf16[96,1536]{1,0:T(8,128)(2,1)S(1)}, u32[]{:S(2)}, u32[]{:S(2)}) collective-permute-start(bf16[96,1536]{1,0:T(8,128)(2,1)S(1)} %copy-done.32), channel_id=1, source_target_pairs={{0,2},{2,0},{1,3},{3,1},{4,6},{6,4},{5,7},{7,5},{8,10},{10,8},{9,1... | collective-permute-start | bytes 884744 | tf_op jit(solution)/shard_map/ppermute | solution.py:262
  79.6 12.7 %collective-permute-done.9 = bf16[96,1536]{1,0:T(8,128)(2,1)S(1)} collective-permute-done((bf16[96,1536]{1,0:T(8,128)(2,1)S(1)}, bf16[96,1536]{1,0:T(8,128)(2,1)S(1)}, u32[]{:S(2)}, u32[]{:S(2)}) %collective-permute-start.9) | collective-permute-done | bytes 294944 | tf_op jit(solution)/shard_map/ppermute | solution.py:262
  93.2 1.8 pad_maximum_fusion.2
  97.2 4.4 %collective-permute-done.12 = bf16[768,1920]{1,0:T(8,128)(2,1)} collective-permute-done((bf16[768,1920]{1,0:T(8,128)(2,1)}, bf16[768,1920]{1,0:T(8,128)(2,1)}, u32[]{:S(2)}, u32[]{:S(2)}) %collective-permute-start.12) | collective-permute-done | bytes 2949152 | tf_op jit(solution)/shard_map/ppermute | solution.py:262
  101.6 3.3 broadcast_select_fusion
  106.2 1.6 fusion.56
  108.7 3.5 %collective-permute-done.13 = bf16[2,96,1536]{2,1,0:T(8,128)(2,1)S(1)} collective-permute-done((bf16[2,96,1536]{2,1,0:T(8,128)(2,1)}, bf16[2,96,1536]{2,1,0:T(8,128)(2,1)S(1)}, u32[]{:S(2)}, u32[]{:S(2)}) %collective-permute-start.13) | collective-permute-done | bytes 589856 | tf_op jit(solution)/shard_map/ppermute | solution.py:262
  115.7 11.8 %fusion.4 = (bf16[1040,3072]{1,0:T(8,128)(2,1)}, bf16[1040,3072]{1,0:T(8,128)(2,1)}) fusion(f32[3072]{0:T(1024)S(1)} %add.295, bf16[1040,768]{1,0:T(8,128)(2,1)S(1)} %add_convert_fusion.3, bf16[768,3072]{1,0:T(8,128)(2,1)S(1)} %pad_maximum_fusion.weight_ref), kind=kOutput, calls=%fused_computation.7 | convolution fusion | flops 4945674240 | bytes 19107840 | tf_op jit(solution)/shard_map/dot_general | solution.py:44
  128.2 1.6 pad_maximum_fusion.4
  131.5 7.1 %convolution_convert_fusion = bf16[3072,384]{1,0:T(8,128)(2,1)S(1)} fusion(bf16[1040,3072]{1,0:T(8,128)(2,1)} %get-tuple-element.183, bf16[1040,768]{1,0:T(8,128)(2,1)S(1)} %bitcast_multiply_fusion.grad_ref.past_ref, s32[]{:T(128)S(6)} %select_n.456), kind=kOutput, calls=%fused_computation.15 | convolution fusion | flops 2454847488 | bytes 9547780 | tf_op jit(solution)/shard_map/dot_general | solution.py:40
  139.2 2.7 broadcast_select_fusion.3
  145.0 5.2 %fusion.8 = bf16[1040,768]{1,0:T(8,128)(2,1)S(1)} fusion(f32[1040,768]{1,0:T(8,128)S(1)} %copy-done.13, bf16[1040,3072]{1,0:T(8,128)(2,1)S(1)} %bitcast.275, bf16[3072,768]{1,0:T(8,128)(2,1)S(1)} %bitcast.228, f32[1040]{0:T(1024)S(1)} %broadcast_in_dim_reshape.4, f32[768]{0:T(1024)S(1)} %add.300), kind=kOutput, calls=%fused_computation.26 | convolution fusion | flops 4910530560 | bytes 15907904 | tf_op jit(solution)/shard_map/dot_general | solution.py:44
  151.5 5.7 %add_convert_fusion.1 = bf16[3072,384]{1,0:T(8,128)(2,1)} fusion(bf16[3072,384]{1,0:T(8,128)(2,1)S(1)} %collective-permute-done.17, bf16[1040,3072]{1,0:T(8,128)(2,1)S(1)} %bitcast.275, bf16[1040,768]{1,0:T(8,128)(2,1)S(1)} %bitcast_multiply_fusion.grad_ref.past_ref, s32[]{:T(128)S(6)} %select_n.416), kind=kOutput, calls=%fused_computation.14 | convolution fusion | flops 2457206784 | bytes 11907076 | tf_op jit(solution)/shard_map/dot_general | solution.py:40
  157.2 8.3 %hidden_back.1 = (bf16[1040,3072]{1,0:T(8,128)(2,1)}, f32[1,3072]{1,0:T(1,128)S(1)}) custom-call(bf16[1040,768]{1,0:T(8,128)(2,1)S(1)} %bitcast_multiply_fusion.grad_ref.past_ref, bf16[3072,768]{1,0:T(8,128)(2,1)S(1)} %bitcast.229, bf16[1040,3072]{1,0:T(8,128)(2,1)S(1)} %bitcast.233), custom_call_target="tpu_custom_call" | custom-call | tf_op jit(solution)/shard_map/hidden_back/pallas_call | solution.py:172
  165.4 6.4 %convolution_convert_fusion.1 = bf16[768,1536]{1,0:T(8,128)(2,1)} fusion(bf16[1040,768]{1,0:T(8,128)(2,1)S(1)} %copy-done.28, bf16[1040,3072]{1,0:T(8,128)(2,1)} %get-tuple-element.198.grad_ref, s32[]{:T(128)S(6)} %select_n.457), kind=kOutput, calls=%fused_computation.27 | convolution fusion | flops 2454847488 | bytes 7151620 | tf_op jit(solution)/shard_map/dot_general | solution.py:40
  171.9 1.9 fusion.49
  178.7 13.8 %matmul_norm_back.2 = (f32[1040,768]{1,0:T(8,128)S(1)}, bf16[1040,768]{1,0:T(8,128)(2,1)S(1)}, f32[8,768]{1,0:T(8,128)S(1)}) custom-call(bf16[1040,3072]{1,0:T(8,128)(2,1)} %get-tuple-element.198.grad_ref, bf16[768,3072]{1,0:T(8,128)(2,1)} %copy-done.14, f32[1040,768]{1,0:T(8,128)} %copy-done.12, f32[1,768]{1,0:T(1,128)S(1)} %slice.301.gain_ref, ...), custom_call_target="tpu_custom_call" | custom-call | tf_op jit(solution)/shard_map/matmul_norm_back/pallas_call | solution.py:232
  195.6 5.7 %add_convert_fusion = bf16[768,1536]{1,0:T(8,128)(2,1)S(1)} fusion(bf16[768,1536]{1,0:T(8,128)(2,1)} %collective-permute-done.20, bf16[1040,768]{1,0:T(8,128)(2,1)S(1)} %copy-done.29, bf16[1040,3072]{1,0:T(8,128)(2,1)} %get-tuple-element.198.grad_ref, s32[]{:T(128)} %select_n.415), kind=kOutput, calls=%fused_computation.13 | convolution fusion | flops 2457206784 | bytes 9511424 | tf_op jit(solution)/shard_map/dot_general | solution.py:40
  210.8 1.7 collective-permute-start.22
  212.5 3.2 convolution_convert_fusion.3
  215.7 2.3 copy-done.1
  218.1 14.4 %attention_back.1 = (bf16[5,208,2304]{2,1,0:T(8,128)(2,1)S(1)}, f32[1,2304]{1,0:T(1,128)S(1)}) custom-call(bf16[5,208,2304]{2,1,0:T(8,128)(2,1)S(1)} %bitcast.227, bf16[5,12,208,208]{3,2,1,0:T(8,128)(2,1)} %get-tuple-element.186.prob_ref, bf16[5,208,768]{2,1,0:T(8,128)(2,1)S(1)} %bitcast.239), custom_call_target="tpu_custom_call" | custom-call | tf_op jit(solution)/shard_map/attention_back/pallas_call | solution.py:139
  232.6 3.8 %convolution_convert_fusion.2 = bf16[768,1152]{1,0:T(8,128)(2,1)} fusion(bf16[1040,768]{1,0:T(8,128)(2,1)S(1)} %copy-done.25, bf16[1040,2304]{1,0:T(8,128)(2,1)S(1)} %bitcast.234, s32[]{:T(128)S(6)} %select_n.464), kind=kOutput, calls=%fused_computation.28 | convolution fusion | flops 1841135616 | bytes 5763076 | tf_op jit(solution)/shard_map/dot_general | solution.py:40
  236.5 1.6 add_convert_fusion.6
  238.2 1.7 add_convert_fusion.4
  241.9 4.9 %collective-permute-start.27 = (bf16[192,768]{1,0:T(8,128)(2,1)S(1)}, bf16[192,768]{1,0:T(8,128)(2,1)S(1)}, u32[]{:S(2)}, u32[]{:S(2)}) collective-permute-start(bf16[192,768]{1,0:T(8,128)(2,1)S(1)} %get-tuple-element.353), channel_id=1, source_target_pairs={{0,2},{2,0},{1,3},{3,1},{4,6},{6,4},{5,7},{7,5},{8,10},{10,8},{9,1... | collective-permute-start | bytes 884744 | tf_op jit(solution)/shard_map/ppermute | solution.py:262
  246.8 4.1 %add_convert_fusion.2 = bf16[768,1152]{1,0:T(8,128)(2,1)S(1)} fusion(bf16[768,1152]{1,0:T(8,128)(2,1)} %collective-permute-done.25, bf16[1040,768]{1,0:T(8,128)(2,1)S(1)} %copy-done.26, bf16[1040,2304]{1,0:T(8,128)(2,1)S(1)} %bitcast.237, s32[]{:T(128)S(6)} %select_n.402), kind=kOutput, calls=%fused_computation.25 | convolution fusion | flops 1842905088 | bytes 7532548 | tf_op jit(solution)/shard_map/dot_general | solution.py:40
  253.9 8.7 %matmul_norm_back.3 = (bf16[1040,768]{1,0:T(8,128)(2,1)S(1)}, f32[8,768]{1,0:T(8,128)S(1)}) custom-call(bf16[1040,2304]{1,0:T(8,128)(2,1)S(1)} %bitcast.238, bf16[768,2304]{1,0:T(8,128)(2,1)S(1)} %copy-done.3, bf16[1040,768]{1,0:T(8,128)(2,1)S(1)} %bitcast.231, f32[1,768]{1,0:T(1,128)S(1)} %slice.306.gain_ref, f32[1040,768]{1,0:T(8,128)S(1)} %copy-done.6), custom_call_target="tpu_custom_call" | custom-call | tf_op jit(solution)/shard_map/matmul_norm_back/pallas_call | solution.py:232
  262.6 1.9 collective-permute-done.27
  264.6 2.2 collective-permute-done.26
  267.3 4.6 %collective-permute-start.30 = (bf16[2,96,1152]{2,1,0:T(8,128)(2,1)S(1)}, bf16[2,96,1152]{2,1,0:T(8,128)(2,1)}, u32[]{:S(2)}, u32[]{:S(2)}) collective-permute-start(bf16[2,96,1152]{2,1,0:T(8,128)(2,1)S(1)} %get-tuple-element.343), channel_id=1, source_target_pairs={{0,1},{1,0},{2,3},{3,2},{4,5},{5,4},{6,7},{7,6},{8,9},{9,8},{10,11... | collective-permute-start | bytes 1327112 | tf_op jit(solution)/shard_map/ppermute | solution.py:262
  277.4 2.1 collective-permute-done.34
  280.1 11.7 %collective-permute-done.31 = bf16[96,1920]{1,0:T(8,128)(2,1)} collective-permute-done((bf16[96,1920]{1,0:T(8,128)(2,1)}, bf16[96,1920]{1,0:T(8,128)(2,1)}, u32[]{:S(2)}, u32[]{:S(2)}) %collective-permute-start.31) | collective-permute-done | bytes 368672 | tf_op jit(solution)/shard_map/ppermute | solution.py:262
  302.8 1.7 collective-permute-done.40
  311.8 2.8 collective-permute-done.41
  314.7 2.6 collective-permute-done.45
  322.0 3.2 collective-permute-done.49
  327.6 1.7 maximum_convert_fusion.1
  (367 shorter events, 105.6 us)
Async XLA Ops:
  2.6 14.8 %collective-permute-start = (bf16[96,1152]{1,0:T(8,128)(2,1)S(1)}, bf16[96,1152]{1,0:T(8,128)(2,1)S(1)}, u32[]{:S(2)}, u32[]{:S(2)}) collective-permute-start(bf16[96,1152]{1,0:T(8,128)(2,1)S(1)} %pad_maximum_fusion.30), channel_id=1, source_target_pairs={{0,2},{2,0},{1,3},{3,1},{4,6},{6,4},{5,7},{7,5},{8,10},{10,8},{9,1... | collective-permute-start | bytes 663560 | tf_op jit(solution)/shard_map/ppermute | solution.py:262
  17.6 11.5 %collective-permute-start.2 = (bf16[2,96,1152]{2,1,0:T(8,128)(2,1)S(1)}, bf16[2,96,1152]{2,1,0:T(8,128)(2,1)S(1)}, u32[]{:S(2)}, u32[]{:S(2)}) collective-permute-start(bf16[2,96,1152]{2,1,0:T(8,128)(2,1)S(1)} %pad_maximum_fusion.23), channel_id=1, source_target_pairs={{0,1},{1,0},{2,3},{3,2},{4,5},{5,4},{6,7},{7,6},{8,9},{9,8},{10,11... | collective-permute-start | bytes 1327112 | tf_op jit(solution)/shard_map/ppermute | solution.py:262
  19.2 9.8 %collective-permute-start.3 = (bf16[2,12,192]{2,1,0:T(8,128)(2,1)S(1)}, bf16[2,12,192]{2,1,0:T(8,128)(2,1)S(1)}, u32[]{:S(2)}, u32[]{:S(2)}) collective-permute-start(bf16[2,12,192]{2,1,0:T(8,128)(2,1)S(1)} %pad_maximum_fusion.33), channel_id=1, source_target_pairs={{0,1},{1,0},{2,3},{3,2},{4,5},{5,4},{6,7},{7,6},{8,9},{9,8},{10,11... | collective-permute-start | bytes 27656 | tf_op jit(solution)/shard_map/ppermute | solution.py:262
  31.9 11.4 %collective-permute-start.4 = (bf16[2,2,96,640]{3,2,0,1:T(8,128)(2,1)}, bf16[2,2,96,640]{3,2,0,1:T(8,128)(2,1)S(1)}, u32[]{:S(2)}, u32[]{:S(2)}) collective-permute-start(bf16[2,2,96,640]{3,2,0,1:T(8,128)(2,1)} %slice.267), channel_id=1, source_target_pairs={{0,8},{8,0},{1,9},{9,1},{2,10},{10,2},{3,11},{11,3},{4,12},{12,4},... | collective-permute-start | bytes 1474568 | tf_op jit(solution)/shard_map/ppermute | solution.py:262
  33.3 8.9 %collective-permute-start.5 = (bf16[2,2,96,512]{3,2,0,1:T(8,128)(2,1)}, bf16[2,2,96,512]{3,2,0,1:T(8,128)(2,1)S(1)}, u32[]{:S(2)}, u32[]{:S(2)}) collective-permute-start(bf16[2,2,96,512]{3,2,0,1:T(8,128)(2,1)} %slice.268), channel_id=1, source_target_pairs={{0,16},{16,0},{1,17},{17,1},{2,18},{18,2},{3,19},{19,3},{4,20},{20... | collective-permute-start | bytes 1179656 | tf_op jit(solution)/shard_map/ppermute | solution.py:262
  34.9 19.1 %collective-permute-start.7 = (bf16[96,1920]{1,0:T(8,128)(2,1)S(1)}, bf16[96,1920]{1,0:T(8,128)(2,1)}, u32[]{:S(2)}, u32[]{:S(2)}) collective-permute-start(bf16[96,1920]{1,0:T(8,128)(2,1)S(1)} %pad_maximum_fusion.26), channel_id=1, source_target_pairs={{0,2},{2,0},{1,3},{3,1},{4,6},{6,4},{5,7},{7,5},{8,10},{10,8},{9,1... | collective-permute-start | bytes 1105928 | tf_op jit(solution)/shard_map/ppermute | solution.py:262
  45.2 10.6 %collective-permute-start.6 = (bf16[768,1152]{1,0:T(8,128)(2,1)}, bf16[768,1152]{1,0:T(8,128)(2,1)}, u32[]{:S(2)}, u32[]{:S(2)}) collective-permute-start(bf16[768,1152]{1,0:T(8,128)(2,1)} %pad_maximum_fusion.5), channel_id=1, source_target_pairs={{0,4},{4,0},{1,5},{5,1},{2,6},{6,2},{3,7},{7,3},{8,12},{12,8},{9,1... | collective-permute-start | bytes 5308424 | tf_op jit(solution)/shard_map/ppermute | solution.py:262
  55.2 17.5 %collective-permute-start.8 = (bf16[2,96,1920]{2,1,0:T(8,128)(2,1)S(1)}, bf16[2,96,1920]{2,1,0:T(8,128)(2,1)S(1)}, u32[]{:S(2)}, u32[]{:S(2)}) collective-permute-start(bf16[2,96,1920]{2,1,0:T(8,128)(2,1)S(1)} %pad_maximum_fusion.18), channel_id=1, source_target_pairs={{0,1},{1,0},{2,3},{3,2},{4,5},{5,4},{6,7},{7,6},{8,9},{9,8},{10,11... | collective-permute-start | bytes 2211848 | tf_op jit(solution)/shard_map/ppermute | solution.py:262
  73.1 19.1 %collective-permute-start.10 = (bf16[2,2,96,1024]{3,2,0,1:T(8,128)(2,1)S(1)}, bf16[2,2,96,1024]{3,2,0,1:T(8,128)(2,1)S(1)}, u32[]{:S(2)}, u32[]{:S(2)}) collective-permute-start(bf16[2,2,96,1024]{3,2,0,1:T(8,128)(2,1)S(1)} %slice.275), channel_id=1, source_target_pairs={{0,8},{8,0},{1,9},{9,1},{2,10},{10,2},{3,11},{11,3},{4,12},{12,4},... | collective-permute-start | bytes 2359304 | tf_op jit(solution)/shard_map/ppermute | solution.py:262
  73.8 18.5 %collective-permute-start.11 = (bf16[2,2,96,896]{3,2,0,1:T(8,128)(2,1)S(1)}, bf16[2,2,96,896]{3,2,0,1:T(8,128)(2,1)S(1)}, u32[]{:S(2)}, u32[]{:S(2)}) collective-permute-start(bf16[2,2,96,896]{3,2,0,1:T(8,128)(2,1)S(1)} %slice.276), channel_id=1, source_target_pairs={{0,16},{16,0},{1,17},{17,1},{2,18},{18,2},{3,19},{19,3},{4,20},{20... | collective-permute-start | bytes 2064392 | tf_op jit(solution)/shard_map/ppermute | solution.py:262
  74.8 17.4 %collective-permute-start.9 = (bf16[96,1536]{1,0:T(8,128)(2,1)S(1)}, bf16[96,1536]{1,0:T(8,128)(2,1)S(1)}, u32[]{:S(2)}, u32[]{:S(2)}) collective-permute-start(bf16[96,1536]{1,0:T(8,128)(2,1)S(1)} %copy-done.32), channel_id=1, source_target_pairs={{0,2},{2,0},{1,3},{3,1},{4,6},{6,4},{5,7},{7,5},{8,10},{10,8},{9,1... | collective-permute-start | bytes 884744 | tf_op jit(solution)/shard_map/ppermute | solution.py:262
  95.9 5.7 %collective-permute-start.12 = (bf16[768,1920]{1,0:T(8,128)(2,1)}, bf16[768,1920]{1,0:T(8,128)(2,1)}, u32[]{:S(2)}, u32[]{:S(2)}) collective-permute-start(bf16[768,1920]{1,0:T(8,128)(2,1)} %pad_maximum_fusion.2), channel_id=1, source_target_pairs={{0,4},{4,0},{1,5},{5,1},{2,6},{6,2},{3,7},{7,3},{8,12},{12,8},{9,1... | collective-permute-start | bytes 8847368 | tf_op jit(solution)/shard_map/ppermute | solution.py:262
  96.2 15.9 %collective-permute-start.13 = (bf16[2,96,1536]{2,1,0:T(8,128)(2,1)}, bf16[2,96,1536]{2,1,0:T(8,128)(2,1)S(1)}, u32[]{:S(2)}, u32[]{:S(2)}) collective-permute-start(bf16[2,96,1536]{2,1,0:T(8,128)(2,1)} %pad_maximum_fusion.21), channel_id=1, source_target_pairs={{0,1},{1,0},{2,3},{3,2},{4,5},{5,4},{6,7},{7,6},{8,9},{9,8},{10,11... | collective-permute-start | bytes 1769480 | tf_op jit(solution)/shard_map/ppermute | solution.py:262
  112.3 15.2 %collective-permute-start.14 = (bf16[2,2,96,768]{3,2,1,0:T(8,128)(2,1)S(1)}, bf16[2,2,96,768]{3,2,1,0:T(8,128)(2,1)S(1)}, u32[]{:S(2)}, u32[]{:S(2)}) collective-permute-start(bf16[2,2,96,768]{3,2,1,0:T(8,128)(2,1)S(1)} %get-tuple-element.331), channel_id=1, source_target_pairs={{0,8},{8,0},{1,9},{9,1},{2,10},{10,2},{3,11},{11,3},{4,12},{12,4},... | collective-permute-start | bytes 1769480 | tf_op jit(solution)/shard_map/ppermute | solution.py:262
  113.0 14.7 %collective-permute-start.15 = (bf16[2,2,96,768]{3,2,1,0:T(8,128)(2,1)S(1)}, bf16[2,2,96,768]{3,2,1,0:T(8,128)(2,1)S(1)}, u32[]{:S(2)}, u32[]{:S(2)}) collective-permute-start(bf16[2,2,96,768]{3,2,1,0:T(8,128)(2,1)S(1)} %get-tuple-element.332), channel_id=1, source_target_pairs={{0,16},{16,0},{1,17},{17,1},{2,18},{18,2},{3,19},{19,3},{4,20},{20... | collective-permute-start | bytes 1769480 | tf_op jit(solution)/shard_map/ppermute | solution.py:262
  130.2 9.0 %collective-permute-start.16 = (bf16[768,1536]{1,0:T(8,128)(2,1)}, bf16[768,1536]{1,0:T(8,128)(2,1)}, u32[]{:S(2)}, u32[]{:S(2)}) collective-permute-start(bf16[768,1536]{1,0:T(8,128)(2,1)} %pad_maximum_fusion.4), channel_id=1, source_target_pairs={{0,4},{4,0},{1,5},{5,1},{2,6},{6,2},{3,7},{7,3},{8,12},{12,8},{9,1... | collective-permute-start | bytes 7077896 | tf_op jit(solution)/shard_map/ppermute | solution.py:262
  138.6 12.8 %collective-permute-start.17 = (bf16[3072,384]{1,0:T(8,128)(2,1)S(1)}, bf16[3072,384]{1,0:T(8,128)(2,1)S(1)}, u32[]{:S(2)}, u32[]{:S(2)}) collective-permute-start(bf16[3072,384]{1,0:T(8,128)(2,1)S(1)} %convolution_convert_fusion), channel_id=1, source_target_pairs={{0,4},{4,0},{1,5},{5,1},{2,6},{6,2},{3,7},{7,3},{8,12},{12,8},{9,1... | collective-permute-start | bytes 7077896 | tf_op jit(solution)/shard_map/ppermute | solution.py:262
  171.8 22.8 %collective-permute-start.20 = (bf16[768,1536]{1,0:T(8,128)(2,1)}, bf16[768,1536]{1,0:T(8,128)(2,1)}, u32[]{:S(2)}, u32[]{:S(2)}) collective-permute-start(bf16[768,1536]{1,0:T(8,128)(2,1)} %convolution_convert_fusion.1), channel_id=1, source_target_pairs={{0,4},{4,0},{1,5},{5,1},{2,6},{6,2},{3,7},{7,3},{8,12},{12,8},{9,1... | collective-permute-start | bytes 7077896 | tf_op jit(solution)/shard_map/ppermute | solution.py:262
  174.9 17.6 %collective-permute-start.18 = (bf16[2,2,192,384]{3,2,1,0:T(8,128)(2,1)}, bf16[2,2,192,384]{3,2,1,0:T(8,128)(2,1)}, u32[]{:S(2)}, u32[]{:S(2)}) collective-permute-start(bf16[2,2,192,384]{3,2,1,0:T(8,128)(2,1)} %get-tuple-element.327), channel_id=1, source_target_pairs={{0,8},{8,0},{1,9},{9,1},{2,10},{10,2},{3,11},{11,3},{4,12},{12,4},... | collective-permute-start | bytes 1769480 | tf_op jit(solution)/shard_map/ppermute | solution.py:262
  177.6 15.7 %collective-permute-start.19 = (bf16[2,2,192,384]{3,2,1,0:T(8,128)(2,1)}, bf16[2,2,192,384]{3,2,1,0:T(8,128)(2,1)}, u32[]{:S(2)}, u32[]{:S(2)}) collective-permute-start(bf16[2,2,192,384]{3,2,1,0:T(8,128)(2,1)} %get-tuple-element.325), channel_id=1, source_target_pairs={{0,16},{16,0},{1,17},{17,1},{2,18},{18,2},{3,19},{19,3},{4,20},{20... | collective-permute-start | bytes 1769480 | tf_op jit(solution)/shard_map/ppermute | solution.py:262
  194.5 6.9 %collective-permute-start.21 = (bf16[768,384]{1,0:T(8,128)(2,1)S(1)}, bf16[768,384]{1,0:T(8,128)(2,1)S(1)}, u32[]{:S(2)}, u32[]{:S(2)}) collective-permute-start(bf16[768,384]{1,0:T(8,128)(2,1)S(1)} %convolution_convert_fusion.4), channel_id=1, source_target_pairs={{0,4},{4,0},{1,5},{5,1},{2,6},{6,2},{3,7},{7,3},{8,12},{12,8},{9,1... | collective-permute-start | bytes 1769480 | tf_op jit(solution)/shard_map/ppermute | solution.py:262
  205.7 26.9 %collective-permute-start.23 = (bf16[2,2,96,1024]{3,2,1,0:T(8,128)(2,1)}, bf16[2,2,96,1024]{3,2,1,0:T(8,128)(2,1)}, u32[]{:S(2)}, u32[]{:S(2)}) collective-permute-start(bf16[2,2,96,1024]{3,2,1,0:T(8,128)(2,1)} %get-tuple-element.307), channel_id=1, source_target_pairs={{0,8},{8,0},{1,9},{9,1},{2,10},{10,2},{3,11},{11,3},{4,12},{12,4},... | collective-permute-start | bytes 2359304 | tf_op jit(solution)/shard_map/ppermute | solution.py:262
  206.4 26.2 %collective-permute-start.24 = (bf16[2,2,96,896]{3,2,1,0:T(8,128)(2,1)}, bf16[2,2,96,896]{3,2,1,0:T(8,128)(2,1)}, u32[]{:S(2)}, u32[]{:S(2)}) collective-permute-start(bf16[2,2,96,896]{3,2,1,0:T(8,128)(2,1)} %get-tuple-element.315), channel_id=1, source_target_pairs={{0,16},{16,0},{1,17},{17,1},{2,18},{18,2},{3,19},{19,3},{4,20},{20... | collective-permute-start | bytes 2064392 | tf_op jit(solution)/shard_map/ppermute | solution.py:262
  210.8 21.8 %collective-permute-start.22 = (bf16[2,192,768]{2,1,0:T(8,128)(2,1)}, bf16[2,192,768]{2,1,0:T(8,128)(2,1)}, u32[]{:S(2)}, u32[]{:S(2)}) collective-permute-start(bf16[2,192,768]{2,1,0:T(8,128)(2,1)} %get-tuple-element.323), channel_id=1, source_target_pairs={{0,1},{1,0},{2,3},{3,2},{4,5},{5,4},{6,7},{7,6},{8,9},{9,8},{10,11... | collective-permute-start | bytes 1769480 | tf_op jit(solution)/shard_map/ppermute | solution.py:262
  236.4 10.3 %collective-permute-start.25 = (bf16[768,1152]{1,0:T(8,128)(2,1)}, bf16[768,1152]{1,0:T(8,128)(2,1)}, u32[]{:S(2)}, u32[]{:S(2)}) collective-permute-start(bf16[768,1152]{1,0:T(8,128)(2,1)} %convolution_convert_fusion.2), channel_id=1, source_target_pairs={{0,4},{4,0},{1,5},{5,1},{2,6},{6,2},{3,7},{7,3},{8,12},{12,8},{9,1... | collective-permute-start | bytes 5308424 | tf_op jit(solution)/shard_map/ppermute | solution.py:262
  241.5 25.3 %collective-permute-start.26 = (bf16[2,96,1920]{2,1,0:T(8,128)(2,1)S(1)}, bf16[2,96,1920]{2,1,0:T(8,128)(2,1)S(1)}, u32[]{:S(2)}, u32[]{:S(2)}) collective-permute-start(bf16[2,96,1920]{2,1,0:T(8,128)(2,1)S(1)} %get-tuple-element.311), channel_id=1, source_target_pairs={{0,1},{1,0},{2,3},{3,2},{4,5},{5,4},{6,7},{7,6},{8,9},{9,8},{10,11... | collective-permute-start | bytes 2211848 | tf_op jit(solution)/shard_map/ppermute | solution.py:262
  241.9 22.7 %collective-permute-start.27 = (bf16[192,768]{1,0:T(8,128)(2,1)S(1)}, bf16[192,768]{1,0:T(8,128)(2,1)S(1)}, u32[]{:S(2)}, u32[]{:S(2)}) collective-permute-start(bf16[192,768]{1,0:T(8,128)(2,1)S(1)} %get-tuple-element.353), channel_id=1, source_target_pairs={{0,2},{2,0},{1,3},{3,1},{4,6},{6,4},{5,7},{7,5},{8,10},{10,8},{9,1... | collective-permute-start | bytes 884744 | tf_op jit(solution)/shard_map/ppermute | solution.py:262
  251.3 15.5 %collective-permute-start.28 = (bf16[2,2,96,640]{3,2,1,0:T(8,128)(2,1)S(1)}, bf16[2,2,96,640]{3,2,1,0:T(8,128)(2,1)S(1)}, u32[]{:S(2)}, u32[]{:S(2)}) collective-permute-start(bf16[2,2,96,640]{3,2,1,0:T(8,128)(2,1)S(1)} %get-tuple-element.339), channel_id=1, source_target_pairs={{0,8},{8,0},{1,9},{9,1},{2,10},{10,2},{3,11},{11,3},{4,12},{12,4},... | collective-permute-start | bytes 1474568 | tf_op jit(solution)/shard_map/ppermute | solution.py:262
  251.9 14.8 %collective-permute-start.29 = (bf16[2,2,96,512]{3,2,1,0:T(8,128)(2,1)S(1)}, bf16[2,2,96,512]{3,2,1,0:T(8,128)(2,1)S(1)}, u32[]{:S(2)}, u32[]{:S(2)}) collective-permute-start(bf16[2,2,96,512]{3,2,1,0:T(8,128)(2,1)S(1)} %get-tuple-element.347), channel_id=1, source_target_pairs={{0,16},{16,0},{1,17},{17,1},{2,18},{18,2},{3,19},{19,3},{4,20},{20... | collective-permute-start | bytes 1179656 | tf_op jit(solution)/shard_map/ppermute | solution.py:262
  267.3 24.5 %collective-permute-start.30 = (bf16[2,96,1152]{2,1,0:T(8,128)(2,1)S(1)}, bf16[2,96,1152]{2,1,0:T(8,128)(2,1)}, u32[]{:S(2)}, u32[]{:S(2)}) collective-permute-start(bf16[2,96,1152]{2,1,0:T(8,128)(2,1)S(1)} %get-tuple-element.343), channel_id=1, source_target_pairs={{0,1},{1,0},{2,3},{3,2},{4,5},{5,4},{6,7},{7,6},{8,9},{9,8},{10,11... | collective-permute-start | bytes 1327112 | tf_op jit(solution)/shard_map/ppermute | solution.py:262
  272.8 19.1 %collective-permute-start.31 = (bf16[96,1920]{1,0:T(8,128)(2,1)}, bf16[96,1920]{1,0:T(8,128)(2,1)}, u32[]{:S(2)}, u32[]{:S(2)}) collective-permute-start(bf16[96,1920]{1,0:T(8,128)(2,1)} %get-tuple-element.349), channel_id=1, source_target_pairs={{0,2},{2,0},{1,3},{3,1},{4,6},{6,4},{5,7},{7,5},{8,10},{10,8},{9,1... | collective-permute-start | bytes 1105928 | tf_op jit(solution)/shard_map/ppermute | solution.py:262
  274.2 5.4 %collective-permute-start.34 = (bf16[192,384]{1,0:T(8,128)(2,1)}, bf16[192,384]{1,0:T(8,128)(2,1)S(1)}, u32[]{:S(2)}, u32[]{:S(2)}) collective-permute-start(bf16[192,384]{1,0:T(8,128)(2,1)} %get-tuple-element.373), channel_id=1, source_target_pairs={{0,8},{8,0},{1,9},{9,1},{2,10},{10,2},{3,11},{11,3},{4,12},{12,4},... | collective-permute-start | bytes 442376 | tf_op jit(solution)/shard_map/ppermute | solution.py:262
  274.7 5.4 %collective-permute-start.33 = (bf16[192,384]{1,0:T(8,128)(2,1)}, bf16[192,384]{1,0:T(8,128)(2,1)S(1)}, u32[]{:S(2)}, u32[]{:S(2)}) collective-permute-start(bf16[192,384]{1,0:T(8,128)(2,1)} %get-tuple-element.374), channel_id=1, source_target_pairs={{0,16},{16,0},{1,17},{17,1},{2,18},{18,2},{3,19},{19,3},{4,20},{20... | collective-permute-start | bytes 442376 | tf_op jit(solution)/shard_map/ppermute | solution.py:262
  294.1 5.1 %collective-permute-start.36 = (f32[12,768]{1,0:T(8,128)S(1)}, f32[12,768]{1,0:T(8,128)S(1)}, u32[]{:S(2)}, u32[]{:S(2)}) collective-permute-start(f32[12,768]{1,0:T(8,128)S(1)} %add.328), channel_id=1, source_target_pairs={{0,8},{8,0},{1,9},{9,1},{2,10},{10,2},{3,11},{11,3},{4,12},{12,4},... | collective-permute-start | bytes 110600 | tf_op jit(solution)/shard_map/ppermute | solution.py:262
  294.6 6.5 %collective-permute-start.38 = (bf16[192,384]{1,0:T(8,128)(2,1)S(1)}, bf16[192,384]{1,0:T(8,128)(2,1)S(1)}, u32[]{:S(2)}, u32[]{:S(2)}) collective-permute-start(bf16[192,384]{1,0:T(8,128)(2,1)S(1)} %get-tuple-element.264), channel_id=1, source_target_pairs={{0,16},{16,0},{1,17},{17,1},{2,18},{18,2},{3,19},{19,3},{4,20},{20... | collective-permute-start | bytes 442376 | tf_op jit(solution)/shard_map/ppermute | solution.py:262
  295.7 10.0 %collective-permute-start.35 = (bf16[96,1152]{1,0:T(8,128)(2,1)S(1)}, bf16[96,1152]{1,0:T(8,128)(2,1)S(1)}, u32[]{:S(2)}, u32[]{:S(2)}) collective-permute-start(bf16[96,1152]{1,0:T(8,128)(2,1)S(1)} %get-tuple-element.359), channel_id=1, source_target_pairs={{0,2},{2,0},{1,3},{3,1},{4,6},{6,4},{5,7},{7,5},{8,10},{10,8},{9,1... | collective-permute-start | bytes 663560 | tf_op jit(solution)/shard_map/ppermute | solution.py:262
  296.5 6.1 %collective-permute-start.37 = (bf16[192,384]{1,0:T(8,128)(2,1)S(1)}, bf16[192,384]{1,0:T(8,128)(2,1)S(1)}, u32[]{:S(2)}, u32[]{:S(2)}) collective-permute-start(bf16[192,384]{1,0:T(8,128)(2,1)S(1)} %get-tuple-element.263), channel_id=1, source_target_pairs={{0,8},{8,0},{1,9},{9,1},{2,10},{10,2},{3,11},{11,3},{4,12},{12,4},... | collective-permute-start | bytes 442376 | tf_op jit(solution)/shard_map/ppermute | solution.py:262
  298.1 6.5 %collective-permute-start.39 = (bf16[96,1024]{1,0:T(8,128)(2,1)S(1)}, bf16[96,1024]{1,0:T(8,128)(2,1)S(1)}, u32[]{:S(2)}, u32[]{:S(2)}) collective-permute-start(bf16[96,1024]{1,0:T(8,128)(2,1)S(1)} %slice.321), channel_id=1, source_target_pairs={{0,16},{16,0},{1,17},{17,1},{2,18},{18,2},{3,19},{19,3},{4,20},{20... | collective-permute-start | bytes 589832 | tf_op jit(solution)/shard_map/ppermute | solution.py:262
  299.2 5.4 %collective-permute-start.40 = (bf16[96,896]{1,0:T(8,128)(2,1)S(1)}, bf16[96,896]{1,0:T(8,128)(2,1)S(1)}, u32[]{:S(2)}, u32[]{:S(2)}) collective-permute-start(bf16[96,896]{1,0:T(8,128)(2,1)S(1)} %slice.322), channel_id=1, source_target_pairs={{0,8},{8,0},{1,9},{9,1},{2,10},{10,2},{3,11},{11,3},{4,12},{12,4},... | collective-permute-start | bytes 516104 | tf_op jit(solution)/shard_map/ppermute | solution.py:262
  305.7 6.1 %collective-permute-start.42 = (bf16[96,512]{1,0:T(8,128)(2,1)S(1)}, bf16[96,512]{1,0:T(8,128)(2,1)S(1)}, u32[]{:S(2)}, u32[]{:S(2)}) collective-permute-start(bf16[96,512]{1,0:T(8,128)(2,1)S(1)} %slice.365), channel_id=1, source_target_pairs={{0,8},{8,0},{1,9},{9,1},{2,10},{10,2},{3,11},{11,3},{4,12},{12,4},... | collective-permute-start | bytes 294920 | tf_op jit(solution)/shard_map/ppermute | solution.py:262
  308.3 6.3 %collective-permute-start.41 = (bf16[96,640]{1,0:T(8,128)(2,1)S(1)}, bf16[96,640]{1,0:T(8,128)(2,1)S(1)}, u32[]{:S(2)}, u32[]{:S(2)}) collective-permute-start(bf16[96,640]{1,0:T(8,128)(2,1)S(1)} %slice.364), channel_id=1, source_target_pairs={{0,16},{16,0},{1,17},{17,1},{2,18},{18,2},{3,19},{19,3},{4,20},{20... | collective-permute-start | bytes 368648 | tf_op jit(solution)/shard_map/ppermute | solution.py:262
  309.4 7.9 %collective-permute-start.45 = (bf16[96,896]{1,0:T(8,128)(2,1)S(1)}, bf16[96,896]{1,0:T(8,128)(2,1)S(1)}, u32[]{:S(2)}, u32[]{:S(2)}) collective-permute-start(bf16[96,896]{1,0:T(8,128)(2,1)S(1)} %add_convert_fusion.17), channel_id=1, source_target_pairs={{0,16},{16,0},{1,17},{17,1},{2,18},{18,2},{3,19},{19,3},{4,20},{20... | collective-permute-start | bytes 516104 | tf_op jit(solution)/shard_map/ppermute | solution.py:262
  310.4 7.0 %collective-permute-start.44 = (bf16[96,1024]{1,0:T(8,128)(2,1)S(1)}, bf16[96,1024]{1,0:T(8,128)(2,1)S(1)}, u32[]{:S(2)}, u32[]{:S(2)}) collective-permute-start(bf16[96,1024]{1,0:T(8,128)(2,1)S(1)} %add_convert_fusion.16), channel_id=1, source_target_pairs={{0,8},{8,0},{1,9},{9,1},{2,10},{10,2},{3,11},{11,3},{4,12},{12,4},... | collective-permute-start | bytes 589832 | tf_op jit(solution)/shard_map/ppermute | solution.py:262
  311.8 5.8 %collective-permute-start.46 = (bf16[768,384]{1,0:T(8,128)(2,1)S(1)}, bf16[768,384]{1,0:T(8,128)(2,1)S(1)}, u32[]{:S(2)}, u32[]{:S(2)}) collective-permute-start(bf16[768,384]{1,0:T(8,128)(2,1)S(1)} %bitcast.254), channel_id=1, source_target_pairs={{0,4},{4,0},{1,5},{5,1},{2,6},{6,2},{3,7},{7,3},{8,12},{12,8},{9,1... | collective-permute-start | bytes 1769480 | tf_op jit(solution)/shard_map/ppermute | solution.py:262
  319.3 6.0 %collective-permute-start.48 = (bf16[96,512]{1,0:T(8,128)(2,1)S(1)}, bf16[96,512]{1,0:T(8,128)(2,1)S(1)}, u32[]{:S(2)}, u32[]{:S(2)}) collective-permute-start(bf16[96,512]{1,0:T(8,128)(2,1)S(1)} %add_convert_fusion.21), channel_id=1, source_target_pairs={{0,16},{16,0},{1,17},{17,1},{2,18},{18,2},{3,19},{19,3},{4,20},{20... | collective-permute-start | bytes 294920 | tf_op jit(solution)/shard_map/ppermute | solution.py:262
  320.2 5.0 %collective-permute-start.49 = (f32[12,768]{1,0:T(8,128)S(1)}, f32[12,768]{1,0:T(8,128)S(1)}, u32[]{:S(2)}, u32[]{:S(2)}) collective-permute-start(f32[12,768]{1,0:T(8,128)S(1)} %add.340), channel_id=1, source_target_pairs={{0,2},{2,0},{1,3},{3,1},{4,6},{6,4},{5,7},{7,5},{8,10},{10,8},{9,1... | collective-permute-start | bytes 110600 | tf_op jit(solution)/shard_map/ppermute | solution.py:262
  321.5 4.9 %collective-permute-start.47 = (bf16[96,640]{1,0:T(8,128)(2,1)S(1)}, bf16[96,640]{1,0:T(8,128)(2,1)S(1)}, u32[]{:S(2)}, u32[]{:S(2)}) collective-permute-start(bf16[96,640]{1,0:T(8,128)(2,1)S(1)} %add_convert_fusion.20), channel_id=1, source_target_pairs={{0,8},{8,0},{1,9},{9,1},{2,10},{10,2},{3,11},{11,3},{4,12},{12,4},... | collective-permute-start | bytes 368648 | tf_op jit(solution)/shard_map/ppermute | solution.py:262
  326.8 5.5 %collective-permute-start.51 = (bf16[192,1152]{1,0:T(8,128)(2,1)S(1)}, bf16[192,1152]{1,0:T(8,128)(2,1)S(1)}, u32[]{:S(2)}, u32[]{:S(2)}) collective-permute-start(bf16[192,1152]{1,0:T(8,128)(2,1)S(1)} %pad_maximum_fusion.24), channel_id=1, source_target_pairs={{0,4},{4,0},{1,5},{5,1},{2,6},{6,2},{3,7},{7,3},{8,12},{12,8},{9,1... | collective-permute-start | bytes 1327112 | tf_op jit(solution)/shard_map/ppermute | solution.py:262
  (50 other events, 267.9 us)

commit v5 on v3

--- a/solution.py
+++ b/solution.py
@@ -244,7 +244,7 @@
         compiler_params=pltpu.CompilerParams(vmem_limit_bytes=28 * 2**20),
         cost_estimate=FREE,
         name="matmul_norm_back",
-    )(*map(stay if both else (lambda v: v), (grad, weight, values)), gain.reshape(1, width), past)
+    )(*map(stay if both else (lambda v: v), (grad, weight)), values, gain.reshape(1, width), past)
 
 
 class Net:

time: 339 us -> 347 us (1.024)
  matrix products: 62.5 us -> 67.7 us
  waiting for transfers between devices: 79.8 us -> 75.3 us
  starting transfers between devices: 53.3 us -> 56.9 us
    ppermute x53, waiting for transfers between devices: 79.8 us -> 75.3 us  [swap(): return lax.ppermute(piece, name, SWAP)]
    dot_general x8, matrix products: 35.7 us -> 39.4 us  [dot_tn(): lax.dot_general(a, b, (((0,), (0,)), ((), ())), preferred_element_type=f32)]
    ppermute x53, starting transfers between devices: 53.3 us -> 56.9 us  [swap(): return lax.ppermute(piece, name, SWAP)]
    unnamed x86 -> x102, local copies, waits for them, and re-layouts: 8.33 us -> 7.72 us
  transfers between devices with their start and end apart: 53 -> 53, of which waited for: 30 -> 26; matrix products, arithmetic and copies ran while one was open for 30% -> 30% of each run, Pallas kernels for 14% -> 13%
where the time goes in v5:
time: 347 us; the launch traced here: 342 us
  waiting for transfers between devices  75.3 us (22%)
  matrix products  67.7 us (20%)
  starting transfers between devices  56.9 us (16%)
  Pallas kernels  52.6 us (15%)
  local copies, waits for them, and re-layouts  43.9 us (13%)
  other arithmetic  41.8 us (12%)
    ppermute x53, waiting for transfers between devices, swap(): return lax.ppermute(piece, name, SWAP)  75.3 us
    ppermute x53, starting transfers between devices, swap(): return lax.ppermute(piece, name, SWAP)  56.9 us
    dot_general x8, matrix products, dot_tn(): lax.dot_general(a, b, (((0,), (0,)), ((), ())), preferred_element_type=f32)  39.4 us
    dot_general x4, matrix products, dot_nn(): return jnp.dot(a, b, preferred_element_type=f32)  25.4 us
    pallas_call x2, Pallas kernels, matmul_norm_back(): pl.pallas_call(norm_back_kernel if both else norm_back_low_kernel, grid=(...  21.5 us
    pallas_call x1, Pallas kernels, attention_back(): pl.pallas_call(attention_back_kernel, grid=(slots,), in_specs=[pl.BlockSp...  14.2 us
    convert_element_type x17, other arithmetic, add(): return (pair[0].astype(f32) + pair[1].astype(f32)).astype(bf16)  11 us
    squeeze x11, local copies, waits for them, and re-layouts, part_with(): send = lax.dynamic_index_in_dim(piece, 1 - bit, spot, keepdims=False)  8.92 us
  transfers between devices with their start and end apart: 53, of which 26 were waited for; matrix products, arithmetic and copies ran while one was open for 30% of the time, Pallas kernels for 13%

profile of v5, /device:TPU:0, one launch (start us, length us, event | category | flops | bytes accessed | tf_op | source)
XLA Modules:
  0.0 341.5 jit_solution(9796239551302225066)
XLA Ops:
  2.6 4.1 %collective-permute-start = (bf16[96,1152]{1,0:T(8,128)(2,1)S(1)}, bf16[96,1152]{1,0:T(8,128)(2,1)S(1)}, u32[]{:S(2)}, u32[]{:S(2)}) collective-permute-start(bf16[96,1152]{1,0:T(8,128)(2,1)S(1)} %pad_maximum_fusion.30), channel_id=1, source_target_pairs={{0,2},{2,0},{1,3},{3,1},{4,6},{6,4},{5,7},{7,5},{8,10},{10,8},{9,1... | collective-permute-start | bytes 663560 | tf_op jit(solution)/shard_map/ppermute | solution.py:262
  15.1 2.3 collective-permute-done.1
  17.6 1.6 collective-permute-start.2
  19.7 9.3 %collective-permute-done.3 = bf16[2,12,192]{2,1,0:T(8,128)(2,1)S(1)} collective-permute-done((bf16[2,12,192]{2,1,0:T(8,128)(2,1)S(1)}, bf16[2,12,192]{2,1,0:T(8,128)(2,1)S(1)}, u32[]{:S(2)}, u32[]{:S(2)}) %collective-permute-start.3) | collective-permute-done | bytes 9248 | tf_op jit(solution)/shard_map/ppermute | solution.py:262
  34.9 3.4 %collective-permute-start.7 = (bf16[96,1920]{1,0:T(8,128)(2,1)S(1)}, bf16[96,1920]{1,0:T(8,128)(2,1)}, u32[]{:S(2)}, u32[]{:S(2)}) collective-permute-start(bf16[96,1920]{1,0:T(8,128)(2,1)S(1)} %pad_maximum_fusion.26), channel_id=1, source_target_pairs={{0,2},{2,0},{1,3},{3,1},{4,6},{6,4},{5,7},{7,5},{8,10},{10,8},{9,1... | collective-permute-start | bytes 1105928 | tf_op jit(solution)/shard_map/ppermute | solution.py:262
  39.7 2.5 collective-permute-done.5
  50.9 3.2 collective-permute-done.7
  55.8 2.3 broadcast_select_fusion.5
  58.5 4.7 %fusion.5 = bf16[1040,2304]{1,0:T(8,128)(2,1)S(1)} fusion(bf16[1040,768]{1,0:T(8,128)(2,1)S(1)} %fusion.12, bf16[768,2304]{1,0:T(8,128)(2,1)S(1)} %pad_maximum_fusion.1.weight_ref, f32[2304]{0:T(1024)S(1)} %pad_maximum_fusion.34), kind=kOutput, calls=%fused_computation.10 | convolution fusion | flops 3685294080 | bytes 9937920 | tf_op jit(solution)/shard_map/dot_general | solution.py:44
  63.1 8.4 %attention.1 = (bf16[5,208,768]{2,1,0:T(8,128)(2,1)S(1)}, bf16[5,12,208,208]{3,2,1,0:T(8,128)(2,1)}) custom-call(bf16[5,208,2304]{2,1,0:T(8,128)(2,1)S(1)} %bitcast.226), custom_call_target="tpu_custom_call" | custom-call | tf_op jit(solution)/shard_map/attention/pallas_call | solution.py:118
  74.9 4.8 %collective-permute-start.9 = (bf16[96,1536]{1,0:T(8,128)(2,1)S(1)}, bf16[96,1536]{1,0:T(8,128)(2,1)S(1)}, u32[]{:S(2)}, u32[]{:S(2)}) collective-permute-start(bf16[96,1536]{1,0:T(8,128)(2,1)S(1)} %copy-done.37), channel_id=1, source_target_pairs={{0,2},{2,0},{1,3},{3,1},{4,6},{6,4},{5,7},{7,5},{8,10},{10,8},{9,1... | collective-permute-start | bytes 884744 | tf_op jit(solution)/shard_map/ppermute | solution.py:262
  79.7 12.7 %collective-permute-done.9 = bf16[96,1536]{1,0:T(8,128)(2,1)S(1)} collective-permute-done((bf16[96,1536]{1,0:T(8,128)(2,1)S(1)}, bf16[96,1536]{1,0:T(8,128)(2,1)S(1)}, u32[]{:S(2)}, u32[]{:S(2)}) %collective-permute-start.9) | collective-permute-done | bytes 294944 | tf_op jit(solution)/shard_map/ppermute | solution.py:262
  95.7 4.2 %collective-permute-done.12 = bf16[768,1920]{1,0:T(8,128)(2,1)} collective-permute-done((bf16[768,1920]{1,0:T(8,128)(2,1)S(1)}, bf16[768,1920]{1,0:T(8,128)(2,1)}, u32[]{:S(2)}, u32[]{:S(2)}) %collective-permute-start.12) | collective-permute-done | bytes 2949152 | tf_op jit(solution)/shard_map/ppermute | solution.py:262
  99.9 2.4 broadcast_select_fusion
  104.2 2.0 copy-done.2
  106.2 1.6 fusion.57
  108.3 2.4 collective-permute-done.13
  115.4 11.8 %fusion.4 = (bf16[1040,3072]{1,0:T(8,128)(2,1)}, bf16[1040,3072]{1,0:T(8,128)(2,1)}) fusion(f32[3072]{0:T(1024)S(1)} %add.295, bf16[1040,768]{1,0:T(8,128)(2,1)S(1)} %add_convert_fusion.3, bf16[768,3072]{1,0:T(8,128)(2,1)S(1)} %pad_maximum_fusion.weight_ref), kind=kOutput, calls=%fused_computation.7 | convolution fusion | flops 4945674240 | bytes 19107840 | tf_op jit(solution)/shard_map/dot_general | solution.py:44
  127.9 1.8 pad_maximum_fusion.4
  132.6 7.6 %convolution_convert_fusion = bf16[3072,384]{1,0:T(8,128)(2,1)S(1)} fusion(bf16[1040,3072]{1,0:T(8,128)(2,1)} %get-tuple-element.182, bf16[1040,768]{1,0:T(8,128)(2,1)S(1)} %bitcast_multiply_fusion.grad_ref.past_ref, s32[]{:T(128)S(6)} %select_n.456), kind=kOutput, calls=%fused_computation.15 | convolution fusion | flops 2454847488 | bytes 9547780 | tf_op jit(solution)/shard_map/dot_general | solution.py:40
  140.8 2.6 broadcast_select_fusion.3
  144.6 7.3 %fusion.8 = bf16[1040,768]{1,0:T(8,128)(2,1)S(1)} fusion(f32[1040,768]{1,0:T(8,128)S(1)} %get-tuple-element.404.value_ref, bf16[1040,3072]{1,0:T(8,128)(2,1)} %get-tuple-element.182, bf16[3072,768]{1,0:T(8,128)(2,1)S(1)} %bitcast.230, f32[1040]{0:T(1024)S(1)} %broadcast_in_dim_reshape.4, f32[768]{0:T(1024)S(1)} %add.300), kind=kOutput, calls=%fused_computation.26 | convolution fusion | flops 4910530560 | bytes 15907904 | tf_op jit(solution)/shard_map/dot_general | solution.py:44
  153.2 9.0 %add_convert_fusion.1 = bf16[3072,384]{1,0:T(8,128)(2,1)} fusion(bf16[3072,384]{1,0:T(8,128)(2,1)S(1)} %collective-permute-done.17, bf16[1040,3072]{1,0:T(8,128)(2,1)} %get-tuple-element.182, bf16[1040,768]{1,0:T(8,128)(2,1)S(1)} %bitcast_multiply_fusion.grad_ref.past_ref, s32[]{:T(128)S(6)} %select_n.416), kind=kOutput, calls=%fused_computation.14 | convolution fusion | flops 2457206784 | bytes 11907076 | tf_op jit(solution)/shard_map/dot_general | solution.py:40
  162.2 8.5 %hidden_back.1 = (bf16[1040,3072]{1,0:T(8,128)(2,1)}, f32[1,3072]{1,0:T(1,128)S(1)}) custom-call(bf16[1040,768]{1,0:T(8,128)(2,1)S(1)} %bitcast_multiply_fusion.grad_ref.past_ref, bf16[3072,768]{1,0:T(8,128)(2,1)S(1)} %bitcast.231, bf16[1040,3072]{1,0:T(8,128)(2,1)S(1)} %bitcast.235), custom_call_target="tpu_custom_call" | custom-call | tf_op jit(solution)/shard_map/hidden_back/pallas_call | solution.py:172
  170.6 6.4 %convolution_convert_fusion.1 = bf16[768,1536]{1,0:T(8,128)(2,1)} fusion(bf16[1040,768]{1,0:T(8,128)(2,1)S(1)} %copy-done.32, bf16[1040,3072]{1,0:T(8,128)(2,1)} %get-tuple-element.197.grad_ref, s32[]{:T(128)S(6)} %select_n.457), kind=kOutput, calls=%fused_computation.27 | convolution fusion | flops 2454847488 | bytes 7151620 | tf_op jit(solution)/shard_map/dot_general | solution.py:40
  177.0 1.9 fusion.50
  185.2 13.2 %matmul_norm_back.2 = (f32[1040,768]{1,0:T(8,128)S(1)}, bf16[1040,768]{1,0:T(8,128)(2,1)S(1)}, f32[8,768]{1,0:T(8,128)S(1)}) custom-call(bf16[1040,3072]{1,0:T(8,128)(2,1)} %get-tuple-element.197.grad_ref, bf16[768,3072]{1,0:T(8,128)(2,1)} %copy-done.16, f32[1040,768]{1,0:T(8,128)S(1)} %get-tuple-element.404.value_ref, f32[1,768]{1,0:T(1,128)S(1)} %slice.301.gain_ref, ...), custom_call_target="tpu_custom_call" | custom-call | tf_op jit(solution)/shard_map/matmul_norm_back/pallas_call | solution.py:232
  201.1 5.7 %add_convert_fusion = bf16[768,1536]{1,0:T(8,128)(2,1)S(1)} fusion(bf16[768,1536]{1,0:T(8,128)(2,1)} %collective-permute-done.20, bf16[1040,768]{1,0:T(8,128)(2,1)S(1)} %copy-done.33, bf16[1040,3072]{1,0:T(8,128)(2,1)} %get-tuple-element.197.grad_ref, s32[]{:T(128)} %select_n.415), kind=kOutput, calls=%fused_computation.13 | convolution fusion | flops 2457206784 | bytes 9511424 | tf_op jit(solution)/shard_map/dot_general | solution.py:40
  216.5 1.7 collective-permute-start.22
  218.3 2.9 convolution_convert_fusion.3
  221.2 14.2 %attention_back.1 = (bf16[5,208,2304]{2,1,0:T(8,128)(2,1)S(1)}, f32[1,2304]{1,0:T(1,128)S(1)}) custom-call(bf16[5,208,2304]{2,1,0:T(8,128)(2,1)S(1)} %bitcast.229, bf16[5,12,208,208]{3,2,1,0:T(8,128)(2,1)} %get-tuple-element.185.prob_ref, bf16[5,208,768]{2,1,0:T(8,128)(2,1)S(1)} %bitcast.241), custom_call_target="tpu_custom_call" | custom-call | tf_op jit(solution)/shard_map/attention_back/pallas_call | solution.py:139
  236.3 4.1 %convolution_convert_fusion.2 = bf16[768,1152]{1,0:T(8,128)(2,1)} fusion(bf16[1040,768]{1,0:T(8,128)(2,1)S(1)} %copy-done.29, bf16[1040,2304]{1,0:T(8,128)(2,1)S(1)} %bitcast.236, s32[]{:T(128)S(6)} %select_n.464), kind=kOutput, calls=%fused_computation.28 | convolution fusion | flops 1841135616 | bytes 5763076 | tf_op jit(solution)/shard_map/dot_general | solution.py:40
  241.1 1.6 add_convert_fusion.6
  246.9 4.8 %collective-permute-start.27 = (bf16[192,768]{1,0:T(8,128)(2,1)}, bf16[192,768]{1,0:T(8,128)(2,1)}, u32[]{:S(2)}, u32[]{:S(2)}) collective-permute-start(bf16[192,768]{1,0:T(8,128)(2,1)} %get-tuple-element.351), channel_id=1, source_target_pairs={{0,2},{2,0},{1,3},{3,1},{4,6},{6,4},{5,7},{7,5},{8,10},{10,8},{9,1... | collective-permute-start | bytes 884744 | tf_op jit(solution)/shard_map/ppermute | solution.py:262
  251.8 4.3 %add_convert_fusion.2 = bf16[768,1152]{1,0:T(8,128)(2,1)S(1)} fusion(bf16[768,1152]{1,0:T(8,128)(2,1)} %collective-permute-done.25, bf16[1040,768]{1,0:T(8,128)(2,1)S(1)} %copy-done.30, bf16[1040,2304]{1,0:T(8,128)(2,1)S(1)} %bitcast.239, s32[]{:T(128)S(6)} %select_n.402), kind=kOutput, calls=%fused_computation.25 | convolution fusion | flops 1842905088 | bytes 7532548 | tf_op jit(solution)/shard_map/dot_general | solution.py:40
  259.7 8.3 %matmul_norm_back.3 = (bf16[1040,768]{1,0:T(8,128)(2,1)S(1)}, f32[8,768]{1,0:T(8,128)S(1)}) custom-call(bf16[1040,2304]{1,0:T(8,128)(2,1)S(1)} %bitcast.240, bf16[768,2304]{1,0:T(8,128)(2,1)S(1)} %copy-done.7, bf16[1040,768]{1,0:T(8,128)(2,1)S(1)} %bitcast.233, f32[1,768]{1,0:T(1,128)S(1)} %slice.306.gain_ref, f32[1040,768]{1,0:T(8,128)S(1)} %copy-done.10), custom_call_target="tpu_custom_call" | custom-call | tf_op jit(solution)/shard_map/matmul_norm_back/pallas_call | solution.py:232
  269.1 2.2 collective-permute-done.26
  275.2 4.6 %collective-permute-start.30 = (bf16[2,96,1152]{2,1,0:T(8,128)(2,1)S(1)}, bf16[2,96,1152]{2,1,0:T(8,128)(2,1)S(1)}, u32[]{:S(2)}, u32[]{:S(2)}) collective-permute-start(bf16[2,96,1152]{2,1,0:T(8,128)(2,1)S(1)} %get-tuple-element.341), channel_id=1, source_target_pairs={{0,1},{1,0},{2,3},{3,2},{4,5},{5,4},{6,7},{7,6},{8,9},{9,8},{10,11... | collective-permute-start | bytes 1327112 | tf_op jit(solution)/shard_map/ppermute | solution.py:262
  284.4 1.7 collective-permute-done.34
  286.6 14.1 %collective-permute-done.31 = bf16[96,1920]{1,0:T(8,128)(2,1)S(1)} collective-permute-done((bf16[96,1920]{1,0:T(8,128)(2,1)S(1)}, bf16[96,1920]{1,0:T(8,128)(2,1)S(1)}, u32[]{:S(2)}, u32[]{:S(2)}) %collective-permute-start.31) | collective-permute-done | bytes 368672 | tf_op jit(solution)/shard_map/ppermute | solution.py:262
  301.0 1.6 collective-permute-start.36
  309.6 1.7 collective-permute-done.40
  317.6 2.7 collective-permute-done.41
  320.4 2.0 collective-permute-done.45
  322.8 1.6 maximum_convert_fusion
  325.3 2.3 collective-permute-start.49
  330.6 3.1 collective-permute-done.47
  334.3 1.7 maximum_convert_fusion.1
  (381 shorter events, 109.4 us)
Async XLA Ops:
  2.6 14.8 %collective-permute-start = (bf16[96,1152]{1,0:T(8,128)(2,1)S(1)}, bf16[96,1152]{1,0:T(8,128)(2,1)S(1)}, u32[]{:S(2)}, u32[]{:S(2)}) collective-permute-start(bf16[96,1152]{1,0:T(8,128)(2,1)S(1)} %pad_maximum_fusion.30), channel_id=1, source_target_pairs={{0,2},{2,0},{1,3},{3,1},{4,6},{6,4},{5,7},{7,5},{8,10},{10,8},{9,1... | collective-permute-start | bytes 663560 | tf_op jit(solution)/shard_map/ppermute | solution.py:262
  17.6 11.5 %collective-permute-start.2 = (bf16[2,96,1152]{2,1,0:T(8,128)(2,1)S(1)}, bf16[2,96,1152]{2,1,0:T(8,128)(2,1)S(1)}, u32[]{:S(2)}, u32[]{:S(2)}) collective-permute-start(bf16[2,96,1152]{2,1,0:T(8,128)(2,1)S(1)} %pad_maximum_fusion.23), channel_id=1, source_target_pairs={{0,1},{1,0},{2,3},{3,2},{4,5},{5,4},{6,7},{7,6},{8,9},{9,8},{10,11... | collective-permute-start | bytes 1327112 | tf_op jit(solution)/shard_map/ppermute | solution.py:262
  19.2 9.8 %collective-permute-start.3 = (bf16[2,12,192]{2,1,0:T(8,128)(2,1)S(1)}, bf16[2,12,192]{2,1,0:T(8,128)(2,1)S(1)}, u32[]{:S(2)}, u32[]{:S(2)}) collective-permute-start(bf16[2,12,192]{2,1,0:T(8,128)(2,1)S(1)} %pad_maximum_fusion.33), channel_id=1, source_target_pairs={{0,1},{1,0},{2,3},{3,2},{4,5},{5,4},{6,7},{7,6},{8,9},{9,8},{10,11... | collective-permute-start | bytes 27656 | tf_op jit(solution)/shard_map/ppermute | solution.py:262
  31.9 11.4 %collective-permute-start.4 = (bf16[2,2,96,640]{3,2,0,1:T(8,128)(2,1)}, bf16[2,2,96,640]{3,2,0,1:T(8,128)(2,1)S(1)}, u32[]{:S(2)}, u32[]{:S(2)}) collective-permute-start(bf16[2,2,96,640]{3,2,0,1:T(8,128)(2,1)} %slice.267), channel_id=1, source_target_pairs={{0,8},{8,0},{1,9},{9,1},{2,10},{10,2},{3,11},{11,3},{4,12},{12,4},... | collective-permute-start | bytes 1474568 | tf_op jit(solution)/shard_map/ppermute | solution.py:262
  33.3 8.9 %collective-permute-start.5 = (bf16[2,2,96,512]{3,2,0,1:T(8,128)(2,1)}, bf16[2,2,96,512]{3,2,0,1:T(8,128)(2,1)S(1)}, u32[]{:S(2)}, u32[]{:S(2)}) collective-permute-start(bf16[2,2,96,512]{3,2,0,1:T(8,128)(2,1)} %slice.268), channel_id=1, source_target_pairs={{0,16},{16,0},{1,17},{17,1},{2,18},{18,2},{3,19},{19,3},{4,20},{20... | collective-permute-start | bytes 1179656 | tf_op jit(solution)/shard_map/ppermute | solution.py:262
  34.9 19.1 %collective-permute-start.7 = (bf16[96,1920]{1,0:T(8,128)(2,1)S(1)}, bf16[96,1920]{1,0:T(8,128)(2,1)}, u32[]{:S(2)}, u32[]{:S(2)}) collective-permute-start(bf16[96,1920]{1,0:T(8,128)(2,1)S(1)} %pad_maximum_fusion.26), channel_id=1, source_target_pairs={{0,2},{2,0},{1,3},{3,1},{4,6},{6,4},{5,7},{7,5},{8,10},{10,8},{9,1... | collective-permute-start | bytes 1105928 | tf_op jit(solution)/shard_map/ppermute | solution.py:262
  45.2 10.6 %collective-permute-start.6 = (bf16[768,1152]{1,0:T(8,128)(2,1)}, bf16[768,1152]{1,0:T(8,128)(2,1)}, u32[]{:S(2)}, u32[]{:S(2)}) collective-permute-start(bf16[768,1152]{1,0:T(8,128)(2,1)} %pad_maximum_fusion.5), channel_id=1, source_target_pairs={{0,4},{4,0},{1,5},{5,1},{2,6},{6,2},{3,7},{7,3},{8,12},{12,8},{9,1... | collective-permute-start | bytes 5308424 | tf_op jit(solution)/shard_map/ppermute | solution.py:262
  55.2 17.5 %collective-permute-start.8 = (bf16[2,96,1920]{2,1,0:T(8,128)(2,1)S(1)}, bf16[2,96,1920]{2,1,0:T(8,128)(2,1)S(1)}, u32[]{:S(2)}, u32[]{:S(2)}) collective-permute-start(bf16[2,96,1920]{2,1,0:T(8,128)(2,1)S(1)} %pad_maximum_fusion.18), channel_id=1, source_target_pairs={{0,1},{1,0},{2,3},{3,2},{4,5},{5,4},{6,7},{7,6},{8,9},{9,8},{10,11... | collective-permute-start | bytes 2211848 | tf_op jit(solution)/shard_map/ppermute | solution.py:262
  73.2 19.2 %collective-permute-start.10 = (bf16[2,2,96,1024]{3,2,0,1:T(8,128)(2,1)S(1)}, bf16[2,2,96,1024]{3,2,0,1:T(8,128)(2,1)S(1)}, u32[]{:S(2)}, u32[]{:S(2)}) collective-permute-start(bf16[2,2,96,1024]{3,2,0,1:T(8,128)(2,1)S(1)} %slice.275), channel_id=1, source_target_pairs={{0,8},{8,0},{1,9},{9,1},{2,10},{10,2},{3,11},{11,3},{4,12},{12,4},... | collective-permute-start | bytes 2359304 | tf_op jit(solution)/shard_map/ppermute | solution.py:262
  73.8 18.5 %collective-permute-start.11 = (bf16[2,2,96,896]{3,2,0,1:T(8,128)(2,1)S(1)}, bf16[2,2,96,896]{3,2,0,1:T(8,128)(2,1)S(1)}, u32[]{:S(2)}, u32[]{:S(2)}) collective-permute-start(bf16[2,2,96,896]{3,2,0,1:T(8,128)(2,1)S(1)} %slice.276), channel_id=1, source_target_pairs={{0,16},{16,0},{1,17},{17,1},{2,18},{18,2},{3,19},{19,3},{4,20},{20... | collective-permute-start | bytes 2064392 | tf_op jit(solution)/shard_map/ppermute | solution.py:262
  74.9 17.4 %collective-permute-start.9 = (bf16[96,1536]{1,0:T(8,128)(2,1)S(1)}, bf16[96,1536]{1,0:T(8,128)(2,1)S(1)}, u32[]{:S(2)}, u32[]{:S(2)}) collective-permute-start(bf16[96,1536]{1,0:T(8,128)(2,1)S(1)} %copy-done.37), channel_id=1, source_target_pairs={{0,2},{2,0},{1,3},{3,1},{4,6},{6,4},{5,7},{7,5},{8,10},{10,8},{9,1... | collective-permute-start | bytes 884744 | tf_op jit(solution)/shard_map/ppermute | solution.py:262
  94.4 5.5 %collective-permute-start.12 = (bf16[768,1920]{1,0:T(8,128)(2,1)S(1)}, bf16[768,1920]{1,0:T(8,128)(2,1)}, u32[]{:S(2)}, u32[]{:S(2)}) collective-permute-start(bf16[768,1920]{1,0:T(8,128)(2,1)S(1)} %pad_maximum_fusion.2), channel_id=1, source_target_pairs={{0,4},{4,0},{1,5},{5,1},{2,6},{6,2},{3,7},{7,3},{8,12},{12,8},{9,1... | collective-permute-start | bytes 8847368 | tf_op jit(solution)/shard_map/ppermute | solution.py:262
  94.8 15.9 %collective-permute-start.13 = (bf16[2,96,1536]{2,1,0:T(8,128)(2,1)}, bf16[2,96,1536]{2,1,0:T(8,128)(2,1)S(1)}, u32[]{:S(2)}, u32[]{:S(2)}) collective-permute-start(bf16[2,96,1536]{2,1,0:T(8,128)(2,1)} %pad_maximum_fusion.21), channel_id=1, source_target_pairs={{0,1},{1,0},{2,3},{3,2},{4,5},{5,4},{6,7},{7,6},{8,9},{9,8},{10,11... | collective-permute-start | bytes 1769480 | tf_op jit(solution)/shard_map/ppermute | solution.py:262
  112.0 15.3 %collective-permute-start.14 = (bf16[2,2,96,768]{3,2,1,0:T(8,128)(2,1)S(1)}, bf16[2,2,96,768]{3,2,1,0:T(8,128)(2,1)S(1)}, u32[]{:S(2)}, u32[]{:S(2)}) collective-permute-start(bf16[2,2,96,768]{3,2,1,0:T(8,128)(2,1)S(1)} %get-tuple-element.329), channel_id=1, source_target_pairs={{0,8},{8,0},{1,9},{9,1},{2,10},{10,2},{3,11},{11,3},{4,12},{12,4},... | collective-permute-start | bytes 1769480 | tf_op jit(solution)/shard_map/ppermute | solution.py:262
  112.6 14.7 %collective-permute-start.15 = (bf16[2,2,96,768]{3,2,1,0:T(8,128)(2,1)S(1)}, bf16[2,2,96,768]{3,2,1,0:T(8,128)(2,1)S(1)}, u32[]{:S(2)}, u32[]{:S(2)}) collective-permute-start(bf16[2,2,96,768]{3,2,1,0:T(8,128)(2,1)S(1)} %get-tuple-element.330), channel_id=1, source_target_pairs={{0,16},{16,0},{1,17},{17,1},{2,18},{18,2},{3,19},{19,3},{4,20},{20... | collective-permute-start | bytes 1769480 | tf_op jit(solution)/shard_map/ppermute | solution.py:262
  129.9 10.9 %collective-permute-start.16 = (bf16[768,1536]{1,0:T(8,128)(2,1)}, bf16[768,1536]{1,0:T(8,128)(2,1)}, u32[]{:S(2)}, u32[]{:S(2)}) collective-permute-start(bf16[768,1536]{1,0:T(8,128)(2,1)} %pad_maximum_fusion.4), channel_id=1, source_target_pairs={{0,4},{4,0},{1,5},{5,1},{2,6},{6,2},{3,7},{7,3},{8,12},{12,8},{9,1... | collective-permute-start | bytes 7077896 | tf_op jit(solution)/shard_map/ppermute | solution.py:262
  140.2 13.0 %collective-permute-start.17 = (bf16[3072,384]{1,0:T(8,128)(2,1)S(1)}, bf16[3072,384]{1,0:T(8,128)(2,1)S(1)}, u32[]{:S(2)}, u32[]{:S(2)}) collective-permute-start(bf16[3072,384]{1,0:T(8,128)(2,1)S(1)} %convolution_convert_fusion), channel_id=1, source_target_pairs={{0,4},{4,0},{1,5},{5,1},{2,6},{6,2},{3,7},{7,3},{8,12},{12,8},{9,1... | collective-permute-start | bytes 7077896 | tf_op jit(solution)/shard_map/ppermute | solution.py:262
  177.0 23.1 %collective-permute-start.20 = (bf16[768,1536]{1,0:T(8,128)(2,1)}, bf16[768,1536]{1,0:T(8,128)(2,1)}, u32[]{:S(2)}, u32[]{:S(2)}) collective-permute-start(bf16[768,1536]{1,0:T(8,128)(2,1)} %convolution_convert_fusion.1), channel_id=1, source_target_pairs={{0,4},{4,0},{1,5},{5,1},{2,6},{6,2},{3,7},{7,3},{8,12},{12,8},{9,1... | collective-permute-start | bytes 7077896 | tf_op jit(solution)/shard_map/ppermute | solution.py:262
  180.1 18.4 %collective-permute-start.18 = (bf16[2,2,192,384]{3,2,1,0:T(8,128)(2,1)}, bf16[2,2,192,384]{3,2,1,0:T(8,128)(2,1)}, u32[]{:S(2)}, u32[]{:S(2)}) collective-permute-start(bf16[2,2,192,384]{3,2,1,0:T(8,128)(2,1)} %get-tuple-element.325), channel_id=1, source_target_pairs={{0,8},{8,0},{1,9},{9,1},{2,10},{10,2},{3,11},{11,3},{4,12},{12,4},... | collective-permute-start | bytes 1769480 | tf_op jit(solution)/shard_map/ppermute | solution.py:262
  182.7 15.8 %collective-permute-start.19 = (bf16[2,2,192,384]{3,2,1,0:T(8,128)(2,1)}, bf16[2,2,192,384]{3,2,1,0:T(8,128)(2,1)}, u32[]{:S(2)}, u32[]{:S(2)}) collective-permute-start(bf16[2,2,192,384]{3,2,1,0:T(8,128)(2,1)} %get-tuple-element.323), channel_id=1, source_target_pairs={{0,16},{16,0},{1,17},{17,1},{2,18},{18,2},{3,19},{19,3},{4,20},{20... | collective-permute-start | bytes 1769480 | tf_op jit(solution)/shard_map/ppermute | solution.py:262
  200.1 6.8 %collective-permute-start.21 = (bf16[768,384]{1,0:T(8,128)(2,1)S(1)}, bf16[768,384]{1,0:T(8,128)(2,1)S(1)}, u32[]{:S(2)}, u32[]{:S(2)}) collective-permute-start(bf16[768,384]{1,0:T(8,128)(2,1)S(1)} %convolution_convert_fusion.4), channel_id=1, source_target_pairs={{0,4},{4,0},{1,5},{5,1},{2,6},{6,2},{3,7},{7,3},{8,12},{12,8},{9,1... | collective-permute-start | bytes 1769480 | tf_op jit(solution)/shard_map/ppermute | solution.py:262
  211.2 24.2 %collective-permute-start.23 = (bf16[2,2,96,1024]{3,2,1,0:T(8,128)(2,1)}, bf16[2,2,96,1024]{3,2,1,0:T(8,128)(2,1)}, u32[]{:S(2)}, u32[]{:S(2)}) collective-permute-start(bf16[2,2,96,1024]{3,2,1,0:T(8,128)(2,1)} %get-tuple-element.305), channel_id=1, source_target_pairs={{0,8},{8,0},{1,9},{9,1},{2,10},{10,2},{3,11},{11,3},{4,12},{12,4},... | collective-permute-start | bytes 2359304 | tf_op jit(solution)/shard_map/ppermute | solution.py:262
  211.8 23.6 %collective-permute-start.24 = (bf16[2,2,96,896]{3,2,1,0:T(8,128)(2,1)}, bf16[2,2,96,896]{3,2,1,0:T(8,128)(2,1)}, u32[]{:S(2)}, u32[]{:S(2)}) collective-permute-start(bf16[2,2,96,896]{3,2,1,0:T(8,128)(2,1)} %get-tuple-element.313), channel_id=1, source_target_pairs={{0,16},{16,0},{1,17},{17,1},{2,18},{18,2},{3,19},{19,3},{4,20},{20... | collective-permute-start | bytes 2064392 | tf_op jit(solution)/shard_map/ppermute | solution.py:262
  216.5 18.9 %collective-permute-start.22 = (bf16[2,192,768]{2,1,0:T(8,128)(2,1)}, bf16[2,192,768]{2,1,0:T(8,128)(2,1)S(1)}, u32[]{:S(2)}, u32[]{:S(2)}) collective-permute-start(bf16[2,192,768]{2,1,0:T(8,128)(2,1)} %get-tuple-element.321), channel_id=1, source_target_pairs={{0,1},{1,0},{2,3},{3,2},{4,5},{5,4},{6,7},{7,6},{8,9},{9,8},{10,11... | collective-permute-start | bytes 1769480 | tf_op jit(solution)/shard_map/ppermute | solution.py:262
  240.3 11.4 %collective-permute-start.25 = (bf16[768,1152]{1,0:T(8,128)(2,1)}, bf16[768,1152]{1,0:T(8,128)(2,1)}, u32[]{:S(2)}, u32[]{:S(2)}) collective-permute-start(bf16[768,1152]{1,0:T(8,128)(2,1)} %convolution_convert_fusion.2), channel_id=1, source_target_pairs={{0,4},{4,0},{1,5},{5,1},{2,6},{6,2},{3,7},{7,3},{8,12},{12,8},{9,1... | collective-permute-start | bytes 5308424 | tf_op jit(solution)/shard_map/ppermute | solution.py:262
  245.8 25.5 %collective-permute-start.26 = (bf16[2,96,1920]{2,1,0:T(8,128)(2,1)}, bf16[2,96,1920]{2,1,0:T(8,128)(2,1)}, u32[]{:S(2)}, u32[]{:S(2)}) collective-permute-start(bf16[2,96,1920]{2,1,0:T(8,128)(2,1)} %get-tuple-element.309), channel_id=1, source_target_pairs={{0,1},{1,0},{2,3},{3,2},{4,5},{5,4},{6,7},{7,6},{8,9},{9,8},{10,11... | collective-permute-start | bytes 2211848 | tf_op jit(solution)/shard_map/ppermute | solution.py:262
  246.9 22.2 %collective-permute-start.27 = (bf16[192,768]{1,0:T(8,128)(2,1)}, bf16[192,768]{1,0:T(8,128)(2,1)}, u32[]{:S(2)}, u32[]{:S(2)}) collective-permute-start(bf16[192,768]{1,0:T(8,128)(2,1)} %get-tuple-element.351), channel_id=1, source_target_pairs={{0,2},{2,0},{1,3},{3,1},{4,6},{6,4},{5,7},{7,5},{8,10},{10,8},{9,1... | collective-permute-start | bytes 884744 | tf_op jit(solution)/shard_map/ppermute | solution.py:262
  257.2 14.2 %collective-permute-start.28 = (bf16[2,2,96,640]{3,2,1,0:T(8,128)(2,1)}, bf16[2,2,96,640]{3,2,1,0:T(8,128)(2,1)}, u32[]{:S(2)}, u32[]{:S(2)}) collective-permute-start(bf16[2,2,96,640]{3,2,1,0:T(8,128)(2,1)} %get-tuple-element.337), channel_id=1, source_target_pairs={{0,8},{8,0},{1,9},{9,1},{2,10},{10,2},{3,11},{11,3},{4,12},{12,4},... | collective-permute-start | bytes 1474568 | tf_op jit(solution)/shard_map/ppermute | solution.py:262
  258.6 12.7 %collective-permute-start.29 = (bf16[2,2,96,512]{3,2,1,0:T(8,128)(2,1)}, bf16[2,2,96,512]{3,2,1,0:T(8,128)(2,1)}, u32[]{:S(2)}, u32[]{:S(2)}) collective-permute-start(bf16[2,2,96,512]{3,2,1,0:T(8,128)(2,1)} %get-tuple-element.345), channel_id=1, source_target_pairs={{0,16},{16,0},{1,17},{17,1},{2,18},{18,2},{3,19},{19,3},{4,20},{20... | collective-permute-start | bytes 1179656 | tf_op jit(solution)/shard_map/ppermute | solution.py:262
  275.2 25.6 %collective-permute-start.30 = (bf16[2,96,1152]{2,1,0:T(8,128)(2,1)S(1)}, bf16[2,96,1152]{2,1,0:T(8,128)(2,1)S(1)}, u32[]{:S(2)}, u32[]{:S(2)}) collective-permute-start(bf16[2,96,1152]{2,1,0:T(8,128)(2,1)S(1)} %get-tuple-element.341), channel_id=1, source_target_pairs={{0,1},{1,0},{2,3},{3,2},{4,5},{5,4},{6,7},{7,6},{8,9},{9,8},{10,11... | collective-permute-start | bytes 1327112 | tf_op jit(solution)/shard_map/ppermute | solution.py:262
  280.8 5.3 %collective-permute-start.34 = (bf16[192,384]{1,0:T(8,128)(2,1)S(1)}, bf16[192,384]{1,0:T(8,128)(2,1)S(1)}, u32[]{:S(2)}, u32[]{:S(2)}) collective-permute-start(bf16[192,384]{1,0:T(8,128)(2,1)S(1)} %get-tuple-element.371), channel_id=1, source_target_pairs={{0,8},{8,0},{1,9},{9,1},{2,10},{10,2},{3,11},{11,3},{4,12},{12,4},... | collective-permute-start | bytes 442376 | tf_op jit(solution)/shard_map/ppermute | solution.py:262
  281.4 5.1 %collective-permute-start.33 = (bf16[192,384]{1,0:T(8,128)(2,1)S(1)}, bf16[192,384]{1,0:T(8,128)(2,1)S(1)}, u32[]{:S(2)}, u32[]{:S(2)}) collective-permute-start(bf16[192,384]{1,0:T(8,128)(2,1)S(1)} %get-tuple-element.372), channel_id=1, source_target_pairs={{0,16},{16,0},{1,17},{17,1},{2,18},{18,2},{3,19},{19,3},{4,20},{20... | collective-permute-start | bytes 442376 | tf_op jit(solution)/shard_map/ppermute | solution.py:262
  282.5 18.3 %collective-permute-start.31 = (bf16[96,1920]{1,0:T(8,128)(2,1)S(1)}, bf16[96,1920]{1,0:T(8,128)(2,1)S(1)}, u32[]{:S(2)}, u32[]{:S(2)}) collective-permute-start(bf16[96,1920]{1,0:T(8,128)(2,1)S(1)} %get-tuple-element.347), channel_id=1, source_target_pairs={{0,2},{2,0},{1,3},{3,1},{4,6},{6,4},{5,7},{7,5},{8,10},{10,8},{9,1... | collective-permute-start | bytes 1105928 | tf_op jit(solution)/shard_map/ppermute | solution.py:262
  301.0 4.6 %collective-permute-start.36 = (f32[12,768]{1,0:T(8,128)S(1)}, f32[12,768]{1,0:T(8,128)S(1)}, u32[]{:S(2)}, u32[]{:S(2)}) collective-permute-start(f32[12,768]{1,0:T(8,128)S(1)} %add.328), channel_id=1, source_target_pairs={{0,8},{8,0},{1,9},{9,1},{2,10},{10,2},{3,11},{11,3},{4,12},{12,4},... | collective-permute-start | bytes 110600 | tf_op jit(solution)/shard_map/ppermute | solution.py:262
  302.5 5.6 %collective-permute-start.38 = (bf16[192,384]{1,0:T(8,128)(2,1)S(1)}, bf16[192,384]{1,0:T(8,128)(2,1)S(1)}, u32[]{:S(2)}, u32[]{:S(2)}) collective-permute-start(bf16[192,384]{1,0:T(8,128)(2,1)S(1)} %get-tuple-element.262), channel_id=1, source_target_pairs={{0,16},{16,0},{1,17},{17,1},{2,18},{18,2},{3,19},{19,3},{4,20},{20... | collective-permute-start | bytes 442376 | tf_op jit(solution)/shard_map/ppermute | solution.py:262
  303.7 8.1 %collective-permute-start.35 = (bf16[96,1152]{1,0:T(8,128)(2,1)S(1)}, bf16[96,1152]{1,0:T(8,128)(2,1)S(1)}, u32[]{:S(2)}, u32[]{:S(2)}) collective-permute-start(bf16[96,1152]{1,0:T(8,128)(2,1)S(1)} %get-tuple-element.357), channel_id=1, source_target_pairs={{0,2},{2,0},{1,3},{3,1},{4,6},{6,4},{5,7},{7,5},{8,10},{10,8},{9,1... | collective-permute-start | bytes 663560 | tf_op jit(solution)/shard_map/ppermute | solution.py:262
  303.8 5.6 %collective-permute-start.37 = (bf16[192,384]{1,0:T(8,128)(2,1)S(1)}, bf16[192,384]{1,0:T(8,128)(2,1)S(1)}, u32[]{:S(2)}, u32[]{:S(2)}) collective-permute-start(bf16[192,384]{1,0:T(8,128)(2,1)S(1)} %get-tuple-element.261), channel_id=1, source_target_pairs={{0,8},{8,0},{1,9},{9,1},{2,10},{10,2},{3,11},{11,3},{4,12},{12,4},... | collective-permute-start | bytes 442376 | tf_op jit(solution)/shard_map/ppermute | solution.py:262
  304.3 7.0 %collective-permute-start.39 = (bf16[96,1024]{1,0:T(8,128)(2,1)S(1)}, bf16[96,1024]{1,0:T(8,128)(2,1)S(1)}, u32[]{:S(2)}, u32[]{:S(2)}) collective-permute-start(bf16[96,1024]{1,0:T(8,128)(2,1)S(1)} %slice.321), channel_id=1, source_target_pairs={{0,16},{16,0},{1,17},{17,1},{2,18},{18,2},{3,19},{19,3},{4,20},{20... | collective-permute-start | bytes 589832 | tf_op jit(solution)/shard_map/ppermute | solution.py:262
  305.6 5.6 %collective-permute-start.40 = (bf16[96,896]{1,0:T(8,128)(2,1)S(1)}, bf16[96,896]{1,0:T(8,128)(2,1)S(1)}, u32[]{:S(2)}, u32[]{:S(2)}) collective-permute-start(bf16[96,896]{1,0:T(8,128)(2,1)S(1)} %slice.322), channel_id=1, source_target_pairs={{0,8},{8,0},{1,9},{9,1},{2,10},{10,2},{3,11},{11,3},{4,12},{12,4},... | collective-permute-start | bytes 516104 | tf_op jit(solution)/shard_map/ppermute | solution.py:262
  311.9 5.7 %collective-permute-start.42 = (bf16[96,512]{1,0:T(8,128)(2,1)S(1)}, bf16[96,512]{1,0:T(8,128)(2,1)S(1)}, u32[]{:S(2)}, u32[]{:S(2)}) collective-permute-start(bf16[96,512]{1,0:T(8,128)(2,1)S(1)} %slice.365), channel_id=1, source_target_pairs={{0,8},{8,0},{1,9},{9,1},{2,10},{10,2},{3,11},{11,3},{4,12},{12,4},... | collective-permute-start | bytes 294920 | tf_op jit(solution)/shard_map/ppermute | solution.py:262
  314.0 6.3 %collective-permute-start.41 = (bf16[96,640]{1,0:T(8,128)(2,1)S(1)}, bf16[96,640]{1,0:T(8,128)(2,1)S(1)}, u32[]{:S(2)}, u32[]{:S(2)}) collective-permute-start(bf16[96,640]{1,0:T(8,128)(2,1)S(1)} %slice.364), channel_id=1, source_target_pairs={{0,16},{16,0},{1,17},{17,1},{2,18},{18,2},{3,19},{19,3},{4,20},{20... | collective-permute-start | bytes 368648 | tf_op jit(solution)/shard_map/ppermute | solution.py:262
  315.1 7.4 %collective-permute-start.45 = (bf16[96,896]{1,0:T(8,128)(2,1)S(1)}, bf16[96,896]{1,0:T(8,128)(2,1)S(1)}, u32[]{:S(2)}, u32[]{:S(2)}) collective-permute-start(bf16[96,896]{1,0:T(8,128)(2,1)S(1)} %add_convert_fusion.17), channel_id=1, source_target_pairs={{0,16},{16,0},{1,17},{17,1},{2,18},{18,2},{3,19},{19,3},{4,20},{20... | collective-permute-start | bytes 516104 | tf_op jit(solution)/shard_map/ppermute | solution.py:262
  316.1 6.4 %collective-permute-start.44 = (bf16[96,1024]{1,0:T(8,128)(2,1)S(1)}, bf16[96,1024]{1,0:T(8,128)(2,1)S(1)}, u32[]{:S(2)}, u32[]{:S(2)}) collective-permute-start(bf16[96,1024]{1,0:T(8,128)(2,1)S(1)} %add_convert_fusion.16), channel_id=1, source_target_pairs={{0,8},{8,0},{1,9},{9,1},{2,10},{10,2},{3,11},{11,3},{4,12},{12,4},... | collective-permute-start | bytes 589832 | tf_op jit(solution)/shard_map/ppermute | solution.py:262
  317.6 5.1 %collective-permute-start.46 = (bf16[768,384]{1,0:T(8,128)(2,1)S(1)}, bf16[768,384]{1,0:T(8,128)(2,1)S(1)}, u32[]{:S(2)}, u32[]{:S(2)}) collective-permute-start(bf16[768,384]{1,0:T(8,128)(2,1)S(1)} %bitcast.256), channel_id=1, source_target_pairs={{0,4},{4,0},{1,5},{5,1},{2,6},{6,2},{3,7},{7,3},{8,12},{12,8},{9,1... | collective-permute-start | bytes 1769480 | tf_op jit(solution)/shard_map/ppermute | solution.py:262
  324.4 6.2 %collective-permute-start.48 = (bf16[96,512]{1,0:T(8,128)(2,1)S(1)}, bf16[96,512]{1,0:T(8,128)(2,1)S(1)}, u32[]{:S(2)}, u32[]{:S(2)}) collective-permute-start(bf16[96,512]{1,0:T(8,128)(2,1)S(1)} %add_convert_fusion.21), channel_id=1, source_target_pairs={{0,16},{16,0},{1,17},{17,1},{2,18},{18,2},{3,19},{19,3},{4,20},{20... | collective-permute-start | bytes 294920 | tf_op jit(solution)/shard_map/ppermute | solution.py:262
  325.3 5.3 %collective-permute-start.49 = (f32[12,768]{1,0:T(8,128)S(1)}, f32[12,768]{1,0:T(8,128)S(1)}, u32[]{:S(2)}, u32[]{:S(2)}) collective-permute-start(f32[12,768]{1,0:T(8,128)S(1)} %add.340), channel_id=1, source_target_pairs={{0,2},{2,0},{1,3},{3,1},{4,6},{6,4},{5,7},{7,5},{8,10},{10,8},{9,1... | collective-permute-start | bytes 110600 | tf_op jit(solution)/shard_map/ppermute | solution.py:262
  328.8 4.9 %collective-permute-start.47 = (bf16[96,640]{1,0:T(8,128)(2,1)S(1)}, bf16[96,640]{1,0:T(8,128)(2,1)S(1)}, u32[]{:S(2)}, u32[]{:S(2)}) collective-permute-start(bf16[96,640]{1,0:T(8,128)(2,1)S(1)} %add_convert_fusion.20), channel_id=1, source_target_pairs={{0,8},{8,0},{1,9},{9,1},{2,10},{10,2},{3,11},{11,3},{4,12},{12,4},... | collective-permute-start | bytes 368648 | tf_op jit(solution)/shard_map/ppermute | solution.py:262
  334.1 5.5 %collective-permute-start.51 = (bf16[192,1152]{1,0:T(8,128)(2,1)S(1)}, bf16[192,1152]{1,0:T(8,128)(2,1)S(1)}, u32[]{:S(2)}, u32[]{:S(2)}) collective-permute-start(bf16[192,1152]{1,0:T(8,128)(2,1)S(1)} %pad_maximum_fusion.24), channel_id=1, source_target_pairs={{0,4},{4,0},{1,5},{5,1},{2,6},{6,2},{3,7},{7,3},{8,12},{12,8},{9,1... | collective-permute-start | bytes 1327112 | tf_op jit(solution)/shard_map/ppermute | solution.py:262
  (57 other events, 314.1 us)
